TPU v7x, 32 devices: a whole 2x2x4 slice. The times are simulated.
32 devices in a mesh: ctx: 8 (over y, x, core), tp: 4 (over z).
Axes of the slice: x: 2, y: 2, z: 4, core: 2. Of those that a mesh axis runs over, the one named last changes fastest.
Arguments:
- layer_in: bfloat16 [8192, 1024], P(('ctx', 'tp')), may hold values from -6 to 6
- gain_one: float32 [1024], replicated, may hold values from 0.5 to 1.5
- w_query: bfloat16 [1024, 1024], P(None, 'tp'), may hold values from -0.1875 to 0.1875
- w_key: bfloat16 [1024, 1024], P(None, 'tp'), may hold values from -0.1875 to 0.1875
- w_value: bfloat16 [1024, 1024], P(None, 'tp'), may hold values from -0.1875 to 0.1875
- w_out: bfloat16 [1024, 1024], P('tp'), may hold values from -3 to 3
- bias_table: float32 [32, 16], P(None, 'tp'), may hold values from -4 to 4
- gain_two: float32 [1024], replicated, may hold values from 0.5 to 1.5
- w_router: bfloat16 [1024, 4], replicated, may hold values from -0.125 to 0.125
- w_gate: bfloat16 [4, 1024, 2816], P(None, None, 'tp'), may hold values from -0.1875 to 0.1875
- w_up: bfloat16 [4, 1024, 2816], P(None, None, 'tp'), may hold values from -0.1875 to 0.1875
- w_down: bfloat16 [4, 2816, 1024], P(None, 'tp'), may hold values from -0.3125 to 0.3125
- lengths: int32 [16], replicated, may hold values from 1 to 6144, 8192 in all
- block_perm: int32 [64], replicated, may hold values from 0 to 63, as said below
- buckets: int32 [128], replicated, may hold values from 0 to 31, as said below
- routes: int32 [8192, 2], P('ctx'), may hold values from 0 to 3, as said below
- cotangent: bfloat16 [8192, 1024], P(('ctx', 'tp')), may hold values from -6 to 6
Outputs:
- layer_out: float32 [8192, 1024], P(('ctx', 'tp'))
- grad_x: float32 [8192, 1024], P(('ctx', 'tp'))
- grad_gain_one: float32 [1024], P('tp')
- grad_w_query: float32 [1024, 1024], P(None, 'tp')
- grad_w_key: float32 [1024, 1024], P(None, 'tp')
- grad_w_value: float32 [1024, 1024], P(None, 'tp')
- grad_w_out: float32 [1024, 1024], P('tp')
- grad_table: float32 [32, 16], P(None, 'tp')
- grad_gain_two: float32 [1024], P('tp')
- grad_w_router: float32 [1024, 4], P('tp')
- grad_w_gate: float32 [4, 1024, 2816], P(None, None, 'tp')
- grad_w_up: float32 [4, 1024, 2816], P(None, None, 'tp')
- grad_w_down: float32 [4, 2816, 1024], P(None, 'tp')
Inputs may be any that keep to these rules, and one draw needn't show every extreme that they name: `lengths`: 16 sequences packed end to end in this order; exactly one has the greatest length 6144 or several have it. A permutation: stored block j of every token array is packed block block_perm[j]; for even j, block_perm[j + 1] = 63 - block_perm[j]. `buckets`: bucket of each distance of 0 to 127 tokens; larger distances take the last entry. Starts at 0, never falls, rises by 0 or 1 from one distance to the next, ends at 31. `routes`: each row names 2 different experts.
All inputs are finite; a program needn't handle non-finite values.
Results may differ from a plain program's by a relative error of at most 0.03.
Values may be sent and summed in bfloat16 or wider, within the bound.
No kernel may reach another device: no remote copies, remote signals or barrier semaphores. Data moves between devices by JAX's collectives and lax.ppermute only.
A program may use at most 192 MiB of HBM per device.

v0:
```python
import jax
import jax.numpy as jnp
from jax import lax
from jax.sharding import PartitionSpec as P

DH = 64
BLOCK = 128


EPS = 1e-06
NEG = -1e30
TILE_CAP = 512
HIGH = lax.Precision.HIGHEST


def shifted(block, axis, distance):
    devices = range(lax.axis_size(axis))
    route = [((i - distance) % len(devices), i) for i in devices]
    return lax.ppermute(block, axis, route)


def token_info(block_perm, ends, first_block, block_count):
    blocks = lax.dynamic_slice_in_dim(block_perm, first_block, block_count, 0)
    offsets = jnp.arange(BLOCK, dtype=jnp.int32)
    places = (blocks[:, None] * BLOCK + offsets[None, :]).reshape(-1)
    owners = jnp.sum((ends[None, :] <= places[:, None]).astype(jnp.int32), axis=1)
    return (blocks, places, owners, owners[::BLOCK], owners[BLOCK - 1 :: BLOCK])


def tile_view(info, start, tile_rows):
    block_count = tile_rows // BLOCK
    block_start = start // BLOCK
    return (
        lax.dynamic_slice_in_dim(info[0], block_start, block_count, 0),
        lax.dynamic_slice_in_dim(info[1], start, tile_rows, 0),
        lax.dynamic_slice_in_dim(info[2], start, tile_rows, 0),
        lax.dynamic_slice_in_dim(info[3], block_start, block_count, 0),
        lax.dynamic_slice_in_dim(info[4], block_start, block_count, 0),
    )


def tile_live(q_view, k_view):
    ordered = q_view[0][:, None] >= k_view[0][None, :]
    shared = q_view[3][:, None] <= k_view[4][None, :]
    return jnp.any(ordered & shared)


def tile_terms(q_view, k_view):
    relation = q_view[0][:, None] - k_view[0][None, :]
    w_same = (relation == 0).astype(jnp.float32)
    w_prev = (relation == 1).astype(jnp.float32)
    w_far = (relation >= 2).astype(jnp.float32)
    allowed = (q_view[2][:, None] == k_view[2][None, :]) & (
        q_view[1][:, None] >= k_view[1][None, :]
    )
    return (allowed, w_same, w_prev, w_far)


def add_bias(scores, w_same, w_prev, w_far, near_same, near_prev, far_bias):
    head_count, tile_rows, _ = scores.shape
    block_count = tile_rows // BLOCK
    split = scores.reshape(head_count, block_count, BLOCK, block_count, BLOCK)
    split = (
        split
        + w_far[None, :, None, :, None] * far_bias[:, None, None, None, None]
        + w_same[None, :, None, :, None] * near_same[:, None, :, None, :]
        + w_prev[None, :, None, :, None] * near_prev[:, None, :, None, :]
    )
    return split.reshape(head_count, tile_rows, tile_rows)


def slot_tables(group_routes, experts, capacity):
    count = group_routes.shape[0]
    top_count = group_routes.shape[1]
    flat = group_routes.T.reshape(-1)
    hot = (flat[:, None] == jnp.arange(experts, dtype=jnp.int32)[None, :]).astype(jnp.int32)
    rank_of = jnp.sum((jnp.cumsum(hot, axis=0) - hot) * hot, axis=1)
    kept = rank_of < capacity
    dest = jnp.where(kept, flat * capacity + rank_of, experts * capacity)
    tokens = jnp.tile(jnp.arange(count, dtype=jnp.int32), top_count)
    token_of_slot = (
        jnp.zeros((experts * capacity + 1,), jnp.int32).at[dest].set(tokens)[: experts * capacity]
    )
    live = jnp.zeros((experts * capacity + 1,), jnp.float32).at[dest].set(1.0)[: experts * capacity]
    return (dest, kept.reshape(top_count, count).astype(jnp.float32), token_of_slot, live)


def on_device(
    layer_in,
    gain_one,
    w_query,
    w_key,
    w_value,
    w_out,
    bias_table,
    gain_two,
    w_router,
    w_gate,
    w_up,
    w_down,
    lengths,
    block_perm,
    buckets,
    routes,
    cotangent,
):
    tp_count = lax.axis_size("tp")
    ctx_count = lax.axis_size("ctx")
    tp_index = lax.axis_index("tp")
    ctx_index = lax.axis_index("ctx")
    rows_dev = layer_in.shape[0]
    width = layer_in.shape[1]
    group_rows = rows_dev * tp_count
    width_loc = w_query.shape[1]
    head_count = width_loc // DH
    tile_rows = min(TILE_CAP, group_rows)
    tile_count = group_rows // tile_rows
    blocks_group = group_rows // BLOCK
    experts = w_gate.shape[0]
    top_count = routes.shape[1]
    capacity = 5 * top_count * group_rows // (4 * experts)
    slot_count = experts * capacity
    score_scale = DH ** (-0.5)
    bucket_count = bias_table.shape[0]
    f32 = jnp.float32
    bf16 = jnp.bfloat16
    x_float = layer_in.astype(f32)
    inv_one = lax.rsqrt(jnp.mean(x_float * x_float, axis=1, keepdims=True) + EPS)
    normed_one = x_float * inv_one
    h_one = (normed_one * gain_one).astype(bf16)
    h_one_all = lax.all_gather(h_one, "tp", axis=0, tiled=True)
    w_qkv = jnp.concatenate([w_query, w_key, w_value], axis=1)
    qkv_rows = jnp.dot(h_one_all, w_qkv, preferred_element_type=f32).astype(bf16)
    queries = qkv_rows[:, :width_loc].reshape(group_rows, head_count, DH)
    kv_home = jnp.stack(
        [qkv_rows[:, width_loc : 2 * width_loc], qkv_rows[:, 2 * width_loc :]]
    ).reshape(2, group_rows, head_count, DH)
    ends = jnp.cumsum(lengths)
    bucket_hot = (buckets[:, None] == jnp.arange(bucket_count, dtype=jnp.int32)[None, :]).astype(
        f32
    )
    dist_bias = jnp.dot(bucket_hot, bias_table, precision=HIGH, preferred_element_type=f32)
    row_ids = jnp.arange(BLOCK, dtype=jnp.int32)
    offset_ids = row_ids[:, None] - row_ids[None, :]
    select_same = (row_ids[None, None, :] == jnp.clip(offset_ids, 0, BLOCK - 1)[:, :, None]).astype(
        f32
    )
    select_prev = (
        row_ids[None, None, :] == jnp.minimum(offset_ids + BLOCK, BLOCK - 1)[:, :, None]
    ).astype(f32)
    near_same = jnp.einsum(
        "ijd,dh->hij", select_same, dist_bias, precision=HIGH, preferred_element_type=f32
    )
    near_prev = jnp.einsum(
        "ijd,dh->hij", select_prev, dist_bias, precision=HIGH, preferred_element_type=f32
    )
    far_bias = dist_bias[BLOCK - 1]
    q_info = token_info(block_perm, ends, ctx_index * blocks_group, blocks_group)

    def cycle_pass(kv_pair):
        return shifted(kv_pair, "ctx", 1)

    def attend_forward(state, kv_pair, source):
        k_info = token_info(block_perm, ends, source * blocks_group, blocks_group)

        def one_tile(index, carry):
            q_start = index // tile_count * tile_rows
            k_start = index % tile_count * tile_rows
            q_view = tile_view(q_info, q_start, tile_rows)
            k_view = tile_view(k_info, k_start, tile_rows)

            def update(inner):
                running, row_max, row_total = inner
                allowed, w_same, w_prev, w_far = tile_terms(q_view, k_view)
                q_tile = lax.dynamic_slice_in_dim(queries, q_start, tile_rows, 0)
                k_tile = lax.dynamic_slice_in_dim(kv_pair[0], k_start, tile_rows, 0)
                v_tile = lax.dynamic_slice_in_dim(kv_pair[1], k_start, tile_rows, 0)
                scores = (
                    jnp.einsum("qhd,khd->hqk", q_tile, k_tile, preferred_element_type=f32)
                    * score_scale
                )
                scores = add_bias(scores, w_same, w_prev, w_far, near_same, near_prev, far_bias)
                old_max = lax.dynamic_slice_in_dim(row_max, q_start, tile_rows, 1)
                new_max = jnp.maximum(
                    old_max, jnp.max(jnp.where(allowed[None], scores, NEG), axis=2)
                )
                weights = jnp.where(allowed[None], jnp.exp(scores - new_max[:, :, None]), 0.0)
                factor = jnp.exp(old_max - new_max)
                old_total = lax.dynamic_slice_in_dim(row_total, q_start, tile_rows, 1)
                new_total = old_total * factor + jnp.sum(weights, axis=2)
                old_run = lax.dynamic_slice_in_dim(running, q_start, tile_rows, 0)
                new_run = old_run * factor.T[:, :, None] + jnp.einsum(
                    "hqk,khd->qhd", weights.astype(bf16), v_tile, preferred_element_type=f32
                )
                return (
                    lax.dynamic_update_slice_in_dim(running, new_run, q_start, 0),
                    lax.dynamic_update_slice_in_dim(row_max, new_max, q_start, 1),
                    lax.dynamic_update_slice_in_dim(row_total, new_total, q_start, 1),
                )

            return lax.cond(tile_live(q_view, k_view), update, lambda inner: inner, carry)

        return lax.fori_loop(0, tile_count * tile_count, one_tile, state)

    state = (
        jnp.zeros((group_rows, head_count, DH), f32),
        jnp.full((head_count, group_rows), NEG, f32),
        jnp.zeros((head_count, group_rows), f32),
    )
    state = attend_forward(state, kv_home, ctx_index)

    def forward_turn(turn, carry):
        kv_pair, inner = carry
        kv_pair = cycle_pass(kv_pair)
        return (kv_pair, attend_forward(inner, kv_pair, (ctx_index - turn) % ctx_count))

    _, state = lax.fori_loop(1, ctx_count, forward_turn, (kv_home, state))
    attended = state[0] / state[2].T[:, :, None]
    log_total = state[1] + jnp.log(state[2])
    attended_bf = attended.reshape(group_rows, width_loc).astype(bf16)
    attn_rows = lax.psum_scatter(
        jnp.dot(attended_bf, w_out, preferred_element_type=f32).astype(jnp.bfloat16),
        "tp",
        scatter_dimension=0,
        tiled=True,
    ).astype(jnp.float32)
    mixed_in = x_float + attn_rows
    inv_two = lax.rsqrt(jnp.mean(mixed_in * mixed_in, axis=1, keepdims=True) + EPS)
    normed_two = mixed_in * inv_two
    h_two = (normed_two * gain_two).astype(bf16)
    h_two_all = lax.all_gather(h_two, "tp", axis=0, tiled=True)
    logits = jnp.dot(h_two_all, w_router, preferred_element_type=f32)
    expo = jnp.exp(logits - jnp.max(logits, axis=1, keepdims=True))
    gates = expo / jnp.sum(expo, axis=1, keepdims=True)
    dest, kept, token_of_slot, live = slot_tables(routes, experts, capacity)
    expert_ids = jnp.arange(experts, dtype=jnp.int32)
    chosen = (routes.T[:, :, None] == expert_ids[None, None, :]).astype(f32)
    picked = jnp.sum(gates[None] * chosen, axis=2) * kept
    weight_slot = jnp.zeros((slot_count + 1,), f32).at[dest].set(picked.reshape(-1))[:slot_count]
    expert_in = jnp.where(
        live[:, None] > 0, jnp.take(h_two_all, token_of_slot, axis=0), jnp.zeros((), bf16)
    ).reshape(experts, capacity, width)
    gate_pre = jnp.einsum("ecd,edf->ecf", expert_in, w_gate, preferred_element_type=f32)
    up_pre = jnp.einsum("ecd,edf->ecf", expert_in, w_up, preferred_element_type=f32)
    hidden = (jax.nn.gelu(gate_pre, approximate=True) * up_pre).astype(bf16)
    expert_out = jnp.einsum("ecf,efd->ecd", hidden, w_down, preferred_element_type=f32).reshape(
        slot_count, width
    )
    rows_back = jnp.take(expert_out, jnp.minimum(dest, slot_count - 1), axis=0).reshape(
        top_count, group_rows, width
    )
    mixed_part = jnp.sum(picked[:, :, None] * rows_back, axis=0)
    mixed_rows = lax.psum_scatter(
        mixed_part.astype(jnp.bfloat16), "tp", scatter_dimension=0, tiled=True
    ).astype(jnp.float32)
    layer_out = mixed_in + mixed_rows
    grad_float = cotangent.astype(f32)
    grad_all = lax.all_gather(cotangent, "tp", axis=0, tiled=True)
    gate_dots = jnp.sum(rows_back * grad_all.astype(f32)[None], axis=2)
    d_expert_out = (
        (jnp.take(grad_all, token_of_slot, axis=0).astype(f32) * weight_slot[:, None])
        .astype(bf16)
        .reshape(experts, capacity, width)
    )
    d_hidden = jnp.einsum("ecd,efd->ecf", d_expert_out, w_down, preferred_element_type=f32)
    grad_down = jnp.einsum("ecf,ecd->efd", hidden, d_expert_out, preferred_element_type=f32)
    _, glu_pull = jax.vjp(
        lambda gate_val, up_val: jax.nn.gelu(gate_val, approximate=True) * up_val, gate_pre, up_pre
    )
    d_gate_pre, d_up_pre = glu_pull(d_hidden)
    d_gate_bf = d_gate_pre.astype(bf16)
    d_up_bf = d_up_pre.astype(bf16)
    grad_gate = jnp.einsum("ecd,ecf->edf", expert_in, d_gate_bf, preferred_element_type=f32)
    grad_up = jnp.einsum("ecd,ecf->edf", expert_in, d_up_bf, preferred_element_type=f32)
    d_expert_in = (
        jnp.einsum("ecf,edf->ecd", d_gate_bf, w_gate, preferred_element_type=f32)
        + jnp.einsum("ecf,edf->ecd", d_up_bf, w_up, preferred_element_type=f32)
    ).reshape(slot_count, width)
    d_h_two_part = (
        jnp.zeros((group_rows, width), f32).at[token_of_slot].add(d_expert_in * live[:, None])
    )
    d_h_two, dots_own = (
        lax.psum_scatter(
            d_h_two_part.astype(jnp.bfloat16), "tp", scatter_dimension=0, tiled=True
        ).astype(jnp.float32),
        lax.psum_scatter(
            gate_dots.T.astype(jnp.bfloat16), "tp", scatter_dimension=0, tiled=True
        ).astype(jnp.float32),
    )
    own_start = tp_index * rows_dev
    gates_own = lax.dynamic_slice_in_dim(gates, own_start, rows_dev, 0)
    routes_own = lax.dynamic_slice_in_dim(routes, own_start, rows_dev, 0)
    kept_own = lax.dynamic_slice_in_dim(kept, own_start, rows_dev, 1)
    hot_own = (routes_own[:, :, None] == expert_ids[None, None, :]).astype(f32)
    d_gates = jnp.sum((dots_own * kept_own.T)[:, :, None] * hot_own, axis=1)
    d_logits = gates_own * (d_gates - jnp.sum(gates_own * d_gates, axis=1, keepdims=True))
    d_h_two = d_h_two + jnp.dot(
        d_logits, w_router.astype(f32).T, precision=HIGH, preferred_element_type=f32
    )
    grad_router_part = jnp.dot(h_two.T, d_logits, precision=HIGH, preferred_element_type=f32)
    d_norm_two = d_h_two * gain_two
    grad_gain_two_part = jnp.sum(d_h_two * normed_two, axis=0)
    d_mixed = grad_float + inv_two * (
        d_norm_two - normed_two * jnp.mean(d_norm_two * normed_two, axis=1, keepdims=True)
    )
    d_attn = d_mixed.astype(bf16)
    piece = lax.all_gather(d_attn, "tp", axis=0, tiled=True)
    d_attended = jnp.einsum("rd,hd->rh", piece, w_out, preferred_element_type=f32)
    grad_out_part = jnp.einsum("rh,rd->hd", attended_bf, piece, preferred_element_type=f32)
    d_attended, grad_out = (d_attended, grad_out_part)
    d_att_bf = d_attended.astype(bf16).reshape(group_rows, head_count, DH)
    row_dsum = jnp.sum(d_att_bf.astype(f32) * attended, axis=2).T

    def attend_back(carry, kv_pair, pair_grads, source):
        k_info = token_info(block_perm, ends, source * blocks_group, blocks_group)

        def one_tile(index, inner):
            q_start = index // tile_count * tile_rows
            k_start = index % tile_count * tile_rows
            q_view = tile_view(q_info, q_start, tile_rows)
            k_view = tile_view(k_info, k_start, tile_rows)

            def update(values_in):
                d_queries, same_sum, prev_sum, far_sum, grads_in = values_in
                allowed, w_same, w_prev, w_far = tile_terms(q_view, k_view)
                q_tile = lax.dynamic_slice_in_dim(queries, q_start, tile_rows, 0)
                k_tile = lax.dynamic_slice_in_dim(kv_pair[0], k_start, tile_rows, 0)
                v_tile = lax.dynamic_slice_in_dim(kv_pair[1], k_start, tile_rows, 0)
                do_tile = lax.dynamic_slice_in_dim(d_att_bf, q_start, tile_rows, 0)
                lse_tile = lax.dynamic_slice_in_dim(log_total, q_start, tile_rows, 1)
                dsum_tile = lax.dynamic_slice_in_dim(row_dsum, q_start, tile_rows, 1)
                scores = (
                    jnp.einsum("qhd,khd->hqk", q_tile, k_tile, preferred_element_type=f32)
                    * score_scale
                )
                scores = add_bias(scores, w_same, w_prev, w_far, near_same, near_prev, far_bias)
                probs = jnp.where(allowed[None], jnp.exp(scores - lse_tile[:, :, None]), 0.0)
                dv_add = jnp.einsum(
                    "hqk,qhd->khd", probs.astype(bf16), do_tile, preferred_element_type=f32
                )
                d_probs = jnp.einsum("qhd,khd->hqk", do_tile, v_tile, preferred_element_type=f32)
                d_scores = (probs * (d_probs - dsum_tile[:, :, None])).astype(bf16)
                dq_add = (
                    jnp.einsum("hqk,khd->qhd", d_scores, k_tile, preferred_element_type=f32)
                    * score_scale
                )
                dk_add = (
                    jnp.einsum("hqk,qhd->khd", d_scores, q_tile, preferred_element_type=f32)
                    * score_scale
                )
                split = d_scores.astype(f32).reshape(
                    head_count, tile_rows // BLOCK, BLOCK, tile_rows // BLOCK, BLOCK
                )
                same_sum = same_sum + jnp.einsum("haibj,ab->hij", split, w_same)
                prev_sum = prev_sum + jnp.einsum("haibj,ab->hij", split, w_prev)
                far_sum = far_sum + jnp.einsum("haibj,ab->h", split, w_far)
                old_q = lax.dynamic_slice_in_dim(d_queries, q_start, tile_rows, 0)
                d_queries = lax.dynamic_update_slice_in_dim(d_queries, old_q + dq_add, q_start, 0)
                old_kv = lax.dynamic_slice_in_dim(grads_in, k_start, tile_rows, 1)
                grads_in = lax.dynamic_update_slice_in_dim(
                    grads_in, old_kv + jnp.stack([dk_add, dv_add]), k_start, 1
                )
                return (d_queries, same_sum, prev_sum, far_sum, grads_in)

            return lax.cond(tile_live(q_view, k_view), update, lambda values_in: values_in, inner)

        result = lax.fori_loop(0, tile_count * tile_count, one_tile, carry + (pair_grads,))
        return (result[:4], result[4])

    back_state = (
        jnp.zeros((group_rows, head_count, DH), f32),
        jnp.zeros((head_count, BLOCK, BLOCK), f32),
        jnp.zeros((head_count, BLOCK, BLOCK), f32),
        jnp.zeros((head_count,), f32),
    )
    zero_pair = jnp.zeros((2, group_rows, head_count, DH), f32)

    def pass_grads(pair_grads):
        return shifted(pair_grads.astype(jnp.bfloat16), "ctx", 1).astype(pair_grads.dtype)

    back_state, pair_grads = attend_back(back_state, kv_home, zero_pair, ctx_index)

    def back_turn(turn, carry):
        kv_pair, grads_now, inner = carry
        kv_pair = cycle_pass(kv_pair)
        grads_now = pass_grads(grads_now)
        inner, grads_now = attend_back(inner, kv_pair, grads_now, (ctx_index - turn) % ctx_count)
        return (kv_pair, grads_now, inner)

    _, pair_grads, back_state = lax.fori_loop(
        1, ctx_count, back_turn, (kv_home, pair_grads, back_state)
    )
    key_grads = pass_grads(pair_grads)
    d_queries, same_sum, prev_sum, far_sum = back_state
    d_cat = jnp.concatenate(
        [
            d_queries.reshape(group_rows, width_loc).astype(bf16),
            key_grads[0].reshape(group_rows, width_loc).astype(bf16),
            key_grads[1].reshape(group_rows, width_loc).astype(bf16),
        ],
        axis=1,
    )
    grad_qkv = jnp.einsum("rd,rh->dh", h_one_all, d_cat, preferred_element_type=f32)
    d_dist = jnp.einsum(
        "ijd,hij->hd", select_same, same_sum, precision=HIGH, preferred_element_type=f32
    ) + jnp.einsum("ijd,hij->hd", select_prev, prev_sum, precision=HIGH, preferred_element_type=f32)
    d_dist = d_dist.at[:, BLOCK - 1].add(far_sum)
    grad_table_part = jnp.dot(bucket_hot.T, d_dist.T, precision=HIGH, preferred_element_type=f32)
    d_h_one_part = jnp.einsum("rh,dh->rd", d_cat, w_qkv, preferred_element_type=f32)
    d_h_one = lax.psum_scatter(
        d_h_one_part.astype(jnp.bfloat16), "tp", scatter_dimension=0, tiled=True
    ).astype(jnp.float32)
    d_norm_one = d_h_one * gain_one
    grad_gain_one_part = jnp.sum(d_h_one * normed_one, axis=0)
    grad_x = d_mixed + inv_one * (
        d_norm_one - normed_one * jnp.mean(d_norm_one * normed_one, axis=1, keepdims=True)
    )
    gain_one_share, gain_two_share, router_share = (
        lax.psum_scatter(grad_gain_one_part, "tp", scatter_dimension=0, tiled=True),
        lax.psum_scatter(grad_gain_two_part, "tp", scatter_dimension=0, tiled=True),
        lax.psum_scatter(grad_router_part, "tp", scatter_dimension=0, tiled=True),
    )
    rest_total = (
        lax.psum(grad_qkv[:, :width_loc].astype(jnp.bfloat16), "ctx").astype(jnp.float32),
        lax.psum(grad_qkv[:, width_loc : 2 * width_loc].astype(jnp.bfloat16), "ctx").astype(
            jnp.float32
        ),
        lax.psum(grad_qkv[:, 2 * width_loc :].astype(jnp.bfloat16), "ctx").astype(jnp.float32),
        lax.psum(grad_out.astype(jnp.bfloat16), "ctx").astype(jnp.float32),
        lax.psum(grad_table_part.astype(jnp.bfloat16), "ctx").astype(jnp.float32),
        lax.psum(gain_one_share.astype(jnp.bfloat16), "ctx").astype(jnp.float32),
        lax.psum(gain_two_share.astype(jnp.bfloat16), "ctx").astype(jnp.float32),
        lax.psum(router_share.astype(jnp.bfloat16), "ctx").astype(jnp.float32),
    )
    return (
        layer_out,
        grad_x,
        rest_total[5],
        rest_total[0],
        rest_total[1],
        rest_total[2],
        rest_total[3],
        rest_total[4],
        rest_total[6],
        rest_total[7],
        lax.psum(grad_gate.astype(jnp.bfloat16), "ctx").astype(jnp.float32),
        lax.psum(grad_up.astype(jnp.bfloat16), "ctx").astype(jnp.float32),
        lax.psum(grad_down.astype(jnp.bfloat16), "ctx").astype(jnp.float32),
    )


def solution(mesh):
    placed = (
        P(("ctx", "tp"), None),
        P(),
        P(None, "tp"),
        P(None, "tp"),
        P(None, "tp"),
        P("tp", None),
        P(None, "tp"),
        P(),
        P(),
        P(None, None, "tp"),
        P(None, None, "tp"),
        P(None, "tp", None),
        P(),
        P(),
        P(),
        P("ctx", None),
        P(("ctx", "tp"), None),
    )
    return jax.shard_map(
        on_device,
        mesh=mesh,
        in_specs=placed,
        out_specs=(
            P(("ctx", "tp"), None),
            P(("ctx", "tp"), None),
            P("tp"),
            P(None, "tp"),
            P(None, "tp"),
            P(None, "tp"),
            P("tp", None),
            P(None, "tp"),
            P("tp"),
            P("tp", None),
            P(None, None, "tp"),
            P(None, None, "tp"),
            P(None, "tp", None),
        ),
        check_vma=False,
    )
```

profile of v0, /device:TPU:0, one launch (start us, length us, event | category | flops | bytes accessed | tf_op | source)
XLA Modules:
  0.0 4828.2 jit_solution(918960752415724423)
XLA Ops:
  69.3 181.8 %while.183 = (s32[]{:T(128)}, f32[1024,4,64]{0,2,1:T(8,128)}, f32[4,1024]{1,0:T(4,128)S(1)}, f32[4,1024]{1,0:T(4,128)S(1)}, s32[8]{0:T(128)S(1)}, /*index=5*/s32...) while((s32[]{:T(128)}, f32[1024,4,64]{0,2,1:T(8,128)}, ...), condition=%wide.region_9.10_spmd.clone, body=%wide.region_3.9_spmd.clone.sunk | while | flops 284171584 | bytes 80132280 | solution.py:203
  251.6 1385.8 %while.185 = (s32[]{:T(128)}, bf16[2,1024,4,64]{1,3,2,0:T(8,128)(2,1)}, f32[1024,4,64]{0,2,1:T(8,128)}, f32[4,1024]{1,0:T(4,128)S(1)}, f32[4,1024]{1,0:T(4,128)S...) while((s32[]{:T(128)}, ...), condition=%wide.region_19.20_spmd.clone, body=%wide.region_10.19_spmd.clone.sunk | while | flops 284221792 | bytes 86441136 | solution.py:217
  267.6 180.2 %while.189 = (s32[]{:T(128)}, f32[1024,4,64]{0,2,1:T(8,128)}, f32[4,1024]{1,0:T(4,128)S(1)}, f32[4,1024]{1,0:T(4,128)S(1)}, s32[8]{0:T(128)S(1)}, /*index=5*/s32...) while((s32[]{:T(128)}, f32[1024,4,64]{0,2,1:T(8,128)}, ...), condition=%wide.region_18.18_spmd.clone, body=%wide.region_12.17_spmd.clone.sunk | while | flops 284171584 | bytes 80132336 | solution.py:203
  465.5 180.2 %while.189 = (s32[]{:T(128)}, f32[1024,4,64]{0,2,1:T(8,128)}, f32[4,1024]{1,0:T(4,128)S(1)}, f32[4,1024]{1,0:T(4,128)S(1)}, s32[8]{0:T(128)S(1)}, /*index=5*/s32...) while((s32[]{:T(128)}, f32[1024,4,64]{0,2,1:T(8,128)}, ...), condition=%wide.region_18.18_spmd.clone, body=%wide.region_12.17_spmd.clone.sunk | while | flops 284171584 | bytes 80132336 | solution.py:203
  663.4 180.2 %while.189 = (s32[]{:T(128)}, f32[1024,4,64]{0,2,1:T(8,128)}, f32[4,1024]{1,0:T(4,128)S(1)}, f32[4,1024]{1,0:T(4,128)S(1)}, s32[8]{0:T(128)S(1)}, /*index=5*/s32...) while((s32[]{:T(128)}, f32[1024,4,64]{0,2,1:T(8,128)}, ...), condition=%wide.region_18.18_spmd.clone, body=%wide.region_12.17_spmd.clone.sunk | while | flops 284171584 | bytes 80132336 | solution.py:203
  861.3 180.2 %while.189 = (s32[]{:T(128)}, f32[1024,4,64]{0,2,1:T(8,128)}, f32[4,1024]{1,0:T(4,128)S(1)}, f32[4,1024]{1,0:T(4,128)S(1)}, s32[8]{0:T(128)S(1)}, /*index=5*/s32...) while((s32[]{:T(128)}, f32[1024,4,64]{0,2,1:T(8,128)}, ...), condition=%wide.region_18.18_spmd.clone, body=%wide.region_12.17_spmd.clone.sunk | while | flops 284171584 | bytes 80132336 | solution.py:203
  1059.2 180.2 %while.189 = (s32[]{:T(128)}, f32[1024,4,64]{0,2,1:T(8,128)}, f32[4,1024]{1,0:T(4,128)S(1)}, f32[4,1024]{1,0:T(4,128)S(1)}, s32[8]{0:T(128)S(1)}, /*index=5*/s32...) while((s32[]{:T(128)}, f32[1024,4,64]{0,2,1:T(8,128)}, ...), condition=%wide.region_18.18_spmd.clone, body=%wide.region_12.17_spmd.clone.sunk | while | flops 284171584 | bytes 80132336 | solution.py:203
  1257.1 180.2 %while.189 = (s32[]{:T(128)}, f32[1024,4,64]{0,2,1:T(8,128)}, f32[4,1024]{1,0:T(4,128)S(1)}, f32[4,1024]{1,0:T(4,128)S(1)}, s32[8]{0:T(128)S(1)}, /*index=5*/s32...) while((s32[]{:T(128)}, f32[1024,4,64]{0,2,1:T(8,128)}, ...), condition=%wide.region_18.18_spmd.clone, body=%wide.region_12.17_spmd.clone.sunk | while | flops 284171584 | bytes 80132336 | solution.py:203
  1455.0 180.2 %while.189 = (s32[]{:T(128)}, f32[1024,4,64]{0,2,1:T(8,128)}, f32[4,1024]{1,0:T(4,128)S(1)}, f32[4,1024]{1,0:T(4,128)S(1)}, s32[8]{0:T(128)S(1)}, /*index=5*/s32...) while((s32[]{:T(128)}, f32[1024,4,64]{0,2,1:T(8,128)}, ...), condition=%wide.region_18.18_spmd.clone, body=%wide.region_12.17_spmd.clone.sunk | while | flops 284171584 | bytes 80132336 | solution.py:203
  2034.3 273.4 %while.186 = (s32[]{:T(128)}, f32[1024,4,64]{0,2,1:T(8,128)}, f32[4,128,128]{2,1,0:T(8,128)}, f32[4,128,128]{2,1,0:T(8,128)}, f32[4]{0:T(128)S(1)}, /*index=5*/f...) while((s32[]{:T(128)}, f32[1024,4,64]{0,2,1:T(8,128)}, ...), condition=%wide.region_46.48_spmd.clone, body=%wide.region_41.47_spmd.clone.sunk | while | flops 691799424 | bytes 116210392 | solution.py:367
  2308.2 2116.2 %while.188 = (s32[]{:T(128)}, bf16[2,1024,4,64]{1,3,2,0:T(8,128)(2,1)}, f32[2,1024,4,64]{1,3,2,0:T(8,128)}, f32[1024,4,64]{0,2,1:T(8,128)}, f32[4,128,128]{2,1,0...) while((s32[]{:T(128)}, ...), condition=%wide.region_55.57_spmd.clone, body=%wide.region_47.56_spmd.clone.sunk | while | flops 692898176 | bytes 133005296 | solution.py:390
  2336.7 271.7 %while.190 = (s32[]{:T(128)}, f32[1024,4,64]{0,2,1:T(8,128)}, f32[4,128,128]{2,1,0:T(8,128)}, f32[4,128,128]{2,1,0:T(8,128)}, f32[4]{0:T(128)S(1)}, /*index=5*/f...) while((s32[]{:T(128)}, f32[1024,4,64]{0,2,1:T(8,128)}, ...), condition=%wide.region_54.55_spmd.clone, body=%wide.region_49.54_spmd.clone.sunk | while | flops 691799424 | bytes 116210448 | solution.py:367
  2638.9 271.7 %while.190 = (s32[]{:T(128)}, f32[1024,4,64]{0,2,1:T(8,128)}, f32[4,128,128]{2,1,0:T(8,128)}, f32[4,128,128]{2,1,0:T(8,128)}, f32[4]{0:T(128)S(1)}, /*index=5*/f...) while((s32[]{:T(128)}, f32[1024,4,64]{0,2,1:T(8,128)}, ...), condition=%wide.region_54.55_spmd.clone, body=%wide.region_49.54_spmd.clone.sunk | while | flops 691799424 | bytes 116210448 | solution.py:367
  2640.6 67.0 %conditional.14 = ((f32[1024,4,64]{0,2,1:T(8,128)}, f32[4,128,128]{2,1,0:T(8,128)}, f32[4,128,128]{2,1,0:T(8,128)}, f32[4]{0:T(128)S(1)}, f32[2,1024,4,64]{1,3,2,0:T(8,128)})) conditional(s32[]{:T(128)} %convert_element_type.652, (f32[1024,4,64]{0,2,1:T(8,128)}, f32[4,128,128]{2,1,0:T(8,128)}, f32[4,128,128]{2,1,0:T(8,128)}, f32[4]{0:T(128)S(1)}, ...), branch_computations={%region_51.51_spmd, %region_52.53_spmd} | conditional | flops 691798272 | bytes 116205104 | solution.py:365
  2941.2 271.7 %while.190 = (s32[]{:T(128)}, f32[1024,4,64]{0,2,1:T(8,128)}, f32[4,128,128]{2,1,0:T(8,128)}, f32[4,128,128]{2,1,0:T(8,128)}, f32[4]{0:T(128)S(1)}, /*index=5*/f...) while((s32[]{:T(128)}, f32[1024,4,64]{0,2,1:T(8,128)}, ...), condition=%wide.region_54.55_spmd.clone, body=%wide.region_49.54_spmd.clone.sunk | while | flops 691799424 | bytes 116210448 | solution.py:367
  2942.9 67.0 %conditional.14 = ((f32[1024,4,64]{0,2,1:T(8,128)}, f32[4,128,128]{2,1,0:T(8,128)}, f32[4,128,128]{2,1,0:T(8,128)}, f32[4]{0:T(128)S(1)}, f32[2,1024,4,64]{1,3,2,0:T(8,128)})) conditional(s32[]{:T(128)} %convert_element_type.652, (f32[1024,4,64]{0,2,1:T(8,128)}, f32[4,128,128]{2,1,0:T(8,128)}, f32[4,128,128]{2,1,0:T(8,128)}, f32[4]{0:T(128)S(1)}, ...), branch_computations={%region_51.51_spmd, %region_52.53_spmd} | conditional | flops 691798272 | bytes 116205104 | solution.py:365
  3243.4 271.7 %while.190 = (s32[]{:T(128)}, f32[1024,4,64]{0,2,1:T(8,128)}, f32[4,128,128]{2,1,0:T(8,128)}, f32[4,128,128]{2,1,0:T(8,128)}, f32[4]{0:T(128)S(1)}, /*index=5*/f...) while((s32[]{:T(128)}, f32[1024,4,64]{0,2,1:T(8,128)}, ...), condition=%wide.region_54.55_spmd.clone, body=%wide.region_49.54_spmd.clone.sunk | while | flops 691799424 | bytes 116210448 | solution.py:367
  3245.2 67.0 %conditional.14 = ((f32[1024,4,64]{0,2,1:T(8,128)}, f32[4,128,128]{2,1,0:T(8,128)}, f32[4,128,128]{2,1,0:T(8,128)}, f32[4]{0:T(128)S(1)}, f32[2,1024,4,64]{1,3,2,0:T(8,128)})) conditional(s32[]{:T(128)} %convert_element_type.652, (f32[1024,4,64]{0,2,1:T(8,128)}, f32[4,128,128]{2,1,0:T(8,128)}, f32[4,128,128]{2,1,0:T(8,128)}, f32[4]{0:T(128)S(1)}, ...), branch_computations={%region_51.51_spmd, %region_52.53_spmd} | conditional | flops 691798272 | bytes 116205104 | solution.py:365
  3545.7 271.7 %while.190 = (s32[]{:T(128)}, f32[1024,4,64]{0,2,1:T(8,128)}, f32[4,128,128]{2,1,0:T(8,128)}, f32[4,128,128]{2,1,0:T(8,128)}, f32[4]{0:T(128)S(1)}, /*index=5*/f...) while((s32[]{:T(128)}, f32[1024,4,64]{0,2,1:T(8,128)}, ...), condition=%wide.region_54.55_spmd.clone, body=%wide.region_49.54_spmd.clone.sunk | while | flops 691799424 | bytes 116210448 | solution.py:367
  3547.4 67.0 %conditional.14 = ((f32[1024,4,64]{0,2,1:T(8,128)}, f32[4,128,128]{2,1,0:T(8,128)}, f32[4,128,128]{2,1,0:T(8,128)}, f32[4]{0:T(128)S(1)}, f32[2,1024,4,64]{1,3,2,0:T(8,128)})) conditional(s32[]{:T(128)} %convert_element_type.652, (f32[1024,4,64]{0,2,1:T(8,128)}, f32[4,128,128]{2,1,0:T(8,128)}, f32[4,128,128]{2,1,0:T(8,128)}, f32[4]{0:T(128)S(1)}, ...), branch_computations={%region_51.51_spmd, %region_52.53_spmd} | conditional | flops 691798272 | bytes 116205104 | solution.py:365
  3847.9 271.7 %while.190 = (s32[]{:T(128)}, f32[1024,4,64]{0,2,1:T(8,128)}, f32[4,128,128]{2,1,0:T(8,128)}, f32[4,128,128]{2,1,0:T(8,128)}, f32[4]{0:T(128)S(1)}, /*index=5*/f...) while((s32[]{:T(128)}, f32[1024,4,64]{0,2,1:T(8,128)}, ...), condition=%wide.region_54.55_spmd.clone, body=%wide.region_49.54_spmd.clone.sunk | while | flops 691799424 | bytes 116210448 | solution.py:367
  4150.2 271.7 %while.190 = (s32[]{:T(128)}, f32[1024,4,64]{0,2,1:T(8,128)}, f32[4,128,128]{2,1,0:T(8,128)}, f32[4,128,128]{2,1,0:T(8,128)}, f32[4]{0:T(128)S(1)}, /*index=5*/f...) while((s32[]{:T(128)}, f32[1024,4,64]{0,2,1:T(8,128)}, ...), condition=%wide.region_54.55_spmd.clone, body=%wide.region_49.54_spmd.clone.sunk | while | flops 691799424 | bytes 116210448 | solution.py:367
  4151.9 67.0 %conditional.14 = ((f32[1024,4,64]{0,2,1:T(8,128)}, f32[4,128,128]{2,1,0:T(8,128)}, f32[4,128,128]{2,1,0:T(8,128)}, f32[4]{0:T(128)S(1)}, f32[2,1024,4,64]{1,3,2,0:T(8,128)})) conditional(s32[]{:T(128)} %convert_element_type.652, (f32[1024,4,64]{0,2,1:T(8,128)}, f32[4,128,128]{2,1,0:T(8,128)}, f32[4,128,128]{2,1,0:T(8,128)}, f32[4]{0:T(128)S(1)}, ...), branch_computations={%region_51.51_spmd, %region_52.53_spmd} | conditional | flops 691798272 | bytes 116205104 | solution.py:365
  4542.9 252.4 %all-reduce.7.cloned.1.call-done = (bf16[1024,256]{1,0:T(8,128)(2,1)}, bf16[1024,256]{1,0:T(8,128)(2,1)}, bf16[1024,256]{1,0:T(8,128)(2,1)}, bf16[256,1024]{1,0:...) async-done(((bf16[1024,256]{1,0:T(8,128)(2,1)}, bf16[1024,256]{1,0:T(8,128)(2,1)}, ...) | async-done | bytes 19398672 | tf_op jit(solution)/shard_map/psum | solution.py:424
  (2945 shorter events, 7678.5 us)
Async XLA Ops:
  7.2 52.8 %all-gather.5.cloned.1.call-start = ((), (), s32[]{:S(2)}) async-start(), calls=%async_computation.6 | async-start | bytes 2621440 | tf_op jit(solution)/shard_map/all_gather | solution.py:131
  11.3 1672.7 %reduce-scatter.11.cloned.1.call-start = ((), (), s32[]{:S(2)}) async-start(), calls=%async_computation.7 | async-start | bytes 2621440 | tf_op jit(solution)/shard_map/reduce_scatter | solution.py:221
  252.1 15.5 collective-permute-start.2
  450.1 15.4 collective-permute-start.2
  648.0 15.4 collective-permute-start.2
  1043.8 15.4 collective-permute-start.2
  1241.6 15.4 collective-permute-start.2
  1439.5 15.4 collective-permute-start.2
  1641.8 89.2 %all-gather.9.cloned.1.call-start = ((), (), s32[]{:S(2)}) async-start(), calls=%async_computation.10 | async-start | bytes 2621440 | tf_op jit(solution)/shard_map/all_gather | solution.py:258
  1642.5 135.1 %all-gather.7.cloned.1.call-start = ((), (), s32[]{:S(2)}) async-start(), calls=%async_computation.8 | async-start | bytes 2621440 | tf_op jit(solution)/shard_map/all_gather | solution.py:231
  1687.4 247.3 %reduce-scatter.19.cloned.1.call-start = ((), (), s32[]{:S(2)}) async-start(), calls=%async_computation.14 | async-start | bytes 327680
  1889.0 88.4 %reduce-scatter.15.cloned.1.call-start = ((), (), s32[]{:S(2)}) async-start(), calls=%async_computation.11 | async-start | bytes 2621440 | tf_op jit(solution)/shard_map/reduce_scatter | solution.py:283
  1934.6 92.0 %all-gather.11.cloned.1.call-start = ((), (), s32[]{:S(2)}) async-start(), calls=%async_computation.12 | async-start | bytes 2621440 | tf_op jit(solution)/shard_map/all_gather | solution.py:307
  1981.2 2504.3 %reduce-scatter.21.cloned.1.call-start = ((), (), s32[]{:S(2)}) async-start(), calls=%async_computation.15 | async-start | bytes 655360
  2310.2 26.4 collective-permute-start
  2612.5 26.4 collective-permute-start
  2914.7 26.4 collective-permute-start
  3217.0 26.4 collective-permute-start
  3519.2 26.4 collective-permute-start
  3821.5 26.4 collective-permute-start
  4123.7 26.4 collective-permute-start
  4428.8 67.2 %reduce-scatter.17.cloned.1.call-start = ((), (), s32[]{:S(2)}) async-start(), calls=%async_computation.13 | async-start | bytes 2621440 | tf_op jit(solution)/shard_map/reduce_scatter | solution.py:410
  4446.0 93.6 %reduce-scatter.13.cloned.1.call-start = ((), (), s32[]{:S(2)}) async-start(), calls=%async_computation.9 | async-start | bytes 2621440 | tf_op jit(solution)/shard_map/reduce_scatter | solution.py:253
  4452.0 343.3 %all-reduce.7.cloned.1.call-start = ((), (), s32[]{:S(2)}) async-start(), calls=%async_computation.16 | async-start | bytes 38797312 | tf_op jit(solution)/shard_map/psum | solution.py:424
  (189 other events, 8654.2 us)
Sparse Core Ops, SparseCore 0:
  11.4 48.6 all-gather.4
  1641.9 42.0 reduce-scatter.10
  1685.6 45.2 all-gather.8
  1733.0 44.5 all-gather.6
  1889.1 18.4 reduce-scatter.18
  1934.7 42.5 reduce-scatter.14
  1981.4 45.2 all-gather.10
  4428.9 20.5 reduce-scatter.20
  4451.9 42.2 reduce-scatter.16
  4496.3 43.2 reduce-scatter.12
  4546.7 248.5 all-reduce.6
where the time goes:
time: 4870 us; the launch traced here: 4830 us
  local copies, waits for them, and re-layouts  2450 us (50%)
  matrix products  991 us (20%)
  waiting for transfers between devices  743 us (15%)
  other arithmetic  553 us (11%)
  loops' own time  49.6 us (1%)
    mul x256, local copies, waits for them, and re-layouts, add_bias(): w_prev[None, :, None, :, None] * near_prev[:, None, :, None, :]  615 us
    mul x192, local copies, waits for them, and re-layouts, add_bias(): w_same[None, :, None, :, None] * near_same[:, None, :, None, :]  604 us
    add x128, local copies, waits for them, and re-layouts, add_bias(): split + w_far[None, :, None, :, None] * far_bias[:, None, None, None, None]  517 us
    dot_general x64, matrix products, update(): jnp.einsum('qhd,khd->hqk', q_tile, k_tile, preferred_element_type=f32)  432 us
    ppermute x22, waiting for transfers between devices, shifted(): return lax.ppermute(block, axis, route)  260 us
    psum x1, waiting for transfers between devices, on_device(): lax.psum(grad_qkv[:, :width_loc].astype(jnp.bfloat16), 'ctx')  252 us
    dynamic_update_slice x32, local copies, waits for them, and re-layouts, update(): lax.dynamic_update_slice_in_dim(grads_in, old_kv + jnp.stack([dk_add, dv_...  173 us
    slice x64, local copies, waits for them, and re-layouts, update(): v_tile = lax.dynamic_slice_in_dim(kv_pair[1], k_start, tile_rows, 0)  108 us
  transfers between devices with their start and end apart: 33, of which 30 were waited for; matrix products, arithmetic and copies ran while one was open for 4% of the time, Pallas kernels for 0%

commit v1 on v0

v1 whole, which is shorter than its diff:
```python
import functools

import jax
import jax.numpy as jnp
from jax import lax
from jax.experimental import pallas as pl
from jax.experimental.pallas import tpu as pltpu
from jax.sharding import PartitionSpec as P

DH = 64
BLOCK = 128


EPS = 1e-06
NEG = -1e30
HIGH = lax.Precision.HIGHEST


LOG2E = 1.4426950408889634
KT = 512
VMEM_LIMIT = 56 * 1024 * 1024


def dot(left, right):
    return jnp.dot(left, right, preferred_element_type=jnp.float32)


def place_pairs(nat_ref, part_refs, k_row, count, keys_flat, keys_tall):
    keys_flat[:, :BLOCK] = jnp.zeros((2 * DH, BLOCK), keys_flat.dtype)
    keys_tall[:BLOCK, :] = jnp.zeros((BLOCK, 2 * DH), keys_tall.dtype)
    for part, ref in enumerate(part_refs):
        row = k_row if part == 0 else 0

        def one(index, _, part=part, ref=ref, row=row):
            at = pl.multiple_of((nat_ref[part * count + index] + 1) * BLOCK, BLOCK)
            pair = ref[index, row : row + 2 * DH, :]
            keys_flat[:, pl.ds(at, BLOCK)] = pair
            keys_tall[pl.ds(at, BLOCK), :] = pair.T
            return 0

        lax.fori_loop(0, count, one, 0)


def fill_near_bias(thr_ref, tab_ref, near_bias, bucket_count):
    key_ids = lax.broadcasted_iota(jnp.int32, (2 * BLOCK, BLOCK), 0)
    query_ids = lax.broadcasted_iota(jnp.int32, (2 * BLOCK, BLOCK), 1)
    distance = query_ids + BLOCK - key_ids
    value = jnp.full((2 * BLOCK, BLOCK), tab_ref[0], jnp.float32)
    for bucket in range(1, bucket_count):
        value = jnp.where(distance >= thr_ref[bucket], tab_ref[bucket], value)
    near_bias[...] = jnp.where(distance >= 0, value, NEG)


def pair_ids(nat_ref, tile, order_ref):
    slot_a = order_ref[2 * tile]
    slot_b = order_ref[2 * tile + 1]
    return slot_a, slot_b, nat_ref[slot_a], nat_ref[slot_b]


def lane_pair(first, second):
    return jnp.concatenate([first, second], axis=1)


def forward_kernel(
    bucket_count,
    parts,
    nat_ref,
    order_ref,
    low_ref,
    thr_ref,
    tab_ref,
    seq_ref,
    *rest,
):
    part_refs = rest[:parts]
    out_ref, full_ref, lse_ref = rest[parts : parts + 3]
    keys_flat, keys_tall, near_bias = rest[parts + 3 :]
    own_ref = part_refs[0]
    count = own_ref.shape[0]
    total = keys_tall.shape[0] - BLOCK
    scale = DH ** (-0.5) * LOG2E
    bf16 = jnp.bfloat16
    place_pairs(nat_ref, part_refs, DH, count, keys_flat, keys_tall)
    fill_near_bias(thr_ref, tab_ref, near_bias, bucket_count)
    near_ids = lax.broadcasted_iota(jnp.int32, (2 * BLOCK, BLOCK), 0)
    far_ids = lax.broadcasted_iota(jnp.int32, (KT, 2 * BLOCK), 0)

    def one_tile(tile, _):
        slot_a, slot_b, blk_a, blk_b = pair_ids(nat_ref, tile, order_ref)
        q_pair = lane_pair(own_ref[slot_a, :DH, :], own_ref[slot_b, :DH, :])
        q_wide = jnp.concatenate([q_pair, jnp.zeros_like(q_pair)], axis=0)
        starts = []
        stats = []
        for half, blk in enumerate((blk_a, blk_b)):
            at = pl.multiple_of(blk * BLOCK, BLOCK)
            start = seq_ref[pl.ds(blk, 1), :]
            starts.append(start)
            s = dot(
                keys_tall[pl.ds(at, 2 * BLOCK), :],
                q_wide[:, half * BLOCK : (half + 1) * BLOCK],
            )
            s = s * scale + near_bias[...]
            s = jnp.where(near_ids >= start - (blk - 1) * BLOCK, s, NEG)
            top = jnp.max(s, axis=0, keepdims=True)
            p = jnp.exp2(s - top)
            acc = dot(keys_flat[DH:, pl.ds(at, 2 * BLOCK)], p.astype(bf16))
            stats.append((top, jnp.sum(p, axis=0, keepdims=True), acc))
        top = lane_pair(stats[0][0], stats[1][0])
        norm = lane_pair(stats[0][1], stats[1][1])
        acc = lane_pair(stats[0][2], stats[1][2])
        start = lane_pair(*starts)
        lane = lax.broadcasted_iota(jnp.int32, (1, 2 * BLOCK), 1)
        stop = jnp.where(lane < BLOCK, (blk_a - 1) * BLOCK, (blk_b - 1) * BLOCK)
        first = low_ref[blk_a] * BLOCK
        steps = (jnp.maximum((blk_b - 1) * BLOCK - first, 0) + KT - 1) // KT

        def far(step, carry):
            top, norm, acc = carry
            begin = first + step * KT
            at = jnp.minimum(begin, total - KT)
            here = pl.multiple_of(at + BLOCK, BLOCK)
            s = dot(keys_tall[pl.ds(here, KT), :], q_wide)
            valid = (far_ids >= jnp.maximum(start, begin) - at) & (far_ids < stop - at)
            s = jnp.where(valid, s * scale, NEG)
            new_top = jnp.maximum(top, jnp.max(s, axis=0, keepdims=True))
            p = jnp.exp2(s - new_top)
            factor = jnp.exp2(top - new_top)
            norm = norm * factor + jnp.sum(p, axis=0, keepdims=True)
            acc = acc * factor + dot(keys_flat[DH:, pl.ds(here, KT)], p.astype(bf16))
            return new_top, norm, acc

        top, norm, acc = lax.fori_loop(0, steps, far, (top, norm, acc))
        result = acc / norm
        lse = top + jnp.log(norm) * LOG2E
        for half, slot in enumerate((slot_a, slot_b)):
            part = result[:, half * BLOCK : (half + 1) * BLOCK]
            full_ref[pl.ds(slot, 1)] = part[None]
            out_ref[pl.ds(slot, 1)] = part.astype(bf16)[None]
            lse_ref[pl.ds(slot, 1), :] = lse[:, half * BLOCK : (half + 1) * BLOCK]
        return 0

    lax.fori_loop(0, count // 2, one_tile, 0)


def backward_kernel(
    bucket_count,
    parts,
    nat_ref,
    order_ref,
    low_ref,
    thr_ref,
    tab_ref,
    seq_ref,
    *rest,
):
    part_refs = rest[:parts]
    dout_ref, full_ref, lse_ref = rest[parts : parts + 3]
    dq_ref = rest[parts + 3]
    dkv_refs = rest[parts + 4 : 2 * parts + 4]
    table_ref = rest[2 * parts + 4]
    keys_flat, keys_tall, near_bias, grads, near_grads = rest[2 * parts + 5 :]
    own_ref = part_refs[0]
    count = own_ref.shape[0]
    total = keys_tall.shape[0] - BLOCK
    scale = DH ** (-0.5) * LOG2E
    bf16 = jnp.bfloat16
    f32 = jnp.float32
    place_pairs(nat_ref, part_refs, DH, count, keys_flat, keys_tall)
    fill_near_bias(thr_ref, tab_ref, near_bias, bucket_count)
    grads[...] = jnp.zeros_like(grads)
    near_grads[...] = jnp.zeros_like(near_grads)
    near_ids = lax.broadcasted_iota(jnp.int32, (2 * BLOCK, BLOCK), 0)
    far_ids = lax.broadcasted_iota(jnp.int32, (KT, 2 * BLOCK), 0)
    low_lane = lax.broadcasted_iota(jnp.int32, (BLOCK, 2 * DH), 1) < DH

    def one_tile(tile, _):
        slot_a, slot_b, blk_a, blk_b = pair_ids(nat_ref, tile, order_ref)
        starts, lses, sums, rights, out_sides, q_sides, dq_near = [], [], [], [], [], [], []
        for slot, blk in ((slot_a, blk_a), (slot_b, blk_b)):
            at = pl.multiple_of(blk * BLOCK, BLOCK)
            start = seq_ref[pl.ds(blk, 1), :]
            q_t = own_ref[slot, :DH, :]
            do_t = dout_ref[slot]
            lse = lse_ref[pl.ds(slot, 1), :]
            dsum = jnp.sum(do_t.astype(f32) * full_ref[slot], axis=0, keepdims=True)
            zero = jnp.zeros_like(q_t)
            right = lane_pair(
                jnp.concatenate([q_t, zero], axis=0), jnp.concatenate([zero, do_t], axis=0)
            )
            both = jnp.concatenate([q_t, do_t], axis=0).T
            none = jnp.zeros_like(both)
            q_side = jnp.where(low_lane, both, none)
            out_side = jnp.where(low_lane, none, both)
            s_dp = dot(keys_tall[pl.ds(at, 2 * BLOCK), :], right)
            s = s_dp[:, :BLOCK] * scale + near_bias[...]
            s = jnp.where(near_ids >= start - (blk - 1) * BLOCK, s, NEG)
            p = jnp.exp2(s - lse)
            ds = (p * (s_dp[:, BLOCK:] - dsum)).astype(bf16)
            grads[pl.ds(at, 2 * BLOCK), :] += dot(
                lane_pair(p.astype(bf16), ds), jnp.concatenate([out_side, q_side], axis=0)
            )
            near_grads[...] += ds.astype(f32)
            dq_near.append(dot(keys_flat[:DH, pl.ds(at, 2 * BLOCK)], ds))
            starts.append(start)
            lses.append(lse)
            sums.append(dsum)
            rights.append(right)
            out_sides.append(out_side)
            q_sides.append(q_side)
        start = lane_pair(*starts)
        lse = lane_pair(*lses)
        dsum = lane_pair(*sums)
        right = jnp.concatenate(
            [
                rights[0][:, :BLOCK],
                rights[1][:, :BLOCK],
                rights[0][:, BLOCK:],
                rights[1][:, BLOCK:],
            ],
            axis=1,
        )
        sides = jnp.concatenate(out_sides + q_sides, axis=0)
        lane = lax.broadcasted_iota(jnp.int32, (1, 2 * BLOCK), 1)
        stop = jnp.where(lane < BLOCK, (blk_a - 1) * BLOCK, (blk_b - 1) * BLOCK)
        first = low_ref[blk_a] * BLOCK
        steps = (jnp.maximum((blk_b - 1) * BLOCK - first, 0) + KT - 1) // KT

        def far(step, dq):
            begin = first + step * KT
            at = jnp.minimum(begin, total - KT)
            here = pl.multiple_of(at + BLOCK, BLOCK)
            s_dp = dot(keys_tall[pl.ds(here, KT), :], right)
            valid = (far_ids >= jnp.maximum(start, begin) - at) & (far_ids < stop - at)
            s = jnp.where(valid, s_dp[:, : 2 * BLOCK] * scale, NEG)
            p = jnp.exp2(s - lse)
            ds = (p * (s_dp[:, 2 * BLOCK :] - dsum)).astype(bf16)
            grads[pl.ds(here, KT), :] += dot(lane_pair(p.astype(bf16), ds), sides)
            return dq + dot(keys_flat[:DH, pl.ds(here, KT)], ds)

        dq = lax.fori_loop(0, steps, far, lane_pair(*dq_near)) * DH ** (-0.5)
        for half, slot in enumerate((slot_a, slot_b)):
            part = dq[:, half * BLOCK : (half + 1) * BLOCK]
            dq_ref[pl.ds(slot, 1)] = part.astype(bf16)[None]
        return 0

    lax.fori_loop(0, count // 2, one_tile, 0)
    key_lane = jnp.where(low_lane, DH ** (-0.5), 1.0)
    for part in range(parts):

        def give(index, _, part=part):
            at = pl.multiple_of((nat_ref[part * count + index] + 1) * BLOCK, BLOCK)
            block = grads[pl.ds(at, BLOCK), :] * key_lane
            dkv_refs[part][pl.ds(index, 1)] = block.T.astype(bf16)[None]
            return 0

        lax.fori_loop(0, count, give, 0)
    key_ids = lax.broadcasted_iota(jnp.int32, (2 * BLOCK, BLOCK), 0)
    query_ids = lax.broadcasted_iota(jnp.int32, (2 * BLOCK, BLOCK), 1)
    distance = query_ids + BLOCK - key_ids
    near = near_grads[...]
    out_lane = lax.broadcasted_iota(jnp.int32, (1, BLOCK), 1)
    above = jnp.sum(near, axis=(0, 1), keepdims=True)
    result = jnp.zeros((1, BLOCK), f32)
    seen = jnp.zeros((1, 1), f32)
    for bucket in range(1, bucket_count):
        kept = jnp.sum(
            jnp.where(distance >= thr_ref[bucket], near, 0.0), axis=(0, 1), keepdims=True
        )
        result = jnp.where(out_lane == bucket - 1, above - kept, result)
        seen = seen + (above - kept)
        above = kept
    table_ref[...] = jnp.where(out_lane == bucket_count - 1, -seen, result)


def attention_call(kernel, parts, bucket_count, scalars, seq_start, arrays, out_shape, total, extra):
    smem = pl.BlockSpec(memory_space=pltpu.SMEM)
    vmem = pl.BlockSpec(memory_space=pltpu.VMEM)
    operands = list(scalars) + [seq_start] + list(arrays)
    scratch = [
        pltpu.VMEM((2 * DH, total + BLOCK), jnp.bfloat16),
        pltpu.VMEM((total + BLOCK, 2 * DH), jnp.bfloat16),
        pltpu.VMEM((2 * BLOCK, BLOCK), jnp.float32),
    ] + extra
    return pl.pallas_call(
        functools.partial(kernel, bucket_count, parts),
        out_shape=out_shape,
        in_specs=[smem] * len(scalars) + [vmem] * (1 + len(arrays)),
        out_specs=[vmem] * len(out_shape),
        scratch_shapes=scratch,
        compiler_params=pltpu.CompilerParams(vmem_limit_bytes=VMEM_LIMIT),
    )(*operands)


def turn_halves(x, axis, amounts, sign):
    halves = x.shape[axis + 1]
    shape = [1] * x.ndim
    shape[axis] = x.shape[axis]
    amounts = amounts.reshape(shape)
    result = x
    for step in range(1, halves):
        result = jnp.where(amounts == step, jnp.roll(x, -sign * step, axis=axis + 1), result)
    return result


def slot_tables(group_routes, experts, capacity):
    count = group_routes.shape[0]
    top_count = group_routes.shape[1]
    flat = group_routes.T.reshape(-1)
    hot = (flat[:, None] == jnp.arange(experts, dtype=jnp.int32)[None, :]).astype(jnp.int32)
    rank_of = jnp.sum((jnp.cumsum(hot, axis=0) - hot) * hot, axis=1)
    kept = rank_of < capacity
    dest = jnp.where(kept, flat * capacity + rank_of, experts * capacity)
    tokens = jnp.tile(jnp.arange(count, dtype=jnp.int32), top_count)
    token_of_slot = (
        jnp.zeros((experts * capacity + 1,), jnp.int32).at[dest].set(tokens)[: experts * capacity]
    )
    live = jnp.zeros((experts * capacity + 1,), jnp.float32).at[dest].set(1.0)[: experts * capacity]
    return (dest, kept.reshape(top_count, count).astype(jnp.float32), token_of_slot, live)


def on_device(
    layer_in,
    gain_one,
    w_query,
    w_key,
    w_value,
    w_out,
    bias_table,
    gain_two,
    w_router,
    w_gate,
    w_up,
    w_down,
    lengths,
    block_perm,
    buckets,
    routes,
    cotangent,
):
    tp_count = lax.axis_size("tp")
    ctx_count = lax.axis_size("ctx")
    tp_index = lax.axis_index("tp")
    ctx_index = lax.axis_index("ctx")
    rows_dev = layer_in.shape[0]
    width = layer_in.shape[1]
    group_rows = rows_dev * tp_count
    width_loc = w_query.shape[1]
    head_count = width_loc // DH
    blocks_group = group_rows // BLOCK
    experts = w_gate.shape[0]
    top_count = routes.shape[1]
    capacity = 5 * top_count * group_rows // (4 * experts)
    slot_count = experts * capacity
    bucket_count = bias_table.shape[0]
    f32 = jnp.float32
    bf16 = jnp.bfloat16
    x_float = layer_in.astype(f32)
    inv_one = lax.rsqrt(jnp.mean(x_float * x_float, axis=1, keepdims=True) + EPS)
    normed_one = x_float * inv_one
    h_one = (normed_one * gain_one).astype(bf16)
    h_one_all = lax.all_gather(h_one, "tp", axis=0, tiled=True)
    w_qkv = jnp.concatenate([w_query, w_key, w_value], axis=1)
    qkv = lax.dot_general(
        w_qkv, h_one_all, (((0,), (1,)), ((), ())), preferred_element_type=f32
    ).astype(bf16)
    team = ctx_count // head_count
    member = ctx_index % team
    my_head = ctx_index // team
    pair_count = blocks_group // team
    slot_blocks = ctx_count * pair_count
    total = ctx_count * group_rows
    pair_ids_m = jnp.arange(pair_count, dtype=jnp.int32)
    turn = (ctx_index + pair_ids_m) % team
    ends = jnp.cumsum(lengths)
    begins = ends - lengths
    places = jnp.arange(total, dtype=jnp.int32)
    seq_start = jnp.max(
        jnp.where(begins[None, :] <= places[:, None], begins[None, :], 0), axis=1
    ).reshape(total // BLOCK, BLOCK)
    low_block = seq_start[:, 0] // BLOCK
    thresholds = jnp.sum(
        (buckets[None, :] < jnp.arange(bucket_count, dtype=jnp.int32)[:, None]).astype(jnp.int32),
        axis=1,
    )
    head_hot = (jnp.arange(head_count, dtype=jnp.int32) == my_head).astype(f32)
    my_table = jnp.sum(bias_table * head_hot[None, :], axis=1)
    near_table = (my_table - my_table[bucket_count - 1]) * LOG2E
    sources = jnp.arange(ctx_count, dtype=jnp.int32)
    members = (member + jnp.arange(team, dtype=jnp.int32)) % team
    half_of = (members[:, None, None] + sources[None, :, None] + pair_ids_m[None, None, :]) % team
    perm_pairs = block_perm.reshape(1, ctx_count, pair_count, team)
    natural = jnp.sum(
        jnp.where(
            half_of[..., None] == jnp.arange(team, dtype=jnp.int32)[None, None, None, :],
            perm_pairs,
            0,
        ),
        axis=3,
    ).reshape(-1)
    own_natural = natural[:slot_blocks]
    rank = jnp.sum((own_natural[None, :] < own_natural[:, None]).astype(jnp.int32), axis=1)
    slots = jnp.arange(slot_blocks, dtype=jnp.int32)
    order = jnp.sum(jnp.where(rank[None, :] == slots[:, None], slots[None, :], 0), axis=1)
    scalars = (natural, order, low_block, thresholds, near_table)

    def to_heads(x, kinds):
        split = x.reshape(kinds, head_count, DH, pair_count, team, BLOCK)
        split = turn_halves(split, 3, turn, 1)
        send = split.transpose(1, 4, 3, 0, 2, 5).reshape(
            ctx_count, pair_count, kinds * DH, BLOCK
        )
        got = lax.all_to_all(send, "ctx", 0, 0, tiled=True)
        return got.reshape(slot_blocks, kinds * DH, BLOCK)

    def from_heads(x, kinds):
        send = x.reshape(ctx_count, pair_count, kinds * DH, BLOCK)
        got = lax.all_to_all(send, "ctx", 0, 0, tiled=True)
        split = got.reshape(head_count, team, pair_count, kinds, DH, BLOCK)
        split = split.transpose(3, 0, 4, 2, 1, 5)
        split = turn_halves(split, 3, turn, -1)
        return split.reshape(kinds * head_count * DH, group_rows)

    def team_shift(x, step):
        route = []
        for device in range(ctx_count):
            base = device // team * team
            route.append((device, base + (device % team + step) % team))
        return lax.ppermute(x, "ctx", route)

    own_qkv = to_heads(qkv, 3)
    own_pairs = own_qkv[:, DH:, :]
    parts = [own_qkv] + [team_shift(own_pairs, -step) for step in range(1, team)]
    head_block = (slot_blocks, DH, BLOCK)
    att_slots, att_full, log_total = attention_call(
        forward_kernel,
        team,
        bucket_count,
        scalars,
        seq_start,
        parts,
        [
            jax.ShapeDtypeStruct(head_block, bf16),
            jax.ShapeDtypeStruct(head_block, f32),
            jax.ShapeDtypeStruct((slot_blocks, BLOCK), f32),
        ],
        total,
        [],
    )
    attended_bf = from_heads(att_slots, 1)
    attn_rows = lax.psum_scatter(
        lax.dot_general(
            attended_bf, w_out, (((0,), (0,)), ((), ())), preferred_element_type=f32
        ).astype(jnp.bfloat16),
        "tp",
        scatter_dimension=0,
        tiled=True,
    ).astype(jnp.float32)
    mixed_in = x_float + attn_rows
    inv_two = lax.rsqrt(jnp.mean(mixed_in * mixed_in, axis=1, keepdims=True) + EPS)
    normed_two = mixed_in * inv_two
    h_two = (normed_two * gain_two).astype(bf16)
    h_two_all = lax.all_gather(h_two, "tp", axis=0, tiled=True)
    logits = jnp.dot(h_two_all, w_router, preferred_element_type=f32)
    expo = jnp.exp(logits - jnp.max(logits, axis=1, keepdims=True))
    gates = expo / jnp.sum(expo, axis=1, keepdims=True)
    dest, kept, token_of_slot, live = slot_tables(routes, experts, capacity)
    expert_ids = jnp.arange(experts, dtype=jnp.int32)
    chosen = (routes.T[:, :, None] == expert_ids[None, None, :]).astype(f32)
    picked = jnp.sum(gates[None] * chosen, axis=2) * kept
    weight_slot = jnp.zeros((slot_count + 1,), f32).at[dest].set(picked.reshape(-1))[:slot_count]
    expert_in = jnp.where(
        live[:, None] > 0, jnp.take(h_two_all, token_of_slot, axis=0), jnp.zeros((), bf16)
    ).reshape(experts, capacity, width)
    gate_pre = jnp.einsum("ecd,edf->ecf", expert_in, w_gate, preferred_element_type=f32)
    up_pre = jnp.einsum("ecd,edf->ecf", expert_in, w_up, preferred_element_type=f32)
    hidden = (jax.nn.gelu(gate_pre, approximate=True) * up_pre).astype(bf16)
    expert_out = jnp.einsum("ecf,efd->ecd", hidden, w_down, preferred_element_type=f32).reshape(
        slot_count, width
    )
    rows_back = jnp.take(expert_out, jnp.minimum(dest, slot_count - 1), axis=0).reshape(
        top_count, group_rows, width
    )
    mixed_part = jnp.sum(picked[:, :, None] * rows_back, axis=0)
    mixed_rows = lax.psum_scatter(
        mixed_part.astype(jnp.bfloat16), "tp", scatter_dimension=0, tiled=True
    ).astype(jnp.float32)
    layer_out = mixed_in + mixed_rows
    grad_float = cotangent.astype(f32)
    grad_all = lax.all_gather(cotangent, "tp", axis=0, tiled=True)
    gate_dots = jnp.sum(rows_back * grad_all.astype(f32)[None], axis=2)
    d_expert_out = (
        (jnp.take(grad_all, token_of_slot, axis=0).astype(f32) * weight_slot[:, None])
        .astype(bf16)
        .reshape(experts, capacity, width)
    )
    d_hidden = jnp.einsum("ecd,efd->ecf", d_expert_out, w_down, preferred_element_type=f32)
    grad_down = jnp.einsum("ecf,ecd->efd", hidden, d_expert_out, preferred_element_type=f32)
    _, glu_pull = jax.vjp(
        lambda gate_val, up_val: jax.nn.gelu(gate_val, approximate=True) * up_val, gate_pre, up_pre
    )
    d_gate_pre, d_up_pre = glu_pull(d_hidden)
    d_gate_bf = d_gate_pre.astype(bf16)
    d_up_bf = d_up_pre.astype(bf16)
    grad_gate = jnp.einsum("ecd,ecf->edf", expert_in, d_gate_bf, preferred_element_type=f32)
    grad_up = jnp.einsum("ecd,ecf->edf", expert_in, d_up_bf, preferred_element_type=f32)
    d_expert_in = (
        jnp.einsum("ecf,edf->ecd", d_gate_bf, w_gate, preferred_element_type=f32)
        + jnp.einsum("ecf,edf->ecd", d_up_bf, w_up, preferred_element_type=f32)
    ).reshape(slot_count, width)
    d_h_two_part = (
        jnp.zeros((group_rows, width), f32).at[token_of_slot].add(d_expert_in * live[:, None])
    )
    d_h_two, dots_own = (
        lax.psum_scatter(
            d_h_two_part.astype(jnp.bfloat16), "tp", scatter_dimension=0, tiled=True
        ).astype(jnp.float32),
        lax.psum_scatter(
            gate_dots.T.astype(jnp.bfloat16), "tp", scatter_dimension=0, tiled=True
        ).astype(jnp.float32),
    )
    own_start = tp_index * rows_dev
    gates_own = lax.dynamic_slice_in_dim(gates, own_start, rows_dev, 0)
    routes_own = lax.dynamic_slice_in_dim(routes, own_start, rows_dev, 0)
    kept_own = lax.dynamic_slice_in_dim(kept, own_start, rows_dev, 1)
    hot_own = (routes_own[:, :, None] == expert_ids[None, None, :]).astype(f32)
    d_gates = jnp.sum((dots_own * kept_own.T)[:, :, None] * hot_own, axis=1)
    d_logits = gates_own * (d_gates - jnp.sum(gates_own * d_gates, axis=1, keepdims=True))
    d_h_two = d_h_two + jnp.dot(
        d_logits, w_router.astype(f32).T, precision=HIGH, preferred_element_type=f32
    )
    grad_router_part = jnp.dot(h_two.T, d_logits, precision=HIGH, preferred_element_type=f32)
    d_norm_two = d_h_two * gain_two
    grad_gain_two_part = jnp.sum(d_h_two * normed_two, axis=0)
    d_mixed = grad_float + inv_two * (
        d_norm_two - normed_two * jnp.mean(d_norm_two * normed_two, axis=1, keepdims=True)
    )
    d_attn = d_mixed.astype(bf16)
    piece = lax.all_gather(d_attn, "tp", axis=0, tiled=True)
    d_attended = jnp.einsum("hd,rd->hr", w_out, piece, preferred_element_type=f32).astype(bf16)
    grad_out = jnp.einsum("hr,rd->hd", attended_bf, piece, preferred_element_type=f32)
    d_att_slots = to_heads(d_attended, 1)
    pair_block = jax.ShapeDtypeStruct((slot_blocks, 2 * DH, BLOCK), bf16)
    back = attention_call(
        backward_kernel,
        team,
        bucket_count,
        scalars,
        seq_start,
        parts + [d_att_slots, att_full, log_total],
        [jax.ShapeDtypeStruct(head_block, bf16)]
        + [pair_block] * team
        + [jax.ShapeDtypeStruct((1, BLOCK), f32)],
        total,
        [
            pltpu.VMEM((total + BLOCK, 2 * DH), f32),
            pltpu.VMEM((2 * BLOCK, BLOCK), f32),
        ],
    )
    pair_grads = back[1].astype(f32)
    for step in range(1, team):
        pair_grads = pair_grads + team_shift(back[1 + step], step).astype(f32)
    d_cat = from_heads(jnp.concatenate([back[0], pair_grads.astype(bf16)], axis=1), 3)
    grad_qkv = jnp.einsum("rd,hr->dh", h_one_all, d_cat, preferred_element_type=f32)
    grad_table_part = back[1 + team][0, :bucket_count, None] * head_hot[None, :]
    d_h_one_part = jnp.einsum("hr,dh->rd", d_cat, w_qkv, preferred_element_type=f32)
    d_h_one = lax.psum_scatter(
        d_h_one_part.astype(jnp.bfloat16), "tp", scatter_dimension=0, tiled=True
    ).astype(jnp.float32)
    d_norm_one = d_h_one * gain_one
    grad_gain_one_part = jnp.sum(d_h_one * normed_one, axis=0)
    grad_x = d_mixed + inv_one * (
        d_norm_one - normed_one * jnp.mean(d_norm_one * normed_one, axis=1, keepdims=True)
    )
    gain_one_share, gain_two_share, router_share = (
        lax.psum_scatter(grad_gain_one_part, "tp", scatter_dimension=0, tiled=True),
        lax.psum_scatter(grad_gain_two_part, "tp", scatter_dimension=0, tiled=True),
        lax.psum_scatter(grad_router_part, "tp", scatter_dimension=0, tiled=True),
    )
    rest_total = (
        lax.psum(grad_qkv[:, :width_loc].astype(jnp.bfloat16), "ctx").astype(jnp.float32),
        lax.psum(grad_qkv[:, width_loc : 2 * width_loc].astype(jnp.bfloat16), "ctx").astype(
            jnp.float32
        ),
        lax.psum(grad_qkv[:, 2 * width_loc :].astype(jnp.bfloat16), "ctx").astype(jnp.float32),
        lax.psum(grad_out.astype(jnp.bfloat16), "ctx").astype(jnp.float32),
        lax.psum(grad_table_part.astype(jnp.bfloat16), "ctx").astype(jnp.float32),
        lax.psum(gain_one_share.astype(jnp.bfloat16), "ctx").astype(jnp.float32),
        lax.psum(gain_two_share.astype(jnp.bfloat16), "ctx").astype(jnp.float32),
        lax.psum(router_share.astype(jnp.bfloat16), "ctx").astype(jnp.float32),
    )
    return (
        layer_out,
        grad_x,
        rest_total[5],
        rest_total[0],
        rest_total[1],
        rest_total[2],
        rest_total[3],
        rest_total[4],
        rest_total[6],
        rest_total[7],
        lax.psum(grad_gate.astype(jnp.bfloat16), "ctx").astype(jnp.float32),
        lax.psum(grad_up.astype(jnp.bfloat16), "ctx").astype(jnp.float32),
        lax.psum(grad_down.astype(jnp.bfloat16), "ctx").astype(jnp.float32),
    )


def solution(mesh):
    placed = (
        P(("ctx", "tp"), None),
        P(),
        P(None, "tp"),
        P(None, "tp"),
        P(None, "tp"),
        P("tp", None),
        P(None, "tp"),
        P(),
        P(),
        P(None, None, "tp"),
        P(None, None, "tp"),
        P(None, "tp", None),
        P(),
        P(),
        P(),
        P("ctx", None),
        P(("ctx", "tp"), None),
    )
    return jax.shard_map(
        on_device,
        mesh=mesh,
        in_specs=placed,
        out_specs=(
            P(("ctx", "tp"), None),
            P(("ctx", "tp"), None),
            P("tp"),
            P(None, "tp"),
            P(None, "tp"),
            P(None, "tp"),
            P("tp", None),
            P(None, "tp"),
            P("tp"),
            P("tp", None),
            P(None, None, "tp"),
            P(None, None, "tp"),
            P(None, "tp", None),
        ),
        check_vma=False,
    )
```

time: 4870 us -> 1090 us (0.22)
  local copies, waits for them, and re-layouts: 2450 us -> 87.8 us
  matrix products: 991 us -> 120 us
  other arithmetic: 553 us -> 119 us
  waiting for transfers between devices: 743 us -> 546 us
  Pallas kernels: 0 us -> 128 us
  loops' own time: 49.6 us -> 0 us
    mul x448 -> x1, local copies, waits for them, and re-layouts: 1220 us -> 0.01 us  [on_device(): grad_table_part = back[1 + team][0, :bucket_count, None] * head_hot[None, :]]
    dot_general x332 -> x6, matrix products: 887 us -> 16.9 us  [the longest x1 4.57 us: on_device(): lax.dot_general(w_qkv, h_one_all, (((0,), (1,)), ((), ())), preferred_ele...]
    add x128 -> x0, local copies, waits for them, and re-layouts: 517 us -> none  [add_bias(): split + w_far[None, :, None, :, None] * far_bias[:, None, None, None, None]]
    dynamic_update_slice x160 -> x0, local copies, waits for them, and re-layouts: 389 us -> none  [the longest x32 173 us: update(): lax.dynamic_update_slice_in_dim(grads_in, old_kv + jnp.stack([dk_add, dv_...]
    ppermute x22 -> x2, waiting for transfers between devices: 260 us -> 2.87 us  [team_shift(): return lax.ppermute(x, 'ctx', route)]
    add x223 -> x1, other arithmetic: 215 us -> 0.07 us  [on_device(): members[:, None, None] + sources[None, :, None] + pair_ids_m[None, None, :]]
    pallas_call x0 -> x2, Pallas kernels: none -> 128 us  [attention_call(): pl.pallas_call(functools.partial(kernel, bucket_count, parts), out_shape=...]
    reduce_sum x79 -> x5, other arithmetic: 118 us -> 1.56 us  [the longest x1 0.65 us: on_device(): jnp.sum((buckets[None, :] < jnp.arange(bucket_count, dtype=jnp.int32)[:,...]
  transfers between devices with their start and end apart: 33 -> 15, of which waited for: 30 -> 12; matrix products, arithmetic and copies ran while one was open for 4% -> 14% of each run, Pallas kernels for 0% -> 0%
where the time goes in v1:
time: 1090 us; the launch traced here: 1070 us
  waiting for transfers between devices  546 us (50%)
  Pallas kernels  128 us (12%)
  matrix products  120 us (11%)
  other arithmetic  119 us (11%)
  local copies, waits for them, and re-layouts  87.8 us (8%)
  blocking collectives  49.6 us (5%)
  between operations  15.6 us (1%)
    psum x1, waiting for transfers between devices, on_device(): lax.psum(grad_qkv[:, :width_loc].astype(jnp.bfloat16), 'ctx')  252 us
    pallas_call x2, Pallas kernels, attention_call(): pl.pallas_call(functools.partial(kernel, bucket_count, parts), out_shape=...  128 us
    all_gather x1, waiting for transfers between devices, on_device(): h_one_all = lax.all_gather(h_one, 'tp', axis=0, tiled=True)  46.5 us
    all_gather x1, waiting for transfers between devices, on_device(): piece = lax.all_gather(d_attn, 'tp', axis=0, tiled=True)  45.4 us
    reduce_scatter x1, waiting for transfers between devices, on_device(): lax.psum_scatter(d_h_two_part.astype(jnp.bfloat16), 'tp', scatter_dimensi...  41.7 us
    reduce_scatter x1, waiting for transfers between devices, on_device(): lax.psum_scatter(lax.dot_general(attended_bf, w_out, (((0,), (0,)), ((),...  40.1 us
    all_gather x1, waiting for transfers between devices, on_device(): h_two_all = lax.all_gather(h_two, 'tp', axis=0, tiled=True)  33.7 us
    scatter-add x1, other arithmetic, on_device(): jnp.zeros((group_rows, width), f32).at[token_of_slot]  25.5 us
  transfers between devices with their start and end apart: 15, of which 12 were waited for; matrix products, arithmetic and copies ran while one was open for 14% of the time, Pallas kernels for 0%

profile of v1, /device:TPU:0, one launch (start us, length us, event | category | flops | bytes accessed | tf_op | source)
XLA Modules:
  0.0 1074.4 jit_solution(2264443876749472033)
XLA Ops:
  13.4 46.5 %all-gather.5.cloned.1.call-done = bf16[1024,1024]{1,0:T(8,128)(2,1)} async-done(((bf16[256,1024]{1,0:T(8,128)(2,1)}), bf16[1024,1024]{1,0:T(8,128)(2,1)}) %all-gather.5.cloned.1.call-update) | async-done | bytes 2097168 | tf_op jit(solution)/shard_map/all_gather | solution.py:361
  79.5 20.5 %all-to-all-done = bf16[8,4,192,128]{3,2,1,0:T(8,128)(2,1)S(1)} async-done(((bf16[8,4,192,128]{3,2,1,0:T(8,128)(2,1)}), bf16[8,4,192,128]{3,2,1,0:T(8,128)(2,1)S(1)}, u32[]{:S(2)}, u32[]{:S(2)}) %all-to-all-start) | async-done | bytes 1572896 | tf_op jit(solution)/shard_map/all_to_all | solution.py:412
  107.6 59.7 %shard_map.264 = (bf16[32,64,128]{2,1,0:T(8,128)(2,1)}, f32[32,64,128]{2,1,0:T(8,128)}, f32[32,128]{1,0:T(8,128)}) custom-call(s32[64]{0:T(128)} %reshape.375.nat_ref, s32[32]{0:T(128)} %select_reduce_fusion.2.order_ref, s32[64]{0:T(128)} %and_select_fusion.low_ref, s32[32]{0:T(128)} %convert_reduce_fusion.thr_ref, f32[32]{0:T(128)} %subtract_multiply_fusion.1.tab_ref, ...), custom_call_target="tpu_custom_call" | custom-call | tf_op jit(solution)/shard_map/pallas_call | solution.py:284
  167.3 13.1 %all_to_all.20 = bf16[8,4,64,128]{3,2,1,0:T(8,128)(2,1)S(1)} all-to-all(bf16[8,4,64,128]{3,2,1,0:T(8,128)(2,1)} %bitcast.158), channel_id=1, replica_groups=mesh['ctx'=8,'tp'=4] {'ctx'}, dimensions={0} | all-to-all | bytes 1048576 | tf_op jit(solution)/shard_map/all_to_all | solution.py:417
  184.5 40.1 %reduce-scatter.11.cloned.1.call-done = bf16[256,1024]{1,0:T(8,128)(2,1)} async-done(((bf16[1024,1024]{1,0:T(8,128)(2,1)}), bf16[256,1024]{1,0:T(8,128)(2,1)}) %reduce-scatter.11.cloned.1.call-update) | async-done | bytes 524304 | tf_op jit(solution)/shard_map/reduce_scatter | solution.py:450
  246.8 24.7 %all-gather.9.cloned.1.call-done = bf16[1024,1024]{1,0:T(8,128)(2,1)} async-done(((bf16[256,1024]{1,0:T(8,128)(2,1)}), bf16[1024,1024]{1,0:T(8,128)(2,1)}) %all-gather.9.cloned.1.call-update) | async-done | bytes 2097168 | tf_op jit(solution)/shard_map/all_gather | solution.py:489
  284.5 33.7 %all-gather.7.cloned.1.call-done = bf16[1024,1024]{1,0:T(8,128)(2,1)} async-done(((bf16[256,1024]{1,0:T(8,128)(2,1)}), bf16[1024,1024]{1,0:T(8,128)(2,1)}) %all-gather.7.cloned.1.call-update) | async-done | bytes 2097168 | tf_op jit(solution)/shard_map/all_gather | solution.py:462
  342.2 10.8 %fusion.51 = f32[4,640,704]{1,2,0:T(8,128)} fusion(bf16[4,640,1024]{2,1,0:T(8,128)(2,1)S(1)} %bitcast.145, bf16[4,1024,704]{1,2,0:T(8,128)(2,1)} %param.29), kind=kOutput, calls=%fused_computation.165 | convolution fusion | flops 3690987520 | bytes 18219008 | tf_op jit(solution)/shard_map/ecd,edf->ecf/dot_general | solution.py:475
  363.4 17.6 %multiply_convert_fusion.1 = (bf16[4,640,704]{1,2,0:T(8,128)(2,1)}, bf16[4,640,704]{1,2,0:T(8,128)(2,1)}, bf16[4,640,704]{1,2,0:T(8,128)(2,1)}) fusion(f32[4,640,704]{1,2,0:T(8,128)} %fusion.50, f32[4,640,704]{1,2,0:T(8,128)} %fusion.51, bf16[4,640,1024]{2,1,0:T(8,128)(2,1)} %bitcast.143, bf16[4,704,1024]{2,1,0:T(8,128)(2,1)} %param.30), kind=kOutput, calls=%fused_computation.21 | convolution fusion | flops 3737845760 | bytes 36241408 | tf_op jit(solution)/shard_map/ecd,efd->ecf/dot_general | solution.py:496
  381.0 12.3 %fusion.53 = f32[4,640,1024]{2,1,0:T(8,128)} fusion(bf16[4,640,704]{1,2,0:T(8,128)(2,1)} %get-tuple-element.48, bf16[4,1024,704]{1,2,0:T(8,128)(2,1)} %param.28), kind=kOutput, calls=%fused_computation.167 | convolution fusion | flops 3690987520 | bytes 19857408 | tf_op jit(solution)/shard_map/ecf,edf->ecd/dot_general | solution.py:507
  393.3 11.1 %fusion.52 = f32[4,640,1024]{2,1,0:T(8,128)} fusion(bf16[4,640,704]{1,2,0:T(8,128)(2,1)S(1)} %copy-done.40, bf16[4,704,1024]{2,1,0:T(8,128)(2,1)} %param.30), kind=kOutput, calls=%fused_computation.166 | convolution fusion | flops 3690987520 | bytes 19857408 | tf_op jit(solution)/shard_map/ecf,efd->ecd/dot_general | solution.py:477
  404.4 15.6 %gather_fusion = f32[2048,1024]{1,0:T(8,128)} fusion(f32[2560,1024]{1,0:T(8,128)} %bitcast.127, s32[2048]{0:T(1024)S(1)} %broadcast_clamp_fusion), kind=kCustom, calls=%fused_computation.2 | custom fusion | bytes 16785408 | tf_op jit(solution)/shard_map/jit(_take)/gather | solution.py:480
  427.0 11.3 %convolution_add_fusion = f32[4,640,1024]{2,1,0:T(8,128)S(1)} fusion(f32[4,640,1024]{2,1,0:T(8,128)} %fusion.53, bf16[4,640,704]{1,2,0:T(8,128)(2,1)} %get-tuple-element.47, bf16[4,1024,704]{1,2,0:T(8,128)(2,1)} %param.29), kind=kOutput, calls=%fused_computation.30 | convolution fusion | flops 3693608960 | bytes 30343168 | tf_op jit(solution)/shard_map/ecf,edf->ecd/dot_general | solution.py:508
  443.1 25.5 %scatter_custom_fusion.3 = f32[1024,1024]{1,0:T(8,128)} fusion(s32[2560]{0:T(1024)S(1)} %compare_select_fusion.2, f32[2560,1024]{1,0:T(8,128)} %bitcast_multiply_fusion, f32[]{:T(128)} %constant.135.clone.1), kind=kCustom, calls=%fused_computation.32 | custom fusion | flops 2621440 | bytes 4194816 | tf_op jit(solution)/shard_map/scatter-add | solution.py:511
  473.7 41.7 %reduce-scatter.15.cloned.1.call-done = bf16[256,1024]{1,0:T(8,128)(2,1)} async-done(((bf16[1024,1024]{1,0:T(8,128)(2,1)}), bf16[256,1024]{1,0:T(8,128)(2,1)}) %reduce-scatter.15.cloned.1.call-update) | async-done | bytes 524304 | tf_op jit(solution)/shard_map/reduce_scatter | solution.py:514
  518.7 45.4 %all-gather.11.cloned.1.call-done = bf16[1024,1024]{1,0:T(8,128)(2,1)} async-done(((bf16[256,1024]{1,0:T(8,128)(2,1)}), bf16[1024,1024]{1,0:T(8,128)(2,1)}) %all-gather.11.cloned.1.call-update) | async-done | bytes 2097168 | tf_op jit(solution)/shard_map/all_gather | solution.py:538
  569.7 13.5 %all_to_all.21 = bf16[8,4,64,128]{3,2,1,0:T(8,128)(2,1)} all-to-all(bf16[8,4,64,128]{3,2,1,0:T(8,128)(2,1)S(1)} %bitcast.153), channel_id=1, replica_groups=mesh['ctx'=8,'tp'=4] {'ctx'}, dimensions={0} | all-to-all | bytes 1048576 | tf_op jit(solution)/shard_map/all_to_all | solution.py:412
  583.2 68.5 %shard_map.265 = (bf16[32,64,128]{2,1,0:T(8,128)(2,1)}, bf16[32,128,128]{2,1,0:T(8,128)(2,1)}, bf16[32,128,128]{2,1,0:T(8,128)(2,1)}, f32[1,128]{1,0:T(1,128)}) custom-call(s32[64]{0:T(128)} %reshape.375.nat_ref, s32[32]{0:T(128)} %select_reduce_fusion.2.order_ref, s32[64]{0:T(128)} %and_select_fusion.low_ref, s32[32]{0:T(128)} %convert_reduce_fusion.thr_ref, ...), custom_call_target="tpu_custom_call" | custom-call | tf_op jit(solution)/shard_map/pallas_call | solution.py:284
  664.7 18.3 %all-to-all-done.3 = bf16[8,4,192,128]{3,2,1,0:T(8,128)(2,1)S(1)} async-done(((bf16[8,4,192,128]{3,2,1,0:T(8,128)(2,1)}), bf16[8,4,192,128]{3,2,1,0:T(8,128)(2,1)S(1)}, u32[]{:S(2)}, u32[]{:S(2)}) %all-to-all-start.3) | async-done | bytes 1572896 | tf_op jit(solution)/shard_map/all_to_all | solution.py:417
  706.2 10.9 %convolution_convert_fusion.2 = bf16[4,704,1024]{2,1,0:T(8,128)(2,1)} fusion(bf16[4,640,704]{1,2,0:T(8,128)(2,1)} %get-tuple-element.49, bf16[4,640,1024]{2,1,0:T(8,128)(2,1)} %bitcast.144), kind=kOutput, calls=%fused_computation.27 | convolution fusion | flops 3693871104 | bytes 14614528 | tf_op jit(solution)/shard_map/ecf,ecd->efd/dot_general | solution.py:497
  742.0 10.2 all-reduce.2
  752.3 12.8 %all-reduce.3 = (bf16[256]{0:T(256)(128)(2,1)S(1)}, bf16[32,4]{0,1:T(4,128)(2,1)S(1)}, bf16[256]{0:T(256)(128)(2,1)S(1)}, bf16[256,4]{0,1:T(4,128)(2,1)S(1)}) all-reduce(bf16[256]{0:T(256)(128)(2,1)S(1)} %dynamic-slice.7, bf16[32,4]{0,1:T(4,128)(2,1)S(1)} %multiply_convert_fusion.4, ...), channel_id=1, replica_groups=mesh['ctx'=8,'tp'=4] {'ctx'}, use_global_device_ids=true, to_apply=%region_32.34 | all-reduce | flops 1664 | bytes 6656 | tf_op jit(solution)/shard_map/psum | solution.py:587
  767.4 18.4 %reduce-scatter.13.cloned.1.call-done = bf16[256,1024]{1,0:T(8,128)(2,1)} async-done(((bf16[1024,1024]{1,0:T(8,128)(2,1)}), bf16[256,1024]{1,0:T(8,128)(2,1)}) %reduce-scatter.13.cloned.1.call-update) | async-done | bytes 524304 | tf_op jit(solution)/shard_map/reduce_scatter | solution.py:484
  789.1 252.5 %all-reduce.7.cloned.1.call-done = (bf16[1024,256]{1,0:T(8,128)(2,1)}, bf16[1024,256]{1,0:T(8,128)(2,1)}, bf16[1024,256]{1,0:T(8,128)(2,1)}, bf16[256,1024]{1,0:...) async-done(((bf16[1024,256]{1,0:T(8,128)(2,1)}, bf16[1024,256]{1,0:T(8,128)(2,1)}, ...) | async-done | bytes 19398672 | tf_op jit(solution)/shard_map/psum | solution.py:580
  (274 shorter events, 223.9 us)
Async XLA Ops:
  7.2 174.4 %copy-start = (bf16[256,1024]{1,0:T(8,128)(2,1)S(1)}, bf16[256,1024]{1,0:T(8,128)(2,1)}, u32[]{:S(2)}) copy-start(bf16[256,1024]{1,0:T(8,128)(2,1)} %param.24) | copy-start | bytes 1572868
  7.2 52.8 %all-gather.5.cloned.1.call-start = ((), (), s32[]{:S(2)}) async-start(), calls=%async_computation.10 | async-start | bytes 2621440 | tf_op jit(solution)/shard_map/all_gather | solution.py:361
  13.4 46.6 %copy-start.19 = (bf16[1024,768]{1,0:T(8,128)(2,1)}, bf16[1024,768]{1,0:T(8,128)(2,1)S(1)}, u32[]{:S(2)}) copy-start(bf16[1024,768]{1,0:T(8,128)(2,1)S(1)} %constant_dynamic-update-slice_fusion) | copy-start | bytes 4718596
  75.4 24.7 %all-to-all-start = ((bf16[8,4,192,128]{3,2,1,0:T(8,128)(2,1)}), bf16[8,4,192,128]{3,2,1,0:T(8,128)(2,1)S(1)}, u32[]{:S(2)}, u32[]{:S(2)}) async-start(bf16[8,4,192,128]{3,2,1,0:T(8,128)(2,1)} %bitcast.137), calls=%async_computation | async-start | bytes 3145728 | tf_op jit(solution)/shard_map/all_to_all | solution.py:412
  79.0 145.6 %reduce-scatter.11.cloned.1.call-start = ((), (), s32[]{:S(2)}) async-start(), calls=%async_computation.11 | async-start | bytes 2621440 | tf_op jit(solution)/shard_map/reduce_scatter | solution.py:450
  101.2 5.3 collective-permute-start
  181.2 44.7 %copy-start.23 = (f32[1024]{0:T(1024)S(1)}, f32[1024]{0:T(1024)}, u32[]{:S(2)}) copy-start(f32[1024]{0:T(1024)} %param.26) | copy-start | bytes 12292
  181.6 46.4 %copy-start.14 = (bf16[256,1024]{1,0:T(8,128)(2,1)}, bf16[256,1024]{1,0:T(8,128)(2,1)S(1)}, u32[]{:S(2)}) copy-start(bf16[256,1024]{1,0:T(8,128)(2,1)S(1)} %reshape.384) | copy-start | bytes 1572868
  183.7 87.8 %all-gather.9.cloned.1.call-start = ((), (), s32[]{:S(2)}) async-start(), calls=%async_computation.14 | async-start | bytes 2621440 | tf_op jit(solution)/shard_map/all_gather | solution.py:489
  184.4 133.9 %all-gather.7.cloned.1.call-start = ((), (), s32[]{:S(2)}) async-start(), calls=%async_computation.12 | async-start | bytes 2621440 | tf_op jit(solution)/shard_map/all_gather | solution.py:462
  228.0 244.7 %reduce-scatter.19.cloned.1.call-start = ((), (), s32[]{:S(2)}) async-start(), calls=%async_computation.18 | async-start | bytes 327680
  426.7 88.7 %reduce-scatter.15.cloned.1.call-start = ((), (), s32[]{:S(2)}) async-start(), calls=%async_computation.15 | async-start | bytes 2621440 | tf_op jit(solution)/shard_map/reduce_scatter | solution.py:514
  468.7 46.7 %copy-start.5 = (bf16[256,1024]{1,0:T(8,128)(2,1)S(1)}, bf16[256,1024]{1,0:T(8,128)(2,1)}, u32[]{:S(2)}) copy-start(bf16[256,1024]{1,0:T(8,128)(2,1)} %reduce-scatter.11.cloned.1.call-done) | copy-start | bytes 1572868
  468.7 48.8 %copy-start.9 = (bf16[256,1024]{1,0:T(8,128)(2,1)S(1)}, bf16[256,1024]{1,0:T(8,128)(2,1)}, u32[]{:S(2)}) copy-start(bf16[256,1024]{1,0:T(8,128)(2,1)} %param.35) | copy-start | bytes 1572868
  472.6 91.5 %all-gather.11.cloned.1.call-start = ((), (), s32[]{:S(2)}) async-start(), calls=%async_computation.16 | async-start | bytes 2621440 | tf_op jit(solution)/shard_map/all_gather | solution.py:538
  517.5 49.0 %copy-start.11 = (f32[256,1024]{1,0:T(8,128)}, f32[256,1024]{1,0:T(8,128)S(1)}, u32[]{:S(2)}) copy-start(f32[256,1024]{1,0:T(8,128)S(1)} %get-tuple-element.67) | copy-start | bytes 3145732
  651.7 2.9 collective-permute-start.1
  658.5 24.5 %all-to-all-start.3 = ((bf16[8,4,192,128]{3,2,1,0:T(8,128)(2,1)}), bf16[8,4,192,128]{3,2,1,0:T(8,128)(2,1)S(1)}, u32[]{:S(2)}, u32[]{:S(2)}) async-start(bf16[8,4,192,128]{3,2,1,0:T(8,128)(2,1)} %bitcast.138), calls=%async_computation.6 | async-start | bytes 3145728 | tf_op jit(solution)/shard_map/all_to_all | solution.py:417
  662.1 77.3 %reduce-scatter.21.cloned.1.call-start = ((), (), s32[]{:S(2)}) async-start(), calls=%async_computation.19 | async-start | bytes 655360
  664.7 75.8 %reduce-scatter.17.cloned.1.call-start = ((), (), s32[]{:S(2)}) async-start(), calls=%async_computation.17 | async-start | bytes 2621440 | tf_op jit(solution)/shard_map/reduce_scatter | solution.py:566
  699.5 86.3 %reduce-scatter.13.cloned.1.call-start = ((), (), s32[]{:S(2)}) async-start(), calls=%async_computation.13 | async-start | bytes 2621440 | tf_op jit(solution)/shard_map/reduce_scatter | solution.py:484
  705.8 335.7 %all-reduce.7.cloned.1.call-start = ((), (), s32[]{:S(2)}) async-start(), calls=%async_computation.20 | async-start | bytes 38797312 | tf_op jit(solution)/shard_map/psum | solution.py:580
  737.4 48.4 %copy-start.10 = (bf16[256,1024]{1,0:T(8,128)(2,1)S(1)}, bf16[256,1024]{1,0:T(8,128)(2,1)}, u32[]{:S(2)}) copy-start(bf16[256,1024]{1,0:T(8,128)(2,1)} %param.35) | copy-start | bytes 1572868
  737.5 48.3 %copy-start.12 = (f32[256,1024]{1,0:T(8,128)S(1)}, f32[256,1024]{1,0:T(8,128)}, u32[]{:S(2)}) copy-start(f32[256,1024]{1,0:T(8,128)} %copy-done.11) | copy-start | bytes 3145732
  (42 other events, 434.9 us)
Sparse Core Ops, SparseCore 0:
  11.3 48.6 all-gather.4
  183.8 40.7 reduce-scatter.10
  226.3 45.1 all-gather.8
  273.6 44.6 all-gather.6
  426.9 18.3 reduce-scatter.18
  472.8 42.6 reduce-scatter.14
  518.8 45.2 all-gather.10
  665.9 20.8 reduce-scatter.20
  699.6 40.8 reduce-scatter.16
  742.6 43.1 reduce-scatter.12
  792.9 248.6 all-reduce.6

commit v2 on v1

--- a/solution.py
+++ b/solution.py
@@ -274,6 +274,7 @@
 
 def attention_call(kernel, parts, bucket_count, scalars, seq_start, arrays, out_shape, total, extra):
     smem = pl.BlockSpec(memory_space=pltpu.SMEM)
+    team_size = parts
     vmem = pl.BlockSpec(memory_space=pltpu.VMEM)
     operands = list(scalars) + [seq_start] + list(arrays)
     scratch = [
@@ -288,6 +289,11 @@
         out_specs=[vmem] * len(out_shape),
         scratch_shapes=scratch,
         compiler_params=pltpu.CompilerParams(vmem_limit_bytes=VMEM_LIMIT),
+        cost_estimate=pl.CostEstimate(
+            flops=total * total * DH * 8,
+            bytes_accessed=total * DH * 400,
+            transcendentals=total * total // (2 * team_size),
+        ),
     )(*operands)
 
 
@@ -302,20 +308,200 @@
     return result
 
 
-def slot_tables(group_routes, experts, capacity):
-    count = group_routes.shape[0]
-    top_count = group_routes.shape[1]
+GELU_A = 0.7978845608028654
+GELU_B = 0.044715
+ROWS = 512
+
+
+def dot_nt(left, right):
+    return lax.dot_general(
+        left, right, (((1,), (1,)), ((), ())), preferred_element_type=jnp.float32
+    )
+
+
+def dot_tn(left, right):
+    return lax.dot_general(
+        left, right, (((0,), (0,)), ((), ())), preferred_element_type=jnp.float32
+    )
+
+
+def lane_of(column, shape):
+    return lax.broadcasted_iota(jnp.int32, shape, 1) == column
+
+
+def pad_units(weight, axis):
+    extra = -weight.shape[axis] % (2 * BLOCK)
+    pads = [(0, 0)] * weight.ndim
+    pads[axis] = (0, extra)
+    return jnp.pad(weight, pads)
+
+
+def expert_kernel(
+    experts,
+    h_ref,
+    router_ref,
+    keep_ref,
+    gate_ref,
+    up_ref,
+    back_ref,
+    dh_ref,
+    hidden_ref,
+    dgate_ref,
+    dup_ref,
+    dlogits_ref,
+    total,
+    gates,
+    dots,
+):
+    expert = pl.program_id(0)
+    rows = pl.ds(pl.multiple_of(pl.program_id(1) * ROWS, ROWS), ROWS)
+    f32 = jnp.float32
+    bf16 = jnp.bfloat16
+    lanes = (ROWS, router_ref.shape[1])
+    h = h_ref[rows, :]
+
+    @pl.when(expert == 0)
+    def _():
+        logits = dot(h, router_ref[...])
+        real = lax.broadcasted_iota(jnp.int32, lanes, 1) < experts
+        logits = jnp.where(real, logits, NEG)
+        expo = jnp.exp(logits - jnp.max(logits, axis=1, keepdims=True))
+        gates[rows, :] = expo / jnp.sum(expo, axis=1, keepdims=True)
+        dots[rows, :] = jnp.zeros(lanes, f32)
+
+    here = lane_of(expert, lanes)
+    weight = jnp.sum(
+        jnp.where(here, gates[rows, :] * keep_ref[rows, :], 0.0), axis=1, keepdims=True
+    )
+    g = dot_nt(h, gate_ref[0])
+    u = dot_nt(h, up_ref[0])
+    c = back_ref[0]
+    square = g * g
+    th = jnp.tanh(GELU_A * g * (1.0 + GELU_B * square))
+    cdf = 0.5 + 0.5 * th
+    gelu = g * cdf
+    slope = cdf + (0.5 * GELU_A) * g * (1.0 - th * th) * (1.0 + 3.0 * GELU_B * square)
+    hidden = (gelu * u).astype(bf16).astype(f32)
+    hidden_ref[0] = (hidden * weight).astype(bf16)
+    dots[rows, :] = jnp.where(here, jnp.sum(hidden * c, axis=1, keepdims=True), dots[rows, :])
+    dc = c * weight
+    dup = (dc * gelu).astype(bf16)
+    dgate = (dc * u * slope).astype(bf16)
+    dup_ref[0] = dup
+    dgate_ref[0] = dgate
+    part = dot(dgate, gate_ref[0]) + dot(dup, up_ref[0])
+
+    @pl.when(expert == 0)
+    def _():
+        total[rows, :] = part
+
+    @pl.when((expert > 0) & (expert < experts - 1))
+    def _():
+        total[rows, :] += part
+
+    @pl.when(expert == experts - 1)
+    def _():
+        probs = gates[rows, :]
+        dg = dots[rows, :] * keep_ref[rows, :]
+        dl = probs * (dg - jnp.sum(probs * dg, axis=1, keepdims=True))
+        dlogits_ref[rows, :] = dl
+        high = dl.astype(bf16)
+        rest = (dl - high.astype(f32)).astype(bf16)
+        extra = dot_nt(high, router_ref[...]) + dot_nt(rest, router_ref[...])
+        dh_ref[rows, :] = (total[rows, :] + part + extra).astype(bf16)
+
+
+def expert_layer(h_all, router_wide, keep_wide, w_gate, w_up, back):
+    experts, units, width = w_gate.shape
+    rows = h_all.shape[0]
+    lanes = router_wide.shape[1]
+    f32 = jnp.float32
+    bf16 = jnp.bfloat16
+    whole = lambda e, c: (0, 0)
+    weights = pl.BlockSpec((1, units, width), lambda e, c: (e, 0, 0))
+    tile = pl.BlockSpec((1, ROWS, units), lambda e, c: (e, c, 0))
+    wide = jax.ShapeDtypeStruct((experts, rows, units), bf16)
+    return pl.pallas_call(
+        functools.partial(expert_kernel, experts),
+        out_shape=[
+            jax.ShapeDtypeStruct((rows, width), bf16),
+            wide,
+            wide,
+            wide,
+            jax.ShapeDtypeStruct((rows, lanes), f32),
+        ],
+        grid=(experts, rows // ROWS),
+        in_specs=[
+            pl.BlockSpec((rows, width), whole),
+            pl.BlockSpec((width, lanes), whole),
+            pl.BlockSpec((rows, lanes), whole),
+            weights,
+            weights,
+            tile,
+        ],
+        out_specs=[
+            pl.BlockSpec((rows, width), whole),
+            tile,
+            tile,
+            tile,
+            pl.BlockSpec((rows, lanes), whole),
+        ],
+        scratch_shapes=[
+            pltpu.VMEM((rows, width), f32),
+            pltpu.VMEM((rows, lanes), f32),
+            pltpu.VMEM((rows, lanes), f32),
+        ],
+        compiler_params=pltpu.CompilerParams(vmem_limit_bytes=VMEM_LIMIT),
+        cost_estimate=pl.CostEstimate(
+            flops=8 * experts * rows * units * width,
+            bytes_accessed=experts * units * (4 * width + 10 * rows) + 4 * rows * width,
+            transcendentals=experts * rows * units,
+        ),
+    )(h_all, router_wide, keep_wide, w_gate, w_up, back)
+
+
+def weight_grads_kernel(first_ref, h_ref, grad_ref, hidden_ref, dgate_ref, dup_ref, *rest):
+    outs = rest[-3:]
+    lefts = (dgate_ref, dup_ref, hidden_ref)
+    rights = (h_ref, h_ref, grad_ref)
+    for index, (left, right, out) in enumerate(zip(lefts, rights, outs)):
+        part = dot_tn(left[0], right[...])[: out.shape[1]]
+        if len(rest) > 3:
+            part = part + rest[index][0].astype(jnp.float32)
+        out[0] = part.astype(out.dtype)
+
+
+def weight_grads(first, count, real, h_all, grad_all, hidden, dgate, dup, arrived):
+    _, rows, units = hidden.shape
+    width = h_all.shape[1]
+    whole = pl.BlockSpec((rows, width), lambda e, first: (0, 0))
+    tile = pl.BlockSpec((1, rows, units), lambda e, first: (first[0] + e, 0, 0))
+    out = pl.BlockSpec((1, real, width), lambda e, first: (e, 0, 0))
+    return pl.pallas_call(
+        weight_grads_kernel,
+        out_shape=[jax.ShapeDtypeStruct((count, real, width), jnp.bfloat16)] * 3,
+        grid_spec=pltpu.PrefetchScalarGridSpec(
+            num_scalar_prefetch=1,
+            grid=(count,),
+            in_specs=[whole, whole, tile, tile, tile] + [out] * len(arrived),
+            out_specs=[out] * 3,
+        ),
+        compiler_params=pltpu.CompilerParams(vmem_limit_bytes=VMEM_LIMIT),
+        cost_estimate=pl.CostEstimate(
+            flops=6 * count * rows * units * width,
+            bytes_accessed=count * units * 6 * (rows + width) + 4 * rows * width,
+            transcendentals=0,
+        ),
+    )(first, h_all, grad_all, hidden, dgate, dup, *arrived)
+
+
+def kept_choices(group_routes, experts, capacity):
+    count, top_count = group_routes.shape
     flat = group_routes.T.reshape(-1)
     hot = (flat[:, None] == jnp.arange(experts, dtype=jnp.int32)[None, :]).astype(jnp.int32)
-    rank_of = jnp.sum((jnp.cumsum(hot, axis=0) - hot) * hot, axis=1)
-    kept = rank_of < capacity
-    dest = jnp.where(kept, flat * capacity + rank_of, experts * capacity)
-    tokens = jnp.tile(jnp.arange(count, dtype=jnp.int32), top_count)
-    token_of_slot = (
-        jnp.zeros((experts * capacity + 1,), jnp.int32).at[dest].set(tokens)[: experts * capacity]
-    )
-    live = jnp.zeros((experts * capacity + 1,), jnp.float32).at[dest].set(1.0)[: experts * capacity]
-    return (dest, kept.reshape(top_count, count).astype(jnp.float32), token_of_slot, live)
+    earlier = jnp.cumsum(hot, axis=0) - hot
+    kept = jnp.where(earlier < capacity, hot, 0)
+    return jnp.sum(kept.reshape(top_count, count, experts), axis=0).astype(jnp.float32)
 
 
 def on_device(
@@ -350,7 +536,8 @@
     experts = w_gate.shape[0]
     top_count = routes.shape[1]
     capacity = 5 * top_count * group_rows // (4 * experts)
-    slot_count = experts * capacity
+    units = w_gate.shape[2]
+    core = ctx_index % 2
     bucket_count = bias_table.shape[0]
     f32 = jnp.float32
     bf16 = jnp.bfloat16
@@ -359,6 +546,71 @@
     normed_one = x_float * inv_one
     h_one = (normed_one * gain_one).astype(bf16)
     h_one_all = lax.all_gather(h_one, "tp", axis=0, tiled=True)
+    gate_wide = pad_units(jnp.swapaxes(w_gate, 1, 2), 1)
+    up_wide = pad_units(jnp.swapaxes(w_up, 1, 2), 1)
+    down_wide = pad_units(w_down, 1)
+    h_one_all, w_out_own, cotangent_own, gate_wide, up_wide, down_wide = (
+        lax.optimization_barrier(
+            (h_one_all, w_out, cotangent, gate_wide, up_wide, down_wide)
+        )
+    )
+
+    def turned(x, axis, step):
+        size = lax.axis_size(axis)
+        return lax.ppermute(x, axis, [(at, (at + step) % size) for at in range(size)])
+
+    def crossed(x, axis, bits):
+        size = lax.axis_size(axis)
+        return lax.ppermute(x, axis, [(at, at ^ bits) for at in range(size)])
+
+    def tp_scatter(x):
+        chunks = x.reshape((tp_count, x.shape[0] // tp_count) + x.shape[1:])
+        pieces = [lax.dynamic_index_in_dim(chunks, tp_index, 0, False)]
+        for step in range(1, tp_count):
+            chunk = lax.dynamic_index_in_dim(chunks, (tp_index + step) % tp_count, 0, False)
+            pieces.append(turned(chunk, "tp", step))
+        return pieces
+
+    def summed(pieces):
+        total = pieces[0].astype(f32)
+        for piece in pieces[1:]:
+            total = total + piece.astype(f32)
+        return total
+
+    chips = ctx_count // 2
+    chip = ctx_index // 2
+
+    def ctx_sum(x):
+        half = x.shape[0] // 2
+        away = lax.dynamic_slice_in_dim(x, (1 - core) * half, half, 0)
+        mine = lax.dynamic_slice_in_dim(x, core * half, half, 0)
+        mine = (mine.astype(f32) + crossed(away, "ctx", 1).astype(f32)).astype(bf16)
+        chunks = mine.reshape((chips, half // chips) + x.shape[1:])
+        total = lax.dynamic_index_in_dim(chunks, chip, 0, False).astype(f32)
+        for bits in range(1, chips):
+            chunk = lax.dynamic_index_in_dim(chunks, chip ^ bits, 0, False)
+            total = total + crossed(chunk, "ctx", 2 * bits).astype(f32)
+        total = total.astype(bf16)
+        result = lax.dynamic_update_index_in_dim(jnp.zeros_like(chunks), total, chip, 0)
+        for bits in range(1, chips):
+            got = crossed(total, "ctx", 2 * bits)
+            result = lax.dynamic_update_index_in_dim(result, got, chip ^ bits, 0)
+        result = result.reshape((half,) + x.shape[1:])
+        other = crossed(result, "ctx", 1)
+        first = jnp.where(core == 0, result, other)
+        second = jnp.where(core == 0, other, result)
+        return jnp.concatenate([first, second], axis=0).astype(f32)
+
+    def sum_everywhere(x):
+        for axis in ("ctx", "tp"):
+            bits = 1
+            while bits < lax.axis_size(axis):
+                x = x + crossed(x, axis, bits)
+                bits *= 2
+        return x
+
+    w_out_all = lax.all_gather(w_out_own, "tp", axis=0, tiled=True)
+    grad_all = lax.all_gather(cotangent_own, "tp", axis=0, tiled=True)
     w_qkv = jnp.concatenate([w_query, w_key, w_value], axis=1)
     qkv = lax.dot_general(
         w_qkv, h_one_all, (((0,), (1,)), ((), ())), preferred_element_type=f32
@@ -427,6 +679,31 @@
             route.append((device, base + (device % team + step) % team))
         return lax.ppermute(x, "ctx", route)
 
+    direct = pair_count == tp_count
+    spot = (ctx_index + tp_index) % team
+
+    def rows_from_heads(x):
+        if direct:
+            got = lax.all_to_all(x, ("ctx", "tp"), 0, 0, tiled=True)
+            split = got.reshape(head_count, 1, team, tp_count, DH, BLOCK)
+            split = turn_halves(split, 1, spot[None], -1)
+            split = split.transpose(3, 0, 4, 1, 2, 5)
+        else:
+            split = from_heads(x, 1).reshape(width_loc, tp_count, rows_dev)
+            split = lax.all_to_all(split.transpose(1, 0, 2), "tp", 0, 0, tiled=True)
+        return split.reshape(tp_count * width_loc, rows_dev)
+
+    def heads_from_rows(x):
+        if direct:
+            split = x.reshape(tp_count, head_count, DH, 1, team, BLOCK)
+            split = split.transpose(1, 3, 4, 0, 2, 5)
+            split = turn_halves(split, 1, spot[None], 1)
+            send = split.reshape(ctx_count * tp_count, DH, BLOCK)
+            return lax.all_to_all(send, ("ctx", "tp"), 0, 0, tiled=True)
+        send = x.reshape(tp_count, width_loc, rows_dev)
+        got = lax.all_to_all(send, "tp", 0, 0, tiled=True)
+        return to_heads(got.transpose(1, 0, 2).reshape(width_loc, group_rows), 1)
+
     own_qkv = to_heads(qkv, 3)
     own_pairs = own_qkv[:, DH:, :]
     parts = [own_qkv] + [team_shift(own_pairs, -step) for step in range(1, team)]
@@ -446,101 +723,70 @@
         total,
         [],
     )
-    attended_bf = from_heads(att_slots, 1)
-    attn_rows = lax.psum_scatter(
-        lax.dot_general(
-            attended_bf, w_out, (((0,), (0,)), ((), ())), preferred_element_type=f32
-        ).astype(jnp.bfloat16),
-        "tp",
-        scatter_dimension=0,
-        tiled=True,
-    ).astype(jnp.float32)
-    mixed_in = x_float + attn_rows
+    attended_rows = rows_from_heads(att_slots)
+    mixed_in = x_float + lax.dot_general(
+        attended_rows, w_out_all, (((0,), (0,)), ((), ())), preferred_element_type=f32
+    )
     inv_two = lax.rsqrt(jnp.mean(mixed_in * mixed_in, axis=1, keepdims=True) + EPS)
     normed_two = mixed_in * inv_two
     h_two = (normed_two * gain_two).astype(bf16)
     h_two_all = lax.all_gather(h_two, "tp", axis=0, tiled=True)
-    logits = jnp.dot(h_two_all, w_router, preferred_element_type=f32)
-    expo = jnp.exp(logits - jnp.max(logits, axis=1, keepdims=True))
-    gates = expo / jnp.sum(expo, axis=1, keepdims=True)
-    dest, kept, token_of_slot, live = slot_tables(routes, experts, capacity)
-    expert_ids = jnp.arange(experts, dtype=jnp.int32)
-    chosen = (routes.T[:, :, None] == expert_ids[None, None, :]).astype(f32)
-    picked = jnp.sum(gates[None] * chosen, axis=2) * kept
-    weight_slot = jnp.zeros((slot_count + 1,), f32).at[dest].set(picked.reshape(-1))[:slot_count]
-    expert_in = jnp.where(
-        live[:, None] > 0, jnp.take(h_two_all, token_of_slot, axis=0), jnp.zeros((), bf16)
-    ).reshape(experts, capacity, width)
-    gate_pre = jnp.einsum("ecd,edf->ecf", expert_in, w_gate, preferred_element_type=f32)
-    up_pre = jnp.einsum("ecd,edf->ecf", expert_in, w_up, preferred_element_type=f32)
-    hidden = (jax.nn.gelu(gate_pre, approximate=True) * up_pre).astype(bf16)
-    expert_out = jnp.einsum("ecf,efd->ecd", hidden, w_down, preferred_element_type=f32).reshape(
-        slot_count, width
-    )
-    rows_back = jnp.take(expert_out, jnp.minimum(dest, slot_count - 1), axis=0).reshape(
-        top_count, group_rows, width
-    )
-    mixed_part = jnp.sum(picked[:, :, None] * rows_back, axis=0)
-    mixed_rows = lax.psum_scatter(
-        mixed_part.astype(jnp.bfloat16), "tp", scatter_dimension=0, tiled=True
-    ).astype(jnp.float32)
-    layer_out = mixed_in + mixed_rows
+    lanes = BLOCK
+    keep = kept_choices(routes, experts, capacity)
+    keep_wide = jnp.pad(keep, ((0, 0), (0, lanes - experts)))
+    router_wide = jnp.pad(w_router, ((0, 0), (0, lanes - experts)))
+    back = jnp.einsum("rd,efd->erf", grad_all, down_wide, preferred_element_type=f32)
+    d_h_part, hidden, d_gate_bf, d_up_bf, d_logits = expert_layer(
+        h_two_all, router_wide, keep_wide, gate_wide, up_wide, back
+    )
+    d_h_two = lax.psum_scatter(d_h_part, "tp", scatter_dimension=0, tiled=True).astype(f32)
+    some = experts // 2
+    operands = (h_two_all, grad_all, hidden, d_gate_bf, d_up_bf)
+    away = weight_grads(
+        ((1 - core) * some).astype(jnp.int32).reshape(1), some, units, *operands, ()
+    )
+    arrived = [crossed(grads, "ctx", 1) for grads in away]
+    mine = weight_grads(
+        (core * some).astype(jnp.int32).reshape(1), some, units, *operands, arrived
+    )
+    d_h_two, *_ = lax.optimization_barrier((d_h_two, *mine))
+    same_core = [list(range(first, ctx_count, 2)) for first in range(2)]
+
+    def both_halves(grads):
+        other = crossed(grads, "ctx", 1)
+        first = jnp.where(core == 0, grads, other)
+        second = jnp.where(core == 0, other, grads)
+        return jnp.concatenate([first, second], axis=0).astype(f32)
+
+    mine = lax.psum(tuple(mine), "ctx", axis_index_groups=same_core)
     grad_float = cotangent.astype(f32)
-    grad_all = lax.all_gather(cotangent, "tp", axis=0, tiled=True)
-    gate_dots = jnp.sum(rows_back * grad_all.astype(f32)[None], axis=2)
-    d_expert_out = (
-        (jnp.take(grad_all, token_of_slot, axis=0).astype(f32) * weight_slot[:, None])
-        .astype(bf16)
-        .reshape(experts, capacity, width)
-    )
-    d_hidden = jnp.einsum("ecd,efd->ecf", d_expert_out, w_down, preferred_element_type=f32)
-    grad_down = jnp.einsum("ecf,ecd->efd", hidden, d_expert_out, preferred_element_type=f32)
-    _, glu_pull = jax.vjp(
-        lambda gate_val, up_val: jax.nn.gelu(gate_val, approximate=True) * up_val, gate_pre, up_pre
-    )
-    d_gate_pre, d_up_pre = glu_pull(d_hidden)
-    d_gate_bf = d_gate_pre.astype(bf16)
-    d_up_bf = d_up_pre.astype(bf16)
-    grad_gate = jnp.einsum("ecd,ecf->edf", expert_in, d_gate_bf, preferred_element_type=f32)
-    grad_up = jnp.einsum("ecd,ecf->edf", expert_in, d_up_bf, preferred_element_type=f32)
-    d_expert_in = (
-        jnp.einsum("ecf,edf->ecd", d_gate_bf, w_gate, preferred_element_type=f32)
-        + jnp.einsum("ecf,edf->ecd", d_up_bf, w_up, preferred_element_type=f32)
-    ).reshape(slot_count, width)
-    d_h_two_part = (
-        jnp.zeros((group_rows, width), f32).at[token_of_slot].add(d_expert_in * live[:, None])
-    )
-    d_h_two, dots_own = (
-        lax.psum_scatter(
-            d_h_two_part.astype(jnp.bfloat16), "tp", scatter_dimension=0, tiled=True
-        ).astype(jnp.float32),
-        lax.psum_scatter(
-            gate_dots.T.astype(jnp.bfloat16), "tp", scatter_dimension=0, tiled=True
-        ).astype(jnp.float32),
-    )
-    own_start = tp_index * rows_dev
-    gates_own = lax.dynamic_slice_in_dim(gates, own_start, rows_dev, 0)
-    routes_own = lax.dynamic_slice_in_dim(routes, own_start, rows_dev, 0)
-    kept_own = lax.dynamic_slice_in_dim(kept, own_start, rows_dev, 1)
-    hot_own = (routes_own[:, :, None] == expert_ids[None, None, :]).astype(f32)
-    d_gates = jnp.sum((dots_own * kept_own.T)[:, :, None] * hot_own, axis=1)
-    d_logits = gates_own * (d_gates - jnp.sum(gates_own * d_gates, axis=1, keepdims=True))
-    d_h_two = d_h_two + jnp.dot(
-        d_logits, w_router.astype(f32).T, precision=HIGH, preferred_element_type=f32
-    )
-    grad_router_part = jnp.dot(h_two.T, d_logits, precision=HIGH, preferred_element_type=f32)
+    grad_router_part = lax.dot_general(
+        h_two_all.astype(f32),
+        d_logits[:, :experts],
+        (((0,), (0,)), ((), ())),
+        precision=HIGH,
+        preferred_element_type=f32,
+    )
     d_norm_two = d_h_two * gain_two
     grad_gain_two_part = jnp.sum(d_h_two * normed_two, axis=0)
     d_mixed = grad_float + inv_two * (
         d_norm_two - normed_two * jnp.mean(d_norm_two * normed_two, axis=1, keepdims=True)
     )
     d_attn = d_mixed.astype(bf16)
-    piece = lax.all_gather(d_attn, "tp", axis=0, tiled=True)
-    d_attended = jnp.einsum("hd,rd->hr", w_out, piece, preferred_element_type=f32).astype(bf16)
-    grad_out = jnp.einsum("hr,rd->hd", attended_bf, piece, preferred_element_type=f32)
-    d_att_slots = to_heads(d_attended, 1)
+    d_attended = lax.dot_general(
+        w_out_all, d_attn, (((1,), (1,)), ((), ())), preferred_element_type=f32
+    ).astype(bf16)
+    d_att_slots = heads_from_rows(d_attended)
+    hidden, d_attn = lax.optimization_barrier((hidden, d_attn))
+    mixed_part = jnp.einsum(
+        "ecf,efd->cd", hidden[:, :, :units], w_down, preferred_element_type=f32
+    )
+    mixed_pieces = tp_scatter(mixed_part.astype(bf16))
+    out_pieces = tp_scatter(
+        jnp.dot(attended_rows, d_attn, preferred_element_type=f32).astype(bf16)
+    )
     pair_block = jax.ShapeDtypeStruct((slot_blocks, 2 * DH, BLOCK), bf16)
-    back = attention_call(
+    back_out = attention_call(
         backward_kernel,
         team,
         bucket_count,
@@ -556,52 +802,72 @@
             pltpu.VMEM((2 * BLOCK, BLOCK), f32),
         ],
     )
-    pair_grads = back[1].astype(f32)
+    mixed_pieces, out_pieces, back_out = lax.optimization_barrier(
+        (mixed_pieces, out_pieces, tuple(back_out))
+    )
+    layer_out = mixed_in + summed(mixed_pieces)
+    grad_out = summed(out_pieces)
+    pair_grads = back_out[1].astype(f32)
     for step in range(1, team):
-        pair_grads = pair_grads + team_shift(back[1 + step], step).astype(f32)
-    d_cat = from_heads(jnp.concatenate([back[0], pair_grads.astype(bf16)], axis=1), 3)
+        pair_grads = pair_grads + team_shift(back_out[1 + step], step).astype(f32)
+    d_cat = from_heads(jnp.concatenate([back_out[0], pair_grads.astype(bf16)], axis=1), 3)
     grad_qkv = jnp.einsum("rd,hr->dh", h_one_all, d_cat, preferred_element_type=f32)
-    grad_table_part = back[1 + team][0, :bucket_count, None] * head_hot[None, :]
+    table_part = jnp.pad(
+        back_out[1 + team][0, :bucket_count, None] * head_hot[None, :],
+        ((0, 0), (0, (tp_count - 1) * head_count)),
+    )
+    table_part = jnp.roll(table_part, tp_index * head_count, axis=1)
+    gain_one_part = jnp.sum(grad_qkv * w_qkv.astype(f32), axis=1) / gain_one
     d_h_one_part = jnp.einsum("hr,dh->rd", d_cat, w_qkv, preferred_element_type=f32)
     d_h_one = lax.psum_scatter(
-        d_h_one_part.astype(jnp.bfloat16), "tp", scatter_dimension=0, tiled=True
-    ).astype(jnp.float32)
+        d_h_one_part.astype(bf16), "tp", scatter_dimension=0, tiled=True
+    ).astype(f32)
     d_norm_one = d_h_one * gain_one
-    grad_gain_one_part = jnp.sum(d_h_one * normed_one, axis=0)
     grad_x = d_mixed + inv_one * (
         d_norm_one - normed_one * jnp.mean(d_norm_one * normed_one, axis=1, keepdims=True)
     )
-    gain_one_share, gain_two_share, router_share = (
-        lax.psum_scatter(grad_gain_one_part, "tp", scatter_dimension=0, tiled=True),
-        lax.psum_scatter(grad_gain_two_part, "tp", scatter_dimension=0, tiled=True),
-        lax.psum_scatter(grad_router_part, "tp", scatter_dimension=0, tiled=True),
-    )
-    rest_total = (
-        lax.psum(grad_qkv[:, :width_loc].astype(jnp.bfloat16), "ctx").astype(jnp.float32),
-        lax.psum(grad_qkv[:, width_loc : 2 * width_loc].astype(jnp.bfloat16), "ctx").astype(
-            jnp.float32
-        ),
-        lax.psum(grad_qkv[:, 2 * width_loc :].astype(jnp.bfloat16), "ctx").astype(jnp.float32),
-        lax.psum(grad_out.astype(jnp.bfloat16), "ctx").astype(jnp.float32),
-        lax.psum(grad_table_part.astype(jnp.bfloat16), "ctx").astype(jnp.float32),
-        lax.psum(gain_one_share.astype(jnp.bfloat16), "ctx").astype(jnp.float32),
-        lax.psum(gain_two_share.astype(jnp.bfloat16), "ctx").astype(jnp.float32),
-        lax.psum(router_share.astype(jnp.bfloat16), "ctx").astype(jnp.float32),
-    )
+    small = jnp.concatenate(
+        [
+            gain_one_part,
+            grad_gain_two_part,
+            grad_router_part.reshape(-1),
+            table_part.reshape(-1),
+        ]
+    )
+    small = sum_everywhere(small.reshape(-1, BLOCK)).reshape(-1)
+    own = width // tp_count
+    gain_one_all, gain_two_all, router_all, table_all = jnp.split(
+        small, [width, 2 * width, (2 + experts) * width]
+    )
+    gain_one_grad = lax.dynamic_slice_in_dim(gain_one_all, tp_index * own, own, 0)
+    gain_two_grad = lax.dynamic_slice_in_dim(gain_two_all, tp_index * own, own, 0)
+    router_grad = lax.dynamic_slice_in_dim(
+        router_all.reshape(width, experts), tp_index * own, own, 0
+    )
+    table_grad = lax.dynamic_slice_in_dim(
+        table_all.reshape(bucket_count, -1), tp_index * head_count, head_count, 1
+    )
+    grad_qkv, mine = lax.optimization_barrier((grad_qkv, mine))
+    out_wide = grad_out.reshape(width, width_loc)
+    wide = jnp.concatenate([grad_qkv, out_wide], axis=1)
+    wide = ctx_sum(wide.astype(bf16))
+    grad_qkv = wide[:, : 3 * width_loc]
+    grad_out = wide[:, 3 * width_loc :].reshape(width_loc, width)
+    grad_gate, grad_up, grad_down = [both_halves(grads) for grads in mine]
     return (
         layer_out,
         grad_x,
-        rest_total[5],
-        rest_total[0],
-        rest_total[1],
-        rest_total[2],
-        rest_total[3],
-        rest_total[4],
-        rest_total[6],
-        rest_total[7],
-        lax.psum(grad_gate.astype(jnp.bfloat16), "ctx").astype(jnp.float32),
-        lax.psum(grad_up.astype(jnp.bfloat16), "ctx").astype(jnp.float32),
-        lax.psum(grad_down.astype(jnp.bfloat16), "ctx").astype(jnp.float32),
+        gain_one_grad,
+        grad_qkv[:, :width_loc],
+        grad_qkv[:, width_loc : 2 * width_loc],
+        grad_qkv[:, 2 * width_loc :],
+        grad_out,
+        table_grad,
+        gain_two_grad,
+        router_grad,
+        jnp.swapaxes(grad_gate, 1, 2),
+        jnp.swapaxes(grad_up, 1, 2),
+        grad_down,
     )
 
 

time: 1090 us -> 645 us (0.59)
  waiting for transfers between devices: 546 us -> 185 us
  Pallas kernels: 128 us -> 206 us
  matrix products: 120 us -> 45.2 us
  other arithmetic: 119 us -> 68.6 us
  blocking collectives: 49.6 us -> 0 us
  starting transfers between devices: 8.25 us -> 49.7 us
  local copies, waits for them, and re-layouts: 87.8 us -> 66.9 us
    psum x1, waiting for transfers between devices: 252 us -> 0.14 us  [on_device(): mine = lax.psum(tuple(mine), 'ctx', axis_index_groups=same_core)]
    reduce_scatter x4 -> x2, waiting for transfers between devices: 100 us -> 0.01 us  [the longest x1 0.01 us: on_device(): lax.psum_scatter(d_h_part, 'tp', scatter_dimension=0, tiled=True)]
    dot_general x14 -> x6, matrix products: 107 us -> 31.3 us  [the longest x1 12.3 us: on_device(): jnp.einsum('rd,efd->erf', grad_all, down_wide, preferred_element_type=f32)]
    pallas_call x0 -> x3, Pallas kernels: none -> 74.3 us  [the longest x1 41.8 us: expert_layer(): pl.pallas_call(functools.partial(expert_kernel, experts), out_shape=[jax....]
    all_gather x2, waiting for transfers between devices: 70.1 us -> 0.02 us  [the longest x1 0.02 us: on_device(): w_out_all = lax.all_gather(w_out_own, 'tp', axis=0, tiled=True)]
    ppermute x0 -> x25, waiting for transfers between devices: none -> 37.7 us  [the longest x19 34 us: crossed(): return lax.ppermute(x, axis, [(at, at ^ bits) for at in range(size)])]
    ppermute x0 -> x25, starting transfers between devices: none -> 34 us  [the longest x19 27 us: crossed(): return lax.ppermute(x, axis, [(at, at ^ bits) for at in range(size)])]
    gather x3 -> x0, local copies, waits for them, and re-layouts: 33.1 us -> none  [the longest x1 15.6 us: on_device(): jnp.take(expert_out, jnp.minimum(dest, slot_count - 1), axis=0)]
  transfers between devices with their start and end apart: 15 -> 38, of which waited for: 12 -> 16; matrix products, arithmetic and copies ran while one was open for 14% -> 25% of each run, Pallas kernels for 0% -> 26%
where the time goes in v2:
time: 645 us; the launch traced here: 637 us
  Pallas kernels  206 us (32%)
  waiting for transfers between devices  185 us (29%)
  other arithmetic  68.6 us (11%)
  local copies, waits for them, and re-layouts  66.9 us (10%)
  starting transfers between devices  49.7 us (8%)
  matrix products  45.2 us (7%)
  between operations  15.4 us (2%)
    pallas_call x2, Pallas kernels, attention_call(): pl.pallas_call(functools.partial(kernel, bucket_count, parts), out_shape=...  131 us
    pallas_call x1, Pallas kernels, expert_layer(): pl.pallas_call(functools.partial(expert_kernel, experts), out_shape=[jax....  41.8 us
    all_to_all x1, waiting for transfers between devices, from_heads(): got = lax.all_to_all(send, 'ctx', 0, 0, tiled=True)  36.5 us
    ppermute x19, waiting for transfers between devices, crossed(): return lax.ppermute(x, axis, [(at, at ^ bits) for at in range(size)])  34 us
    all_gather x1, waiting for transfers between devices, on_device(): h_one_all = lax.all_gather(h_one, 'tp', axis=0, tiled=True)  32.9 us
    pallas_call x2, Pallas kernels, weight_grads(): pl.pallas_call(weight_grads_kernel, out_shape=[jax.ShapeDtypeStruct((coun...  32.5 us
    all_gather x1, waiting for transfers between devices, on_device(): h_two_all = lax.all_gather(h_two, 'tp', axis=0, tiled=True)  29.4 us
    ppermute x19, starting transfers between devices, crossed(): return lax.ppermute(x, axis, [(at, at ^ bits) for at in range(size)])  27 us
  transfers between devices with their start and end apart: 38, of which 16 were waited for; matrix products, arithmetic and copies ran while one was open for 25% of the time, Pallas kernels for 26%

profile of v2, /device:TPU:0, one launch (start us, length us, event | category | flops | bytes accessed | tf_op | source)
XLA Modules:
  0.0 637.2 jit_solution(8308280405996838109)
XLA Ops:
  10.6 6.7 %pad.22.gate_ref = bf16[4,768,1024]{2,1,0:T(8,128)(2,1)} pad(bf16[4,704,1024]{2,1,0:T(8,128)(2,1)} %bitcast.129, bf16[]{:T(256)} %constant.190.clone.1), padding=0_0x0_64x0_0 | pad | bytes 12058626 | tf_op jit(solution)/shard_map/jit(_pad)/pad | solution.py:336
  26.4 32.9 %all-gather.5.cloned.1.call-done = bf16[1024,1024]{1,0:T(8,128)(2,1)} async-done(((bf16[256,1024]{1,0:T(8,128)(2,1)}), bf16[1024,1024]{1,0:T(8,128)(2,1)}) %all-gather.5.cloned.1.call-update) | async-done | bytes 2097168 | tf_op jit(solution)/shard_map/all_gather | solution.py:548
  67.2 5.2 fusion.5
  78.3 20.5 %all-to-all-done = bf16[8,4,192,128]{3,2,1,0:T(8,128)(2,1)S(1)} async-done(((bf16[8,4,192,128]{3,2,1,0:T(8,128)(2,1)}), bf16[8,4,192,128]{3,2,1,0:T(8,128)(2,1)S(1)}, u32[]{:S(2)}, u32[]{:S(2)}) %all-to-all-start) | async-done | bytes 1572896 | tf_op jit(solution)/shard_map/all_to_all | solution.py:664
  104.4 61.3 %shard_map.264 = (bf16[32,64,128]{2,1,0:T(8,128)(2,1)}, f32[32,64,128]{2,1,0:T(8,128)}, f32[32,128]{1,0:T(8,128)}) custom-call(s32[64]{0:T(128)} %reshape.312.nat_ref, s32[32]{0:T(128)} %select_reduce_fusion.1.order_ref, s32[64]{0:T(128)} %and_select_fusion.1.low_ref, s32[32]{0:T(128)} %convert_reduce_fusion.thr_ref, f32[32]{0:T(128)} %subtract_multiply_fusion.tab_ref, ...), custom_call_target="tpu_custom_call" | custom-call | flops 34359738368 | bytes 209715200 | tf_op jit(solution)/shard_map/pallas_call | solution.py:285
  168.7 14.1 %all-to-all-done.1 = bf16[32,64,128]{2,1,0:T(8,128)(2,1)S(1)} async-done(((bf16[32,64,128]{2,1,0:T(8,128)(2,1)}), bf16[32,64,128]{2,1,0:T(8,128)(2,1)S(1)}, u32[]{:S(2)}, u32[]{:S(2)}) %all-to-all-start.1) | async-done | bytes 524320 | tf_op jit(solution)/shard_map/all_to_all | solution.py:687
  193.0 12.3 %convolution_bitcast_fusion.back_ref = f32[4,1024,768]{2,1,0:T(8,128)} fusion(bf16[4,768,1024]{2,1,0:T(8,128)(2,1)} %pad.24, bf16[1024,1024]{1,0:T(8,128)(2,1)} %all-gather.11.cloned.1.call-done.grad_ref), kind=kOutput, calls=%fused_computation.5 | convolution fusion | flops 6442450944 | bytes 20971520 | tf_op jit(solution)/shard_map/rd,efd->erf/dot_general | solution.py:738
  205.2 29.4 %all-gather.9.cloned.1.call-done.h_ref = bf16[1024,1024]{1,0:T(8,128)(2,1)} async-done(((bf16[256,1024]{1,0:T(8,128)(2,1)}), bf16[1024,1024]{1,0:T(8,128)(2,1)}) %all-gather.9.cloned.1.call-update) | async-done | bytes 2097168 | tf_op jit(solution)/shard_map/all_gather | solution.py:733
  234.6 41.8 %shard_map.265 = (bf16[1024,1024]{1,0:T(8,128)(2,1)}, bf16[4,1024,768]{2,1,0:T(8,128)(2,1)}, bf16[4,1024,768]{2,1,0:T(8,128)(2,1)}, bf16[4,1024,768]{2,1,0:T(8,128)(2,1)}, f32[1024,128]{1,0:T(8,128)}) custom-call(bf16[1024,1024]{1,0:T(8,128)(2,1)} %all-gather.9.cloned.1.call-done.h_ref, bf16[1024,128]{1,0:T(8,128)(2,1)} %pad.25.router_ref, ...), custom_call_target="tpu_custom_call" | custom-call | flops 25769803776 | bytes 48234496 | tf_op jit(solution)/shard_map/pallas_call | solution.py:424
  276.9 15.4 %shard_map.266 = (bf16[2,704,1024]{2,1,0:T(8,128)(2,1)}, bf16[2,704,1024]{2,1,0:T(8,128)(2,1)}, bf16[2,704,1024]{2,1,0:T(8,128)(2,1)}) custom-call(s32[1]{0:T(128)} %bitcast.15.first_ref, bf16[1024,1024]{1,0:T(8,128)(2,1)} %all-gather.9.cloned.1.call-done.h_ref, bf16[1024,1024]{1,0:T(8,128)(2,1)} %all-gather.11.cloned.1.call-done.grad_ref, ...), custom_call_target="tpu_custom_call" | custom-call | flops 9663676416 | bytes 23068672 | tf_op jit(solution)/shard_map/pallas_call | solution.py:480
  292.9 5.1 collective-permute-done.1.rest_0_
  306.2 17.1 %shard_map.267 = (bf16[2,704,1024]{2,1,0:T(8,128)(2,1)}, bf16[2,704,1024]{2,1,0:T(8,128)(2,1)}, bf16[2,704,1024]{2,1,0:T(8,128)(2,1)}) custom-call(s32[1]{0:T(128)} %bitcast.14.first_ref, bf16[1024,1024]{1,0:T(8,128)(2,1)} %all-gather.9.cloned.1.call-done.h_ref, bf16[1024,1024]{1,0:T(8,128)(2,1)} %all-gather.11.cloned.1.call-done.grad_ref, ...), custom_call_target="tpu_custom_call" | custom-call | flops 9663676416 | bytes 23068672 | tf_op jit(solution)/shard_map/pallas_call | solution.py:480
  345.2 10.0 %bitcast_convert_fusion = bf16[1024,1024]{1,0:T(8,128)(2,1)S(1)} fusion(bf16[4,704,1024]{2,1,0:T(8,128)(2,1)} %param.28, bf16[4,1024,768]{2,1,0:T(8,128)(2,1)} %get-tuple-element.74.hidden_ref), kind=kOutput, calls=%fused_computation.6 | convolution fusion | flops 5906628608 | bytes 14155776 | tf_op jit(solution)/shard_map/ecf,efd->cd/dot_general | solution.py:781
  361.6 11.6 %all-to-all-done.2.rest_2_ = bf16[32,64,128]{2,1,0:T(8,128)(2,1)} async-done(((bf16[32,64,128]{2,1,0:T(8,128)(2,1)}), bf16[32,64,128]{2,1,0:T(8,128)(2,1)}, u32[]{:S(2)}, u32[]{:S(2)}) %all-to-all-start.2) | async-done | bytes 524320 | tf_op jit(solution)/shard_map/all_to_all | solution.py:702
  373.2 70.1 %shard_map.268 = (bf16[32,64,128]{2,1,0:T(8,128)(2,1)}, bf16[32,128,128]{2,1,0:T(8,128)(2,1)}, bf16[32,128,128]{2,1,0:T(8,128)(2,1)}, f32[1,128]{1,0:T(1,128)}) custom-call(s32[64]{0:T(128)} %reshape.312.nat_ref, s32[32]{0:T(128)} %select_reduce_fusion.1.order_ref, s32[64]{0:T(128)} %and_select_fusion.1.low_ref, s32[32]{0:T(128)} %convert_reduce_fusion.thr_ref, ...), custom_call_target="tpu_custom_call" | custom-call | flops 34359738368 | bytes 209715200 | tf_op jit(solution)/shard_map/pallas_call | solution.py:285
  453.8 36.5 %all-to-all-done.3 = bf16[8,4,192,128]{3,2,1,0:T(8,128)(2,1)} async-done(((bf16[8,4,192,128]{3,2,1,0:T(8,128)(2,1)}), bf16[8,4,192,128]{3,2,1,0:T(8,128)(2,1)}, u32[]{:S(2)}, u32[]{:S(2)}) %all-to-all-start.3) | async-done | bytes 1572896 | tf_op jit(solution)/shard_map/all_to_all | solution.py:669
  495.8 6.5 %broadcast_select_fusion = bf16[3,4,64,4,2,128]{5,4,3,2,1,0:T(2,128)(2,1)} fusion(pred[4]{0:T(512)(128)(4,1)S(1)} %copy-done.30, bf16[3,4,64,4,1,128]{5,4,3,2,1,0:T(2,128)(2,1)S(1)} %get-tuple-element.179, bf16[3,4,64,4,1,128]{5,4,3,2,1,0:T(2,128)(2,1)S(1)} %get-tuple-element.178, bf16[4,2,4,3,64,128]{5,4,3,2,1,0:T(8,128)(2,1)} %bitcast.30), kind=kLoop, calls=%fused_computation.8 | loop fusion | flops 3932160 | bytes 4718596 | tf_op jit(solution)/shard_map/jit(_where)/select_n | solution.py:307
  515.4 5.4 multiply_reduce_fusion
  541.5 10.8 %collective-permute-done.13 = f32[52,128]{1,0:T(8,128)S(1)} collective-permute-done((f32[52,128]{1,0:T(8,128)S(1)}, f32[52,128]{1,0:T(8,128)S(1)}, u32[]{:S(2)}, u32[]{:S(2)}) %collective-permute-start.13) | collective-permute-done | bytes 26656 | tf_op jit(solution)/shard_map/ppermute | solution.py:564
  552.3 11.9 %collective-permute-start.14 = (f32[52,128]{1,0:T(8,128)S(1)}, f32[52,128]{1,0:T(8,128)S(1)}, u32[]{:S(2)}, u32[]{:S(2)}) collective-permute-start(f32[52,128]{1,0:T(8,128)S(1)} %add.319), channel_id=1, source_target_pairs={{0,1},{1,0},{2,3},{3,2},{4,5},{5,4},{6,7},{7,6},{8,9},{9,8},{10,11... | collective-permute-start | bytes 79880 | tf_op jit(solution)/shard_map/ppermute | solution.py:564
  584.5 7.2 %collective-permute-done.21 = bf16[128,1024]{1,0:T(8,128)(2,1)} collective-permute-done((bf16[128,1024]{1,0:T(8,128)(2,1)}, bf16[128,1024]{1,0:T(8,128)(2,1)}, u32[]{:S(2)}, u32[]{:S(2)}) %collective-permute-start.21) | collective-permute-done | bytes 262176 | tf_op jit(solution)/shard_map/ppermute | solution.py:564
  610.0 5.2 maximum_convert_fusion
  617.3 5.2 convert_bitcast_fusion
  624.7 5.2 convert_bitcast_fusion.1
  (286 shorter events, 174.5 us)
Async XLA Ops:
  7.2 52.1 %all-gather.5.cloned.1.call-start = ((), (), s32[]{:S(2)}) async-start(), calls=%async_computation.6 | async-start | bytes 2621440 | tf_op jit(solution)/shard_map/all_gather | solution.py:548
  10.5 174.9 %all-gather.7.cloned.1.call-start = ((), (), s32[]{:S(2)}) async-start(), calls=%async_computation.7 | async-start | bytes 2621440 | tf_op jit(solution)/shard_map/all_gather | solution.py:612
  74.0 24.8 %all-to-all-start = ((bf16[8,4,192,128]{3,2,1,0:T(8,128)(2,1)}), bf16[8,4,192,128]{3,2,1,0:T(8,128)(2,1)S(1)}, u32[]{:S(2)}, u32[]{:S(2)}) async-start(bf16[8,4,192,128]{3,2,1,0:T(8,128)(2,1)} %bitcast.6), calls=%async_computation | async-start | bytes 3145728 | tf_op jit(solution)/shard_map/all_to_all | solution.py:664
  77.8 115.2 %all-gather.11.cloned.1.call-start = ((), (), s32[]{:S(2)}) async-start(), calls=%async_computation.9 | async-start | bytes 2621440 | tf_op jit(solution)/shard_map/all_gather | solution.py:613
  165.8 17.0 %all-to-all-start.1 = ((bf16[32,64,128]{2,1,0:T(8,128)(2,1)}), bf16[32,64,128]{2,1,0:T(8,128)(2,1)S(1)}, u32[]{:S(2)}, u32[]{:S(2)}) async-start(bf16[32,64,128]{2,1,0:T(8,128)(2,1)} %get-tuple-element.57), calls=%async_computation.1 | async-start | bytes 1048576 | tf_op jit(solution)/shard_map/all_to_all | solution.py:687
  168.4 66.2 %all-gather.9.cloned.1.call-start = ((), (), s32[]{:S(2)}) async-start(), calls=%async_computation.8 | async-start | bytes 2621440 | tf_op jit(solution)/shard_map/all_gather | solution.py:733
  189.0 134.3 %reduce-scatter.3.cloned.1.call-start = ((), (), s32[]{:S(2)}) async-start(), calls=%async_computation.10 | async-start | bytes 2621440 | tf_op jit(solution)/shard_map/reduce_scatter | solution.py:742
  276.4 244.5 %all-reduce.9.cloned.1.call-start = ((), (), s32[]{:S(2)}) async-start(), calls=%async_computation.12 | async-start | bytes 17301504 | tf_op jit(solution)/shard_map/psum | solution.py:761
  333.0 40.2 %all-to-all-start.2 = ((bf16[32,64,128]{2,1,0:T(8,128)(2,1)}), bf16[32,64,128]{2,1,0:T(8,128)(2,1)}, u32[]{:S(2)}, u32[]{:S(2)}) async-start(bf16[32,64,128]{2,1,0:T(8,128)(2,1)} %bitcast.144), calls=%async_computation.3 | async-start | bytes 1048576 | tf_op jit(solution)/shard_map/all_to_all | solution.py:702
  339.6 21.8 %collective-permute-start.7 = (bf16[256,1024]{1,0:T(8,128)(2,1)S(1)}, bf16[256,1024]{1,0:T(8,128)(2,1)}, u32[]{:S(2)}, u32[]{:S(2)}) collective-permute-start(bf16[256,1024]{1,0:T(8,128)(2,1)S(1)} %get-tuple-element.172), channel_id=1, source_target_pairs={{0,1},{1,2},{2,3},{3,0},{4,5},{5,6},{6,7},{7,4},{8,9},{9,10},{10,1... | collective-permute-start | bytes 1572872 | tf_op jit(solution)/shard_map/ppermute | solution.py:560
  341.4 102.0 %collective-permute-start.8 = (bf16[256,1024]{1,0:T(8,128)(2,1)}, bf16[256,1024]{1,0:T(8,128)(2,1)}, u32[]{:S(2)}, u32[]{:S(2)}) collective-permute-start(bf16[256,1024]{1,0:T(8,128)(2,1)} %get-tuple-element.171), channel_id=1, source_target_pairs={{0,2},{1,3},{2,0},{3,1},{4,6},{5,7},{6,4},{7,5},{8,10},{9,11},{10,... | collective-permute-start | bytes 1572872 | tf_op jit(solution)/shard_map/ppermute | solution.py:560
  343.8 99.5 %collective-permute-start.9 = (bf16[256,1024]{1,0:T(8,128)(2,1)}, bf16[256,1024]{1,0:T(8,128)(2,1)}, u32[]{:S(2)}, u32[]{:S(2)}) collective-permute-start(bf16[256,1024]{1,0:T(8,128)(2,1)} %get-tuple-element.170), channel_id=1, source_target_pairs={{0,3},{1,0},{2,1},{3,2},{4,7},{5,4},{6,5},{7,6},{8,11},{9,8},{10,9... | collective-permute-start | bytes 1572872 | tf_op jit(solution)/shard_map/ppermute | solution.py:560
  356.7 86.7 %collective-permute-start.4 = (bf16[256,1024]{1,0:T(8,128)(2,1)}, bf16[256,1024]{1,0:T(8,128)(2,1)S(1)}, u32[]{:S(2)}, u32[]{:S(2)}) collective-permute-start(bf16[256,1024]{1,0:T(8,128)(2,1)} %get-tuple-element.176), channel_id=1, source_target_pairs={{0,1},{1,2},{2,3},{3,0},{4,5},{5,6},{6,7},{7,4},{8,9},{9,10},{10,1... | collective-permute-start | bytes 1572872 | tf_op jit(solution)/shard_map/ppermute | solution.py:560
  357.2 86.2 %collective-permute-start.5 = (bf16[256,1024]{1,0:T(8,128)(2,1)}, bf16[256,1024]{1,0:T(8,128)(2,1)}, u32[]{:S(2)}, u32[]{:S(2)}) collective-permute-start(bf16[256,1024]{1,0:T(8,128)(2,1)} %get-tuple-element.175), channel_id=1, source_target_pairs={{0,2},{1,3},{2,0},{3,1},{4,6},{5,7},{6,4},{7,5},{8,10},{9,11},{10,... | collective-permute-start | bytes 1572872 | tf_op jit(solution)/shard_map/ppermute | solution.py:560
  361.4 82.0 %collective-permute-start.6 = (bf16[256,1024]{1,0:T(8,128)(2,1)}, bf16[256,1024]{1,0:T(8,128)(2,1)}, u32[]{:S(2)}, u32[]{:S(2)}) collective-permute-start(bf16[256,1024]{1,0:T(8,128)(2,1)} %get-tuple-element.174), channel_id=1, source_target_pairs={{0,3},{1,0},{2,1},{3,2},{4,7},{5,4},{6,5},{7,6},{8,11},{9,8},{10,9... | collective-permute-start | bytes 1572872 | tf_op jit(solution)/shard_map/ppermute | solution.py:560
  449.4 40.9 %all-to-all-start.3 = ((bf16[8,4,192,128]{3,2,1,0:T(8,128)(2,1)}), bf16[8,4,192,128]{3,2,1,0:T(8,128)(2,1)}, u32[]{:S(2)}, u32[]{:S(2)}) async-start(bf16[8,4,192,128]{3,2,1,0:T(8,128)(2,1)} %bitcast.128), calls=%async_computation.4 | async-start | bytes 3145728 | tf_op jit(solution)/shard_map/all_to_all | solution.py:669
  453.7 142.3 %reduce-scatter.5.cloned.1.call-start = ((), (), s32[]{:S(2)}) async-start(), calls=%async_computation.11 | async-start | bytes 2621440 | tf_op jit(solution)/shard_map/reduce_scatter | solution.py:822
  537.6 26.6 %collective-permute-start.17 = (bf16[128,1024]{1,0:T(8,128)(2,1)S(1)}, bf16[128,1024]{1,0:T(8,128)(2,1)}, u32[]{:S(2)}, u32[]{:S(2)}) collective-permute-start(bf16[128,1024]{1,0:T(8,128)(2,1)S(1)} %get-tuple-element.182), channel_id=1, source_target_pairs={{0,8},{4,12},{8,0},{12,4},{16,24},{20,28},{24,16},{28,20},{1,9},{5... | collective-permute-start | bytes 786440 | tf_op jit(solution)/shard_map/ppermute | solution.py:564
  537.9 26.3 %collective-permute-start.18 = (bf16[128,1024]{1,0:T(8,128)(2,1)S(1)}, bf16[128,1024]{1,0:T(8,128)(2,1)}, u32[]{:S(2)}, u32[]{:S(2)}) collective-permute-start(bf16[128,1024]{1,0:T(8,128)(2,1)S(1)} %get-tuple-element.184), channel_id=1, source_target_pairs={{0,16},{4,20},{8,24},{12,28},{16,0},{20,4},{24,8},{28,12},{1,17},{... | collective-permute-start | bytes 786440 | tf_op jit(solution)/shard_map/ppermute | solution.py:564
  539.4 24.9 %collective-permute-start.19 = (bf16[128,1024]{1,0:T(8,128)(2,1)S(1)}, bf16[128,1024]{1,0:T(8,128)(2,1)}, u32[]{:S(2)}, u32[]{:S(2)}) collective-permute-start(bf16[128,1024]{1,0:T(8,128)(2,1)S(1)} %get-tuple-element.183), channel_id=1, source_target_pairs={{0,24},{4,28},{8,16},{12,20},{16,8},{20,12},{24,0},{28,4},{1,25},{... | collective-permute-start | bytes 786440 | tf_op jit(solution)/shard_map/ppermute | solution.py:564
  567.5 16.3 %collective-permute-start.20 = (bf16[128,1024]{1,0:T(8,128)(2,1)}, bf16[128,1024]{1,0:T(8,128)(2,1)S(1)}, u32[]{:S(2)}, u32[]{:S(2)}) collective-permute-start(bf16[128,1024]{1,0:T(8,128)(2,1)} %get-tuple-element.157), channel_id=1, source_target_pairs={{0,8},{4,12},{8,0},{12,4},{16,24},{20,28},{24,16},{28,20},{1,9},{5... | collective-permute-start | bytes 786440 | tf_op jit(solution)/shard_map/ppermute | solution.py:564
  576.0 30.9 %collective-permute-start.26 = (bf16[2,704,1024]{2,1,0:T(8,128)(2,1)}, bf16[2,704,1024]{2,1,0:T(8,128)(2,1)}, u32[]{:S(2)}, u32[]{:S(2)}) collective-permute-start(bf16[2,704,1024]{2,1,0:T(8,128)(2,1)} %get-tuple-element.98), channel_id=1, source_target_pairs={{0,4},{4,0},{8,12},{12,8},{16,20},{20,16},{24,28},{28,24},{1,5},{5... | collective-permute-start | bytes 8650760 | tf_op jit(solution)/shard_map/ppermute | solution.py:564
  581.4 33.8 %collective-permute-start.25 = (bf16[2,704,1024]{2,1,0:T(8,128)(2,1)}, bf16[2,704,1024]{2,1,0:T(8,128)(2,1)}, u32[]{:S(2)}, u32[]{:S(2)}) collective-permute-start(bf16[2,704,1024]{2,1,0:T(8,128)(2,1)} %get-tuple-element.97), channel_id=1, source_target_pairs={{0,4},{4,0},{8,12},{12,8},{16,20},{20,16},{24,28},{28,24},{1,5},{5... | collective-permute-start | bytes 8650760 | tf_op jit(solution)/shard_map/ppermute | solution.py:564
  597.4 25.1 %collective-permute-start.24 = (bf16[2,704,1024]{2,1,0:T(8,128)(2,1)}, bf16[2,704,1024]{2,1,0:T(8,128)(2,1)}, u32[]{:S(2)}, u32[]{:S(2)}) collective-permute-start(bf16[2,704,1024]{2,1,0:T(8,128)(2,1)} %get-tuple-element.96), channel_id=1, source_target_pairs={{0,4},{4,0},{8,12},{12,8},{16,20},{20,16},{24,28},{28,24},{1,5},{5... | collective-permute-start | bytes 8650760 | tf_op jit(solution)/shard_map/ppermute | solution.py:564
  (56 other events, 500.7 us)
Sparse Core Ops, SparseCore 0:
  10.6 48.6 all-gather.4
  67.3 44.6 all-gather.6
  113.6 44.9 all-gather.10
  189.2 45.3 all-gather.8
  276.6 42.5 reduce-scatter.2
  324.6 196.2 all-reduce.8
  523.8 46.0 reduce-scatter.4

commit v3 on v2

v3 whole, which is shorter than its diff:
```python
import functools

import jax
import jax.numpy as jnp
from jax import lax
from jax.experimental import pallas as pl
from jax.experimental.pallas import tpu as pltpu
from jax.sharding import PartitionSpec as P

DH = 64
BLOCK = 128


EPS = 1e-06
NEG = -1e30
HIGH = lax.Precision.HIGHEST


LOG2E = 1.4426950408889634
KT = 512
GROUPS = 2
BACK_COST = 2
VMEM_LIMIT = 56 * 1024 * 1024


def dot(left, right):
    return jnp.dot(left, right, preferred_element_type=jnp.float32)


def place_pairs(nat_ref, part_refs, k_row, count, keys_flat, keys_tall):
    keys_flat[:, :BLOCK] = jnp.zeros((2 * DH, BLOCK), keys_flat.dtype)
    keys_tall[:BLOCK, :] = jnp.zeros((BLOCK, 2 * DH), keys_tall.dtype)
    for part, ref in enumerate(part_refs):
        row = k_row if part == 0 else 0

        def one(index, _, part=part, ref=ref, row=row):
            at = pl.multiple_of((nat_ref[part * count + index] + 1) * BLOCK, BLOCK)
            pair = ref[index, row : row + 2 * DH, :]
            keys_flat[:, pl.ds(at, BLOCK)] = pair
            keys_tall[pl.ds(at, BLOCK), :] = pair.T
            return 0

        lax.fori_loop(0, count, one, 0, unroll=8)


def fill_near_bias(thr_ref, tab_ref, near_bias, bucket_count):
    key_ids = lax.broadcasted_iota(jnp.int32, (2 * BLOCK, BLOCK), 0)
    query_ids = lax.broadcasted_iota(jnp.int32, (2 * BLOCK, BLOCK), 1)
    distance = query_ids + BLOCK - key_ids
    value = jnp.full((2 * BLOCK, BLOCK), tab_ref[0], jnp.float32)
    for bucket in range(1, bucket_count):
        value = jnp.where(distance >= thr_ref[bucket], tab_ref[bucket], value)
    near_bias[...] = jnp.where(distance >= 0, value, NEG)


def lane_pair(first, second):
    return jnp.concatenate([first, second], axis=1)


def tile_group(nat_ref, order_ref, low_ref, high_ref, index):
    slots = (order_ref[2 * index], order_ref[2 * index + 1])
    blocks = (nat_ref[slots[0]], nat_ref[slots[1]])
    lane = lax.broadcasted_iota(jnp.int32, (1, 2 * BLOCK), 1)
    stop = jnp.where(lane < BLOCK, (blocks[0] - 1) * BLOCK, (blocks[1] - 1) * BLOCK)
    first = low_ref[blocks[0]] * BLOCK
    steps = (jnp.maximum((blocks[1] - 1) * BLOCK - first, 0) + KT - 1) // KT
    return slots, blocks, stop, first, steps, high_ref[blocks[1]], (blocks[0] - 1) * BLOCK


def far_place(group, step, total):
    begin = group[3] + step * KT
    at = jnp.minimum(begin, total - KT)
    return begin, at, pl.multiple_of(at + BLOCK, BLOCK)


def all_inside(groups, step):
    inside = True
    for group in groups:
        begin = group[3] + step * KT
        inside = inside & (begin >= group[5]) & (begin + KT <= group[6])
    return inside


def far_valid(far_ids, group, start, begin, at):
    return (far_ids >= jnp.maximum(start, begin) - at) & (far_ids < group[2] - at)


def forward_kernel(
    bucket_count,
    parts,
    nat_ref,
    order_ref,
    low_ref,
    high_ref,
    thr_ref,
    tab_ref,
    seq_ref,
    *rest,
):
    part_refs = rest[:parts]
    out_ref, full_ref, lse_ref = rest[parts : parts + 3]
    keys_flat, keys_tall, near_bias = rest[parts + 3 :]
    own_ref = part_refs[0]
    count = own_ref.shape[0]
    total = keys_tall.shape[0] - BLOCK
    scale = DH ** (-0.5) * LOG2E
    bf16 = jnp.bfloat16
    place_pairs(nat_ref, part_refs, DH, count, keys_flat, keys_tall)
    fill_near_bias(thr_ref, tab_ref, near_bias, bucket_count)
    near_ids = lax.broadcasted_iota(jnp.int32, (2 * BLOCK, BLOCK), 0)
    far_ids = lax.broadcasted_iota(jnp.int32, (KT, 2 * BLOCK), 0)

    def one_tile(tile, _):
        groups = [
            tile_group(nat_ref, order_ref, low_ref, high_ref, GROUPS * tile + index)
            for index in range(GROUPS)
        ]
        queries, starts, init = [], [], []
        for slots, blocks, *_ in groups:
            q_pair = lane_pair(own_ref[slots[0], :DH, :], own_ref[slots[1], :DH, :])
            q_wide = jnp.concatenate([q_pair, jnp.zeros_like(q_pair)], axis=0)
            sides = []
            for half, blk in enumerate(blocks):
                at = pl.multiple_of(blk * BLOCK, BLOCK)
                start = seq_ref[pl.ds(blk, 1), :]
                s = dot(
                    keys_tall[pl.ds(at, 2 * BLOCK), :],
                    q_wide[:, half * BLOCK : (half + 1) * BLOCK],
                )
                s = s * scale + near_bias[...]
                s = jnp.where(near_ids >= start - (blk - 1) * BLOCK, s, NEG)
                top = jnp.max(s, axis=0, keepdims=True)
                p = jnp.exp2(s - top)
                acc = dot(keys_flat[DH:, pl.ds(at, 2 * BLOCK)], p.astype(bf16))
                sides.append((start, top, jnp.sum(p, axis=0, keepdims=True), acc))
            start, *stats = [lane_pair(x, y) for x, y in zip(*sides)]
            queries.append(q_wide)
            starts.append(start)
            init.append(tuple(stats))

        def update(step, carry, masked):
            places = [far_place(group, step, total) for group in groups]
            scores = [
                dot(keys_tall[pl.ds(here, KT), :], q_wide)
                for (_, _, here), q_wide in zip(places, queries)
            ]
            middle = []
            for index, (top, norm, acc) in enumerate(carry):
                begin, at, here = places[index]
                s = scores[index] * scale
                if masked:
                    valid = far_valid(far_ids, groups[index], starts[index], begin, at)
                    s = jnp.where(valid, s, NEG)
                new_top = jnp.maximum(top, jnp.max(s, axis=0, keepdims=True))
                p = jnp.exp2(s - new_top)
                factor = jnp.exp2(top - new_top)
                norm = norm * factor + jnp.sum(p, axis=0, keepdims=True)
                middle.append((new_top, norm, acc * factor, p.astype(bf16)))
            return tuple(
                (top, norm, acc + dot(keys_flat[DH:, pl.ds(here, KT)], p))
                for (top, norm, acc, p), (_, _, here) in zip(middle, places)
            )

        def far(step, carry):
            return lax.cond(
                all_inside(groups, step),
                lambda inner: update(step, inner, False),
                lambda inner: update(step, inner, True),
                carry,
            )

        steps = functools.reduce(jnp.maximum, [group[4] for group in groups])
        final = lax.fori_loop(0, steps, far, tuple(init))
        for (slots, *_), (top, norm, acc) in zip(groups, final):
            result = acc / norm
            lse = top + jnp.log(norm) * LOG2E
            for half, slot in enumerate(slots):
                part = result[:, half * BLOCK : (half + 1) * BLOCK]
                full_ref[pl.ds(slot, 1)] = part[None]
                out_ref[pl.ds(slot, 1)] = part.astype(bf16)[None]
                lse_ref[pl.ds(slot, 1), :] = lse[:, half * BLOCK : (half + 1) * BLOCK]
        return 0

    lax.fori_loop(0, count // (2 * GROUPS), one_tile, 0)


def backward_kernel(
    bucket_count,
    parts,
    nat_ref,
    order_ref,
    low_ref,
    high_ref,
    thr_ref,
    tab_ref,
    seq_ref,
    *rest,
):
    part_refs = rest[:parts]
    dout_ref, full_ref, lse_ref = rest[parts : parts + 3]
    dq_ref = rest[parts + 3]
    dkv_refs = rest[parts + 4 : 2 * parts + 4]
    table_ref = rest[2 * parts + 4]
    keys_flat, keys_tall, near_bias, grads, near_grads = rest[2 * parts + 5 :]
    own_ref = part_refs[0]
    count = own_ref.shape[0]
    total = keys_tall.shape[0] - BLOCK
    scale = DH ** (-0.5) * LOG2E
    bf16 = jnp.bfloat16
    f32 = jnp.float32
    place_pairs(nat_ref, part_refs, DH, count, keys_flat, keys_tall)
    fill_near_bias(thr_ref, tab_ref, near_bias, bucket_count)
    grads[...] = jnp.zeros_like(grads)
    near_grads[...] = jnp.zeros_like(near_grads)
    near_ids = lax.broadcasted_iota(jnp.int32, (2 * BLOCK, BLOCK), 0)
    far_ids = lax.broadcasted_iota(jnp.int32, (KT, 2 * BLOCK), 0)
    low_lane = lax.broadcasted_iota(jnp.int32, (BLOCK, 2 * DH), 1) < DH

    def one_tile(tile, _):
        groups = [
            tile_group(nat_ref, order_ref, low_ref, high_ref, GROUPS * tile + index)
            for index in range(GROUPS)
        ]
        fixed, init = [], []
        for slots, blocks, *_ in groups:
            sides = []
            for slot, blk in zip(slots, blocks):
                at = pl.multiple_of(blk * BLOCK, BLOCK)
                start = seq_ref[pl.ds(blk, 1), :]
                q_t = own_ref[slot, :DH, :]
                do_t = dout_ref[slot]
                lse = lse_ref[pl.ds(slot, 1), :]
                dsum = jnp.sum(do_t.astype(f32) * full_ref[slot], axis=0, keepdims=True)
                zero = jnp.zeros_like(q_t)
                q_wide = jnp.concatenate([q_t, zero], axis=0)
                do_wide = jnp.concatenate([zero, do_t], axis=0)
                both = jnp.concatenate([q_t, do_t], axis=0).T
                none = jnp.zeros_like(both)
                q_side = jnp.where(low_lane, both, none)
                out_side = jnp.where(low_lane, none, both)
                s_dp = dot(keys_tall[pl.ds(at, 2 * BLOCK), :], lane_pair(q_wide, do_wide))
                s = s_dp[:, :BLOCK] * scale + near_bias[...]
                s = jnp.where(near_ids >= start - (blk - 1) * BLOCK, s, NEG)
                p = jnp.exp2(s - lse)
                ds = (p * (s_dp[:, BLOCK:] - dsum)).astype(bf16)
                grads[pl.ds(at, 2 * BLOCK), :] += dot(
                    lane_pair(p.astype(bf16), ds),
                    jnp.concatenate([out_side, q_side], axis=0),
                )
                near_grads[...] += ds.astype(f32)
                dq = dot(keys_flat[:DH, pl.ds(at, 2 * BLOCK)], ds)
                sides.append((start, lse, dsum, q_wide, do_wide, dq, out_side, q_side))
            wide = [lane_pair(x, y) for x, y in zip(*[side[:6] for side in sides])]
            start, lse, dsum, q_wide, do_wide, dq = wide
            right = lane_pair(q_wide, do_wide)
            tall = jnp.concatenate(
                [sides[0][6], sides[1][6], sides[0][7], sides[1][7]], axis=0
            )
            fixed.append((start, lse, dsum, right, tall))
            init.append(dq)

        def update(step, carry, masked):
            places = [far_place(group, step, total) for group in groups]
            products = [
                dot(keys_tall[pl.ds(here, KT), :], right)
                for (_, _, here), (_, _, _, right, _) in zip(places, fixed)
            ]
            middle = []
            for index, (start, lse, dsum, _, _) in enumerate(fixed):
                begin, at, _ = places[index]
                s = products[index][:, : 2 * BLOCK] * scale
                if masked:
                    valid = far_valid(far_ids, groups[index], start, begin, at)
                    s = jnp.where(valid, s, NEG)
                p = jnp.exp2(s - lse)
                ds = (p * (products[index][:, 2 * BLOCK :] - dsum)).astype(bf16)
                middle.append((p.astype(bf16), ds))
            result = []
            for (p, ds), (_, _, here), (*_, tall), dq in zip(middle, places, fixed, carry):
                grads[pl.ds(here, KT), :] += dot(lane_pair(p, ds), tall)
                result.append(dq + dot(keys_flat[:DH, pl.ds(here, KT)], ds))
            return tuple(result)

        def far(step, carry):
            return lax.cond(
                all_inside(groups, step),
                lambda inner: update(step, inner, False),
                lambda inner: update(step, inner, True),
                carry,
            )

        steps = functools.reduce(jnp.maximum, [group[4] for group in groups])
        final = lax.fori_loop(0, steps, far, tuple(init))
        for (slots, *_), dq in zip(groups, final):
            dq = dq * DH ** (-0.5)
            for half, slot in enumerate(slots):
                part = dq[:, half * BLOCK : (half + 1) * BLOCK]
                dq_ref[pl.ds(slot, 1)] = part.astype(bf16)[None]
        return 0

    lax.fori_loop(0, count // (2 * GROUPS), one_tile, 0)
    key_lane = jnp.where(low_lane, DH ** (-0.5), 1.0)
    for part in range(parts):

        def give(index, _, part=part):
            at = pl.multiple_of((nat_ref[part * count + index] + 1) * BLOCK, BLOCK)
            block = grads[pl.ds(at, BLOCK), :] * key_lane
            dkv_refs[part][pl.ds(index, 1)] = block.T.astype(bf16)[None]
            return 0

        lax.fori_loop(0, count, give, 0, unroll=8)
    key_ids = lax.broadcasted_iota(jnp.int32, (2 * BLOCK, BLOCK), 0)
    query_ids = lax.broadcasted_iota(jnp.int32, (2 * BLOCK, BLOCK), 1)
    distance = query_ids + BLOCK - key_ids
    near = near_grads[...]
    out_lane = lax.broadcasted_iota(jnp.int32, (1, BLOCK), 1)
    above = jnp.sum(near, axis=(0, 1), keepdims=True)
    result = jnp.zeros((1, BLOCK), f32)
    seen = jnp.zeros((1, 1), f32)
    for bucket in range(1, bucket_count):
        kept = jnp.sum(
            jnp.where(distance >= thr_ref[bucket], near, 0.0), axis=(0, 1), keepdims=True
        )
        result = jnp.where(out_lane == bucket - 1, above - kept, result)
        seen = seen + (above - kept)
        above = kept
    table_ref[...] = jnp.where(out_lane == bucket_count - 1, -seen, result)


def attention_call(kernel, parts, bucket_count, scalars, seq_start, arrays, out_shape, total, extra, cost):
    smem = pl.BlockSpec(memory_space=pltpu.SMEM)
    team_size = parts
    vmem = pl.BlockSpec(memory_space=pltpu.VMEM)
    operands = list(scalars) + [seq_start] + list(arrays)
    scratch = [
        pltpu.VMEM((2 * DH, total + BLOCK), jnp.bfloat16),
        pltpu.VMEM((total + BLOCK, 2 * DH), jnp.bfloat16),
        pltpu.VMEM((2 * BLOCK, BLOCK), jnp.float32),
    ] + extra
    return pl.pallas_call(
        functools.partial(kernel, bucket_count, parts),
        out_shape=out_shape,
        in_specs=[smem] * len(scalars) + [vmem] * (1 + len(arrays)),
        out_specs=[vmem] * len(out_shape),
        scratch_shapes=scratch,
        compiler_params=pltpu.CompilerParams(vmem_limit_bytes=VMEM_LIMIT),
        cost_estimate=pl.CostEstimate(
            flops=total * total * DH * cost,
            bytes_accessed=total * DH * 50 * cost,
            transcendentals=0,
        ),
    )(*operands)


def turn_halves(x, axis, amounts, sign):
    halves = x.shape[axis + 1]
    shape = [1] * x.ndim
    shape[axis] = x.shape[axis]
    amounts = amounts.reshape(shape)
    result = x
    for step in range(1, halves):
        result = jnp.where(amounts == step, jnp.roll(x, -sign * step, axis=axis + 1), result)
    return result


GELU_A = 0.7978845608028654
GELU_B = 0.044715
ROWS = 512


def dot_nt(left, right):
    return lax.dot_general(
        left, right, (((1,), (1,)), ((), ())), preferred_element_type=jnp.float32
    )


def dot_tn(left, right):
    return lax.dot_general(
        left, right, (((0,), (0,)), ((), ())), preferred_element_type=jnp.float32
    )


def lane_of(column, shape):
    return lax.broadcasted_iota(jnp.int32, shape, 1) == column


def project_kernel(turn_ref, h_ref, query_ref, key_ref, value_ref, out_ref):
    heads, team = out_ref.shape[:2]
    turn = turn_ref[pl.program_id(0)]
    h = h_ref[...]
    for kind, weight in enumerate((query_ref, key_ref, value_ref)):
        flat = dot(h, weight[...]).T.astype(out_ref.dtype)
        rows = slice(kind * DH, (kind + 1) * DH)
        for half in range(team):
            member = lax.rem(half - turn + team, team)
            columns = flat[:, half * BLOCK : (half + 1) * BLOCK]
            for head in range(heads):
                block = columns[head * DH : (head + 1) * DH]
                out_ref[head, pl.ds(member, 1), 0, rows, :] = block[None]


def project(turn, h_all, weights, heads, team):
    rows, width = h_all.shape
    pairs = rows // (team * BLOCK)
    local = weights[0].shape[1]
    weight = pl.BlockSpec((width, local), lambda m, turn: (0, 0))
    return pl.pallas_call(
        project_kernel,
        out_shape=jax.ShapeDtypeStruct((heads, team, pairs, 3 * DH, BLOCK), jnp.bfloat16),
        grid_spec=pltpu.PrefetchScalarGridSpec(
            num_scalar_prefetch=1,
            grid=(pairs,),
            in_specs=[pl.BlockSpec((team * BLOCK, width), lambda m, turn: (m, 0))]
            + [weight] * 3,
            out_specs=pl.BlockSpec(
                (heads, team, 1, 3 * DH, BLOCK), lambda m, turn: (0, 0, m, 0, 0)
            ),
        ),
        compiler_params=pltpu.CompilerParams(vmem_limit_bytes=VMEM_LIMIT),
        cost_estimate=pl.CostEstimate(
            flops=6 * rows * width * local,
            bytes_accessed=2 * rows * (width + 3 * local) + 6 * width * local,
            transcendentals=0,
        ),
    )(turn, h_all, *weights)


def unproject_kernel(
    turn_ref,
    got_ref,
    h_ref,
    query_ref,
    key_ref,
    value_ref,
    out_ref,
    small_ref,
    gain_ref,
    dh_ref,
    wide_ref,
    total,
):
    heads, team = got_ref.shape[:2]
    local = query_ref.shape[1]
    step = pl.program_id(0)
    turn = turn_ref[step]
    h = h_ref[...]

    @pl.when(step == 0)
    def _():
        total[...] = jnp.zeros_like(total)

    dh = jnp.zeros(dh_ref.shape, jnp.float32)
    for kind, weight in enumerate((query_ref, key_ref, value_ref)):
        halves = []
        for half in range(team):
            member = lax.rem(half - turn + team, team)
            blocks = [
                got_ref[head, pl.ds(member, 1), 0, kind * DH : (kind + 1) * DH, :][0]
                for head in range(heads)
            ]
            halves.append(jnp.concatenate(blocks, axis=0))
        flat = jnp.concatenate(halves, axis=1)
        dh = dh + dot_nt(flat.T, weight[...])
        total[kind * local : (kind + 1) * local, :] += dot(flat, h)
    dh_ref[...] = dh.astype(dh_ref.dtype)

    @pl.when(step == pl.num_programs(0) - 1)
    def _():
        gain = jnp.zeros(gain_ref.shape, jnp.float32)
        for kind, weight in enumerate((query_ref, key_ref, value_ref)):
            rows = slice(kind * local, (kind + 1) * local)
            part = total[rows, :]
            wide_ref[rows, :] = part.astype(wide_ref.dtype)
            tall = weight[...].T.astype(jnp.float32)
            gain = gain + jnp.sum(part * tall, axis=0, keepdims=True)
        wide_ref[3 * local : 4 * local, :] = out_ref[...]
        row_ids = lax.broadcasted_iota(jnp.int32, small_ref.shape, 0)
        small = jnp.where(row_ids == 0, gain / gain_ref[...], small_ref[...])
        wide_ref[4 * local :, :] = small.astype(wide_ref.dtype)


def unproject(turn, got, h_all, weights, grad_out, small, gain):
    heads, team, pairs = got.shape[:3]
    rows, width = h_all.shape
    local = weights[0].shape[1]
    wide_rows = 4 * local + small.shape[0]
    block = pl.BlockSpec((team * BLOCK, width), lambda m, turn: (m, 0))
    whole = lambda m, turn: (0, 0)
    return pl.pallas_call(
        unproject_kernel,
        out_shape=[
            jax.ShapeDtypeStruct((rows, width), jnp.bfloat16),
            jax.ShapeDtypeStruct((wide_rows, width), jnp.bfloat16),
        ],
        grid_spec=pltpu.PrefetchScalarGridSpec(
            num_scalar_prefetch=1,
            grid=(pairs,),
            in_specs=[
                pl.BlockSpec(
                    (heads, team, 1, 3 * DH, BLOCK), lambda m, turn: (0, 0, m, 0, 0)
                ),
                block,
            ]
            + [pl.BlockSpec((width, local), whole)] * 3
            + [
                pl.BlockSpec((local, width), whole),
                pl.BlockSpec(small.shape, whole),
                pl.BlockSpec((1, width), whole),
            ],
            out_specs=[block, pl.BlockSpec((wide_rows, width), whole)],
            scratch_shapes=[pltpu.VMEM((3 * local, width), jnp.float32)],
        ),
        compiler_params=pltpu.CompilerParams(vmem_limit_bytes=VMEM_LIMIT),
        cost_estimate=pl.CostEstimate(
            flops=12 * rows * width * local,
            bytes_accessed=2 * rows * (2 * width + 3 * local) + 12 * width * local,
            transcendentals=0,
        ),
    )(turn, got, h_all, *weights, grad_out, small, gain)


def place_kernel(count, first_ref, *refs):
    for source, target in zip(refs[:count], refs[-count:]):
        target[...] = source[...].astype(target.dtype)


def place_half(first, halves, targets):
    some, units, width = halves[0].shape
    count = len(halves)
    source = pl.BlockSpec((1, units, width), lambda e, first: (e, 0, 0))
    target = pl.BlockSpec((1, units, width), lambda e, first: (first[0] + e, 0, 0))
    passed = [pl.BlockSpec(memory_space=pl.ANY)] * len(targets)
    return pl.pallas_call(
        functools.partial(place_kernel, count),
        out_shape=[jax.ShapeDtypeStruct((2 * some, units, width), jnp.float32)] * count,
        grid_spec=pltpu.PrefetchScalarGridSpec(
            num_scalar_prefetch=1,
            grid=(some,),
            in_specs=[source] * count + passed,
            out_specs=[target] * count,
        ),
        input_output_aliases={1 + count + at: at for at in range(len(targets))},
        compiler_params=pltpu.CompilerParams(vmem_limit_bytes=VMEM_LIMIT),
        cost_estimate=pl.CostEstimate(
            flops=0, bytes_accessed=6 * count * halves[0].size, transcendentals=0
        ),
    )(first, *halves, *targets)


def pad_units(weight, axis):
    extra = -weight.shape[axis] % (2 * BLOCK)
    pads = [(0, 0)] * weight.ndim
    pads[axis] = (0, extra)
    return jnp.pad(weight, pads)


def expert_kernel(
    experts,
    h_ref,
    router_ref,
    keep_ref,
    gate_ref,
    up_ref,
    back_ref,
    *rest,
):
    dh_ref, hidden_ref, dgate_ref, dup_ref, drouter_ref, total, gates, dots = rest[-8:]
    expert = pl.program_id(0)
    rows = slice(0, ROWS)
    f32 = jnp.float32
    bf16 = jnp.bfloat16
    lanes = (ROWS, router_ref.shape[1])
    h = h_ref[rows, :]

    @pl.when(expert == 0)
    def _():
        logits = dot(h, router_ref[...])
        real = lax.broadcasted_iota(jnp.int32, lanes, 1) < experts
        logits = jnp.where(real, logits, NEG)
        expo = jnp.exp(logits - jnp.max(logits, axis=1, keepdims=True))
        gates[rows, :] = expo / jnp.sum(expo, axis=1, keepdims=True)
        dots[rows, :] = jnp.zeros(lanes, f32)

    here = lane_of(expert, lanes)
    weight = jnp.sum(
        jnp.where(here, gates[rows, :] * keep_ref[rows, :], 0.0), axis=1, keepdims=True
    )
    g = dot_nt(h, gate_ref[0])
    u = dot_nt(h, up_ref[0])
    c = back_ref[0]
    square = g * g
    th = jnp.tanh(GELU_A * g * (1.0 + GELU_B * square))
    cdf = 0.5 + 0.5 * th
    gelu = g * cdf
    slope = cdf + (0.5 * GELU_A) * g * (1.0 - th * th) * (1.0 + 3.0 * GELU_B * square)
    hidden = (gelu * u).astype(bf16).astype(f32)
    hidden_ref[0] = (hidden * weight).astype(bf16)
    dots[rows, :] = jnp.where(here, jnp.sum(hidden * c, axis=1, keepdims=True), dots[rows, :])
    dc = c * weight
    dup = (dc * gelu).astype(bf16)
    dgate = (dc * u * slope).astype(bf16)
    dup_ref[0] = dup
    dgate_ref[0] = dgate
    part = dot(dgate, gate_ref[0]) + dot(dup, up_ref[0])

    @pl.when(expert == 0)
    def _():
        total[rows, :] = part

    @pl.when((expert > 0) & (expert < experts - 1))
    def _():
        total[rows, :] += part

    @pl.when(expert == experts - 1)
    def _():
        probs = gates[rows, :]
        dg = dots[rows, :] * keep_ref[rows, :]
        dl = probs * (dg - jnp.sum(probs * dg, axis=1, keepdims=True))
        high = dl.astype(bf16)
        low = (dl - high.astype(f32)).astype(bf16)
        drouter = dot_tn(high, h) + dot_tn(low, h)
        drouter_ref[...] = drouter[: drouter_ref.shape[0]]
        extra = dot_nt(high, router_ref[...]) + dot_nt(low, router_ref[...])
        dh_ref[rows, :] = (total[rows, :] + part + extra).astype(bf16)


def expert_layer(part, h_part, router_wide, keep_wide, w_gate, w_up, back, filled):
    experts, units, width = w_gate.shape
    rows = back.shape[1]
    lanes = router_wide.shape[1]
    f32 = jnp.float32
    bf16 = jnp.bfloat16
    whole = lambda e: (0, 0)
    weights = pl.BlockSpec((1, units, width), lambda e: (e, 0, 0))
    tile = pl.BlockSpec((1, ROWS, units), lambda e: (e, part, 0))
    wide = jax.ShapeDtypeStruct((experts, rows, units), bf16)
    return pl.pallas_call(
        functools.partial(expert_kernel, experts),
        out_shape=[
            jax.ShapeDtypeStruct((ROWS, width), bf16),
            wide,
            wide,
            wide,
            jax.ShapeDtypeStruct((8, width), f32),
        ],
        grid=(experts,),
        in_specs=[
            pl.BlockSpec((ROWS, width), whole),
            pl.BlockSpec((width, lanes), whole),
            pl.BlockSpec((ROWS, lanes), lambda e: (part, 0)),
            weights,
            weights,
            tile,
        ]
        + [pl.BlockSpec(memory_space=pl.ANY)] * len(filled),
        out_specs=[
            pl.BlockSpec((ROWS, width), whole),
            tile,
            tile,
            tile,
            pl.BlockSpec((8, width), whole),
        ],
        scratch_shapes=[
            pltpu.VMEM((ROWS, width), f32),
            pltpu.VMEM((ROWS, lanes), f32),
            pltpu.VMEM((ROWS, lanes), f32),
        ],
        input_output_aliases={6 + at: 1 + at for at in range(len(filled))},
        compiler_params=pltpu.CompilerParams(vmem_limit_bytes=VMEM_LIMIT),
        cost_estimate=pl.CostEstimate(
            flops=8 * experts * ROWS * units * width,
            bytes_accessed=experts * units * (4 * width + 10 * ROWS) + 4 * ROWS * width,
            transcendentals=experts * ROWS * units,
        ),
    )(h_part, router_wide, keep_wide, w_gate, w_up, back, *filled)


def weight_grads_kernel(first_ref, left_ref, low_ref, high_ref, *rest):
    out = rest[-1]
    left = left_ref[0]
    part = dot_tn(left[:ROWS], low_ref[...]) + dot_tn(left[ROWS:], high_ref[...])
    part = part[: out.shape[1]]
    if len(rest) > 1:
        part = part + rest[0][0].astype(jnp.float32)
    out[0] = part.astype(out.dtype)


def weight_grads(first, count, real, left, rights, arrived):
    _, rows, units = left.shape
    width = rights[0].shape[1]
    parts = [
        pl.BlockSpec((ROWS, width), lambda e, first, at=at: (at, 0))
        for at in ((0, 0) if rights[0].shape[0] == ROWS else (0, 1))
    ]
    out = pl.BlockSpec((1, real, width), lambda e, first: (e, 0, 0))
    return pl.pallas_call(
        weight_grads_kernel,
        out_shape=jax.ShapeDtypeStruct((count, real, width), jnp.bfloat16),
        grid_spec=pltpu.PrefetchScalarGridSpec(
            num_scalar_prefetch=1,
            grid=(count,),
            in_specs=[pl.BlockSpec((1, rows, units), lambda e, first: (first[0] + e, 0, 0))]
            + parts
            + [out] * len(arrived),
            out_specs=out,
        ),
        compiler_params=pltpu.CompilerParams(vmem_limit_bytes=VMEM_LIMIT),
        cost_estimate=pl.CostEstimate(
            flops=count * rows * units * width // 4,
            bytes_accessed=rows * width,
            transcendentals=0,
        ),
    )(first, left, *rights, *arrived)


def kept_choices(group_routes, experts, capacity):
    count, top_count = group_routes.shape
    flat = group_routes.T.reshape(-1)
    hot = (flat[:, None] == jnp.arange(experts, dtype=jnp.int32)[None, :]).astype(jnp.int32)
    earlier = jnp.cumsum(hot, axis=0) - hot
    kept = jnp.where(earlier < capacity, hot, 0)
    return jnp.sum(kept.reshape(top_count, count, experts), axis=0).astype(jnp.float32)


def on_device(
    layer_in,
    gain_one,
    w_query,
    w_key,
    w_value,
    w_out,
    bias_table,
    gain_two,
    w_router,
    w_gate,
    w_up,
    w_down,
    lengths,
    block_perm,
    buckets,
    routes,
    cotangent,
):
    tp_count = lax.axis_size("tp")
    ctx_count = lax.axis_size("ctx")
    tp_index = lax.axis_index("tp")
    ctx_index = lax.axis_index("ctx")
    rows_dev = layer_in.shape[0]
    width = layer_in.shape[1]
    group_rows = rows_dev * tp_count
    width_loc = w_query.shape[1]
    head_count = width_loc // DH
    blocks_group = group_rows // BLOCK
    experts = w_gate.shape[0]
    top_count = routes.shape[1]
    capacity = 5 * top_count * group_rows // (4 * experts)
    units = w_gate.shape[2]
    core = ctx_index % 2
    bucket_count = bias_table.shape[0]
    f32 = jnp.float32
    bf16 = jnp.bfloat16
    x_float = layer_in.astype(f32)
    inv_one = lax.rsqrt(jnp.mean(x_float * x_float, axis=1, keepdims=True) + EPS)
    normed_one = x_float * inv_one
    h_one = (normed_one * gain_one).astype(bf16)
    h_one_all = lax.all_gather(h_one, "tp", axis=0, tiled=True)
    gate_wide = pad_units(jnp.swapaxes(w_gate, 1, 2), 1)
    up_wide = pad_units(jnp.swapaxes(w_up, 1, 2), 1)
    down_wide = pad_units(w_down, 1)
    h_one_all, w_out_own, cotangent_own, gate_wide, up_wide, down_wide = (
        lax.optimization_barrier(
            (h_one_all, w_out, cotangent, gate_wide, up_wide, down_wide)
        )
    )

    def turned(x, axis, step):
        size = lax.axis_size(axis)
        return lax.ppermute(x, axis, [(at, (at + step) % size) for at in range(size)])

    def crossed(x, axis, bits):
        size = lax.axis_size(axis)
        return lax.ppermute(x, axis, [(at, at ^ bits) for at in range(size)])

    def tp_scatter(x):
        chunks = x.reshape((tp_count, x.shape[0] // tp_count) + x.shape[1:])
        pieces = [lax.dynamic_index_in_dim(chunks, tp_index, 0, False)]
        for step in range(1, tp_count):
            chunk = lax.dynamic_index_in_dim(chunks, (tp_index + step) % tp_count, 0, False)
            pieces.append(turned(chunk, "tp", step))
        return pieces

    def summed(pieces):
        total = pieces[0].astype(f32)
        for piece in pieces[1:]:
            total = total + piece.astype(f32)
        return total

    chips = ctx_count // 2
    chip = ctx_index // 2

    def core_scatter(x):
        half = x.shape[0] // 2
        away = lax.dynamic_slice_in_dim(x, (1 - core) * half, half, 0)
        mine = lax.dynamic_slice_in_dim(x, core * half, half, 0)
        return (mine.astype(f32) + crossed(away, "ctx", 1).astype(f32)).astype(bf16)

    def chip_scatter(x):
        chunks = x.reshape((chips, x.shape[0] // chips) + x.shape[1:])
        total = lax.dynamic_index_in_dim(chunks, chip, 0, False).astype(f32)
        for bits in range(1, chips):
            chunk = lax.dynamic_index_in_dim(chunks, chip ^ bits, 0, False)
            total = total + crossed(chunk, "ctx", 2 * bits).astype(f32)
        return total.astype(bf16)

    def chip_gather(x):
        result = jnp.zeros((chips,) + x.shape, x.dtype)
        result = lax.dynamic_update_index_in_dim(result, x, chip, 0)
        for bits in range(1, chips):
            got = crossed(x, "ctx", 2 * bits)
            result = lax.dynamic_update_index_in_dim(result, got, chip ^ bits, 0)
        return result.reshape((chips * x.shape[0],) + x.shape[1:])

    w_out_all = lax.all_gather(w_out_own, "tp", axis=0, tiled=True)
    half_rows = rows_dev // 2

    def by_half(x):
        split = x.reshape((tp_count, 2, half_rows) + x.shape[1:])
        return jnp.swapaxes(split, 0, 1).reshape(x.shape)

    def by_device(x):
        split = x.reshape((2, tp_count, half_rows) + x.shape[1:])
        return jnp.swapaxes(split, 0, 1).reshape(x.shape)

    grad_all = by_half(lax.all_gather(cotangent_own, "tp", axis=0, tiled=True))
    team = ctx_count // head_count
    member = ctx_index % team
    my_head = ctx_index // team
    pair_count = blocks_group // team
    slot_blocks = ctx_count * pair_count
    total = ctx_count * group_rows
    pair_ids_m = jnp.arange(pair_count, dtype=jnp.int32)
    turn = (ctx_index + pair_ids_m) % team
    ends = jnp.cumsum(lengths)
    begins = ends - lengths
    places = jnp.arange(total, dtype=jnp.int32)
    seq_start = jnp.max(
        jnp.where(begins[None, :] <= places[:, None], begins[None, :], 0), axis=1
    ).reshape(total // BLOCK, BLOCK)
    low_block = seq_start[:, 0] // BLOCK
    high_start = seq_start[:, BLOCK - 1]
    thresholds = jnp.sum(
        (buckets[None, :] < jnp.arange(bucket_count, dtype=jnp.int32)[:, None]).astype(jnp.int32),
        axis=1,
    )
    head_hot = (jnp.arange(head_count, dtype=jnp.int32) == my_head).astype(f32)
    my_table = jnp.sum(bias_table * head_hot[None, :], axis=1)
    near_table = (my_table - my_table[bucket_count - 1]) * LOG2E
    sources = jnp.arange(ctx_count, dtype=jnp.int32)
    members = (member + jnp.arange(team, dtype=jnp.int32)) % team
    half_of = (members[:, None, None] + sources[None, :, None] + pair_ids_m[None, None, :]) % team
    perm_pairs = block_perm.reshape(1, ctx_count, pair_count, team)
    natural = jnp.sum(
        jnp.where(
            half_of[..., None] == jnp.arange(team, dtype=jnp.int32)[None, None, None, :],
            perm_pairs,
            0,
        ),
        axis=3,
    ).reshape(-1)
    own_natural = natural[:slot_blocks]
    rank = jnp.sum((own_natural[None, :] < own_natural[:, None]).astype(jnp.int32), axis=1)
    slots = jnp.arange(slot_blocks, dtype=jnp.int32)
    order = jnp.sum(jnp.where(rank[None, :] == slots[:, None], slots[None, :], 0), axis=1)
    scalars = (natural, order, low_block, high_start, thresholds, near_table)

    def to_heads(x, kinds):
        split = x.reshape(kinds, head_count, DH, pair_count, team, BLOCK)
        split = turn_halves(split, 3, turn, 1)
        send = split.transpose(1, 4, 3, 0, 2, 5).reshape(
            ctx_count, pair_count, kinds * DH, BLOCK
        )
        got = lax.all_to_all(send, "ctx", 0, 0, tiled=True)
        return got.reshape(slot_blocks, kinds * DH, BLOCK)

    def from_heads(x, kinds):
        send = x.reshape(ctx_count, pair_count, kinds * DH, BLOCK)
        got = lax.all_to_all(send, "ctx", 0, 0, tiled=True)
        split = got.reshape(head_count, team, pair_count, kinds, DH, BLOCK)
        split = split.transpose(3, 0, 4, 2, 1, 5)
        split = turn_halves(split, 3, turn, -1)
        return split.reshape(kinds * head_count * DH, group_rows)

    def team_shift(x, step):
        route = []
        for device in range(ctx_count):
            base = device // team * team
            route.append((device, base + (device % team + step) % team))
        return lax.ppermute(x, "ctx", route)

    direct = pair_count == tp_count
    spot = (ctx_index + tp_index) % team

    def rows_from_heads(x):
        if direct:
            got = lax.all_to_all(x, ("ctx", "tp"), 0, 0, tiled=True)
            split = got.reshape(head_count, 1, team, tp_count, DH, BLOCK)
            split = turn_halves(split, 1, spot[None], -1)
            split = split.transpose(3, 0, 4, 1, 2, 5)
        else:
            split = from_heads(x, 1).reshape(width_loc, tp_count, rows_dev)
            split = lax.all_to_all(split.transpose(1, 0, 2), "tp", 0, 0, tiled=True)
        return split.reshape(tp_count * width_loc, rows_dev)

    def heads_from_rows(x):
        if direct:
            split = x.reshape(tp_count, head_count, DH, 1, team, BLOCK)
            split = split.transpose(1, 3, 4, 0, 2, 5)
            split = turn_halves(split, 1, spot[None], 1)
            send = split.reshape(ctx_count * tp_count, DH, BLOCK)
            return lax.all_to_all(send, ("ctx", "tp"), 0, 0, tiled=True)
        send = x.reshape(tp_count, width_loc, rows_dev)
        got = lax.all_to_all(send, "tp", 0, 0, tiled=True)
        return to_heads(got.transpose(1, 0, 2).reshape(width_loc, group_rows), 1)

    w_heads = (w_query, w_key, w_value)
    send = project(turn, h_one_all, w_heads, head_count, team)
    own_qkv = lax.all_to_all(
        send.reshape(ctx_count, pair_count, 3 * DH, BLOCK), "ctx", 0, 0, tiled=True
    ).reshape(slot_blocks, 3 * DH, BLOCK)
    own_pairs = own_qkv[:, DH:, :]
    parts = [own_qkv] + [team_shift(own_pairs, -step) for step in range(1, team)]
    head_block = (slot_blocks, DH, BLOCK)
    att_slots, att_full, log_total = attention_call(
        forward_kernel,
        team,
        bucket_count,
        scalars,
        seq_start,
        parts,
        [
            jax.ShapeDtypeStruct(head_block, bf16),
            jax.ShapeDtypeStruct(head_block, f32),
            jax.ShapeDtypeStruct((slot_blocks, BLOCK), f32),
        ],
        total,
        [],
        8,
    )
    attended_rows = rows_from_heads(att_slots)
    mixed_in = x_float + lax.dot_general(
        attended_rows, w_out_all, (((0,), (0,)), ((), ())), preferred_element_type=f32
    )
    inv_two = lax.rsqrt(jnp.mean(mixed_in * mixed_in, axis=1, keepdims=True) + EPS)
    normed_two = mixed_in * inv_two
    h_two = (normed_two * gain_two).astype(bf16)
    h_two_parts = [
        lax.all_gather(h_two[at : at + half_rows], "tp", axis=0, tiled=True)
        for at in (0, half_rows)
    ]
    lanes = BLOCK
    keep = by_half(kept_choices(routes, experts, capacity))
    keep_wide = jnp.pad(keep, ((0, 0), (0, lanes - experts)))
    router_wide = jnp.pad(w_router, ((0, 0), (0, lanes - experts)))
    back = jnp.einsum("rd,efd->erf", grad_all, down_wide, preferred_element_type=f32)
    filled, d_h_two, router_parts = [], [], []
    for part, h_part in enumerate(h_two_parts):
        d_h_part, *filled, router_part = expert_layer(
            part, h_part, router_wide, keep_wide, gate_wide, up_wide, back, filled
        )
        router_parts.append(router_part)
        d_h_two.append(
            lax.psum_scatter(d_h_part, "tp", scatter_dimension=0, tiled=True)
        )
    hidden, d_gate_bf, d_up_bf = filled
    hidden, d_up_bf, d_h_two[0] = lax.optimization_barrier((hidden, d_up_bf, d_h_two[0]))
    some = experts // 2
    core_first = (core * some).astype(jnp.int32).reshape(1)
    away_first = ((1 - core) * some).astype(jnp.int32).reshape(1)
    operands = (
        (d_gate_bf, h_two_parts),
        (d_up_bf, h_two_parts),
        (hidden, (grad_all, grad_all)),
    )
    away = [
        weight_grads(away_first, some, units, left, rights, ()) for left, rights in operands
    ]
    mine = [
        weight_grads(core_first, some, units, left, rights, (crossed(grads, "ctx", 1),))
        for (left, rights), grads in zip(operands, away)
    ]
    d_h_two, _ = lax.optimization_barrier((d_h_two, mine))
    d_h_two = jnp.concatenate(d_h_two, axis=0).astype(f32)
    same_core = [list(range(first, ctx_count, 2)) for first in range(2)]
    def both_halves(grads):
        other = crossed(grads, "ctx", 1)
        first = jnp.where(core == 0, grads, other)
        second = jnp.where(core == 0, other, grads)
        return jnp.concatenate([first, second], axis=0).astype(f32)

    mine = lax.psum(tuple(mine), "ctx", axis_index_groups=same_core)
    grad_float = cotangent.astype(f32)
    grad_router_part = (router_parts[0] + router_parts[1])[:experts]
    d_norm_two = d_h_two * gain_two
    grad_gain_two_part = jnp.sum(d_h_two * normed_two, axis=0)
    d_mixed = grad_float + inv_two * (
        d_norm_two - normed_two * jnp.mean(d_norm_two * normed_two, axis=1, keepdims=True)
    )
    d_attn = d_mixed.astype(bf16)
    d_attended = lax.dot_general(
        w_out_all, d_attn, (((1,), (1,)), ((), ())), preferred_element_type=f32
    ).astype(bf16)
    d_att_slots = heads_from_rows(d_attended)
    hidden, d_attn = lax.optimization_barrier((hidden, d_attn))
    mixed_part = jnp.einsum(
        "ecf,efd->cd", hidden[:, :, :units], w_down, preferred_element_type=f32
    )
    out_part = jnp.dot(attended_rows, d_attn, preferred_element_type=f32)
    d_att_slots, mixed_part, out_part = lax.optimization_barrier(
        (d_att_slots, by_device(mixed_part.astype(bf16)), out_part.astype(bf16))
    )
    out_pieces = tp_scatter(out_part)
    pair_block = jax.ShapeDtypeStruct((slot_blocks, 2 * DH, BLOCK), bf16)
    back_out = attention_call(
        backward_kernel,
        team,
        bucket_count,
        scalars,
        seq_start,
        parts + [d_att_slots, att_full, log_total],
        [jax.ShapeDtypeStruct(head_block, bf16)]
        + [pair_block] * team
        + [jax.ShapeDtypeStruct((1, BLOCK), f32)],
        total,
        [
            pltpu.VMEM((total + BLOCK, 2 * DH), f32),
            pltpu.VMEM((2 * BLOCK, BLOCK), f32),
        ],
        BACK_COST,
    )
    out_pieces, back_out = lax.optimization_barrier((out_pieces, tuple(back_out)))
    pair_grads = back_out[1].astype(f32)
    for step in range(1, team):
        pair_grads = pair_grads + team_shift(back_out[1 + step], step).astype(f32)
    send = jnp.concatenate([back_out[0], pair_grads.astype(bf16)], axis=1)
    got = lax.all_to_all(
        send.reshape(ctx_count, pair_count, 3 * DH, BLOCK), "ctx", 0, 0, tiled=True
    )
    grad_out = summed(out_pieces)
    small_rows = 16 * chips
    table_part = back_out[1 + team][0, :bucket_count, None] * head_hot[None, :]
    table_row = jnp.pad(table_part.reshape(1, -1), ((0, 0), (0, width - table_part.size)))
    small = jnp.concatenate(
        [
            jnp.zeros((1, width), f32),
            grad_gain_two_part[None],
            grad_router_part,
            table_row,
            jnp.zeros((small_rows - 3 - experts, width), f32),
        ],
        axis=0,
    )
    d_h_one_part, wide = unproject(
        turn,
        got.reshape(head_count, team, pair_count, 3 * DH, BLOCK),
        h_one_all,
        w_heads,
        grad_out.astype(bf16),
        small,
        gain_one[None],
    )
    d_h_pieces = tp_scatter(d_h_one_part)
    wide = chip_scatter(core_scatter(wide))
    wide, d_h_pieces = lax.optimization_barrier((wide, d_h_pieces))
    mine, mixed_part, _ = lax.optimization_barrier((mine, mixed_part, wide))
    mixed_rows = lax.psum_scatter(mixed_part, "tp", scatter_dimension=0, tiled=True)
    layer_out = mixed_in + mixed_rows.astype(f32)
    others = [crossed(grads, "ctx", 1) for grads in mine]
    expert_grads = place_half(core_first, mine, [])
    wide, expert_grads = lax.optimization_barrier((chip_gather(wide), expert_grads))
    expert_grads = place_half(away_first, others, expert_grads)
    d_h_one = summed(d_h_pieces)
    d_norm_one = d_h_one * gain_one
    grad_x = d_mixed + inv_one * (
        d_norm_one - normed_one * jnp.mean(d_norm_one * normed_one, axis=1, keepdims=True)
    )
    wide = both_halves(wide)
    grad_qkv = wide[: 3 * width_loc].T
    grad_out = wide[3 * width_loc : 4 * width_loc]
    small = wide[4 * width_loc :]
    over_rows = small[: 2 + experts]
    own = width // tp_count
    slices = over_rows.reshape(2 + experts, tp_count, own).transpose(1, 0, 2)
    over_rows = summed(tp_scatter(slices.reshape(-1, own)))
    gain_one_grad = over_rows[0]
    gain_two_grad = over_rows[1]
    router_grad = over_rows[2:].T
    table_grad = small[2 + experts, : bucket_count * head_count].reshape(
        bucket_count, head_count
    )
    return (
        layer_out,
        grad_x,
        gain_one_grad,
        grad_qkv[:, :width_loc],
        grad_qkv[:, width_loc : 2 * width_loc],
        grad_qkv[:, 2 * width_loc :],
        grad_out,
        table_grad,
        gain_two_grad,
        router_grad,
        jnp.swapaxes(expert_grads[0], 1, 2),
        jnp.swapaxes(expert_grads[1], 1, 2),
        expert_grads[2],
    )


def solution(mesh):
    placed = (
        P(("ctx", "tp"), None),
        P(),
        P(None, "tp"),
        P(None, "tp"),
        P(None, "tp"),
        P("tp", None),
        P(None, "tp"),
        P(),
        P(),
        P(None, None, "tp"),
        P(None, None, "tp"),
        P(None, "tp", None),
        P(),
        P(),
        P(),
        P("ctx", None),
        P(("ctx", "tp"), None),
    )
    return jax.shard_map(
        on_device,
        mesh=mesh,
        in_specs=placed,
        out_specs=(
            P(("ctx", "tp"), None),
            P(("ctx", "tp"), None),
            P("tp"),
            P(None, "tp"),
            P(None, "tp"),
            P(None, "tp"),
            P("tp", None),
            P(None, "tp"),
            P("tp"),
            P("tp", None),
            P(None, None, "tp"),
            P(None, None, "tp"),
            P(None, "tp", None),
        ),
        check_vma=False,
    )
```

time: 645 us -> 578 us (0.90)
  other arithmetic: 68.6 us -> 30.6 us
  Pallas kernels: 206 us -> 226 us
  matrix products: 45.2 us -> 26.9 us
  local copies, waits for them, and re-layouts: 66.9 us -> 50.8 us
  starting transfers between devices: 49.7 us -> 40.8 us
    pallas_call x2 -> x10, Pallas kernels: 32.5 us -> 75.4 us  [the longest x6 42 us: weight_grads(): pl.pallas_call(weight_grads_kernel, out_shape=jax.ShapeDtypeStruct((count...]
    pallas_call x2, Pallas kernels: 131 us -> 103 us  [attention_call(): pl.pallas_call(functools.partial(kernel, bucket_count, parts), out_shape=...]
    ppermute x6 -> x9, waiting for transfers between devices: 3.71 us -> 28.3 us  [turned(): lax.ppermute(x, axis, [(at, (at + step) % size) for at in range(size)])]
    ppermute x19 -> x14, waiting for transfers between devices: 34 us -> 15.2 us  [crossed(): return lax.ppermute(x, axis, [(at, at ^ bits) for at in range(size)])]
    ppermute x19 -> x14, starting transfers between devices: 27 us -> 8.58 us  [crossed(): return lax.ppermute(x, axis, [(at, at ^ bits) for at in range(size)])]
    dot_general x5 -> x1, matrix products: 18.8 us -> 0.71 us  [on_device(): out_part = jnp.dot(attended_rows, d_attn, preferred_element_type=f32)]
    all_gather x2 -> x3, waiting for transfers between devices: 29.4 us -> 13.3 us  [the longest x2 13.3 us: on_device(): lax.all_gather(h_two[at:at + half_rows], 'tp', axis=0, tiled=True)]
    transpose x3 -> x0, other arithmetic: 15.5 us -> none  [the longest x1 5.19 us: to_heads(): split.transpose(1, 4, 3, 0, 2, 5)]
  transfers between devices with their start and end apart: 38 -> 38, of which waited for: 16 -> 16; matrix products, arithmetic and copies ran while one was open for 25% -> 17% of each run, Pallas kernels for 26% -> 39%
where the time goes in v3:
time: 578 us; the launch traced here: 573 us
  Pallas kernels  226 us (39%)
  waiting for transfers between devices  183 us (32%)
  local copies, waits for them, and re-layouts  50.8 us (9%)
  starting transfers between devices  40.8 us (7%)
  other arithmetic  30.6 us (5%)
  matrix products  26.9 us (5%)
  between operations  15.2 us (3%)
    pallas_call x2, Pallas kernels, attention_call(): pl.pallas_call(functools.partial(kernel, bucket_count, parts), out_shape=...  103 us
    pallas_call x2, Pallas kernels, expert_layer(): pl.pallas_call(functools.partial(expert_kernel, experts), out_shape=[jax....  47.3 us
    all_to_all x2, waiting for transfers between devices, on_device(): lax.all_to_all(send.reshape(ctx_count, pair_count, 3 * DH, BLOCK), 'ctx',...  45.3 us
    pallas_call x6, Pallas kernels, weight_grads(): pl.pallas_call(weight_grads_kernel, out_shape=jax.ShapeDtypeStruct((count...  42 us
    all_gather x1, waiting for transfers between devices, on_device(): h_one_all = lax.all_gather(h_one, 'tp', axis=0, tiled=True)  35.2 us
    ppermute x9, waiting for transfers between devices, turned(): lax.ppermute(x, axis, [(at, (at + step) % size) for at in range(size)])  28.3 us
    pallas_call x2, Pallas kernels, place_half(): pl.pallas_call(functools.partial(place_kernel, count), out_shape=[jax.Sha...  17.7 us
    ppermute x9, starting transfers between devices, turned(): lax.ppermute(x, axis, [(at, (at + step) % size) for at in range(size)])  17.5 us
  transfers between devices with their start and end apart: 38, of which 16 were waited for; matrix products, arithmetic and copies ran while one was open for 17% of the time, Pallas kernels for 39%

profile of v3, /device:TPU:0, one launch (start us, length us, event | category | flops | bytes accessed | tf_op | source)
XLA Modules:
  0.0 573.4 jit_solution(7336310624050452598)
XLA Ops:
  10.6 6.7 %pad.22.gate_ref = bf16[4,768,1024]{2,1,0:T(8,128)(2,1)} pad(bf16[4,704,1024]{2,1,0:T(8,128)(2,1)} %bitcast.144, bf16[]{:T(256)} %constant.187.clone.1), padding=0_0x0_64x0_0 | pad | bytes 12058626 | tf_op jit(solution)/shard_map/jit(_pad)/pad | solution.py:554
  24.1 35.2 %all-gather.6.cloned.1.call-done.h_ref = bf16[1024,1024]{1,0:T(8,128)(2,1)} async-done(((bf16[256,1024]{1,0:T(8,128)(2,1)}), bf16[1024,1024]{1,0:T(8,128)(2,1)}) %all-gather.6.cloned.1.call-update) | async-done | bytes 2097168 | tf_op jit(solution)/shard_map/all_gather | solution.py:766
  70.4 20.5 %all-to-all-done = bf16[8,4,192,128]{3,2,1,0:T(8,128)(2,1)S(1)} async-done(((bf16[8,4,192,128]{3,2,1,0:T(8,128)(2,1)}), bf16[8,4,192,128]{3,2,1,0:T(8,128)(2,1)S(1)}, u32[]{:S(2)}, u32[]{:S(2)}) %all-to-all-start) | async-done | bytes 1572896 | tf_op jit(solution)/shard_map/all_to_all | solution.py:927
  97.2 47.7 %shard_map.265 = (bf16[32,64,128]{2,1,0:T(8,128)(2,1)}, f32[32,64,128]{2,1,0:T(8,128)}, f32[32,128]{1,0:T(8,128)}) custom-call(s32[64]{0:T(128)} %reshape.310.nat_ref, s32[32]{0:T(128)} %select_reduce_fusion.1.order_ref, s32[64]{0:T(128)} %and_select_fusion.1.low_ref, s32[64]{0:T(128)} %get-tuple-element.178.high_ref, s32[32]{0:T(128)} %convert_reduce_fusion.thr_ref, ...), custom_call_target="tpu_custom_call" | custom-call | flops 34359738368 | bytes 209715200 | tf_op jit(solution)/shard_map/pallas_call | solution.py:340
  147.5 14.8 %all-to-all-done.1 = bf16[32,64,128]{2,1,0:T(8,128)(2,1)S(1)} async-done(((bf16[32,64,128]{2,1,0:T(8,128)(2,1)}), bf16[32,64,128]{2,1,0:T(8,128)(2,1)S(1)}, u32[]{:S(2)}, u32[]{:S(2)}) %all-to-all-start.1) | async-done | bytes 524320 | tf_op jit(solution)/shard_map/all_to_all | solution.py:905
  174.8 13.0 %convolution_bitcast_fusion.back_ref = f32[4,1024,768]{2,1,0:T(8,128)} fusion(bf16[4,768,1024]{2,1,0:T(8,128)(2,1)} %pad.24, bf16[1024,1024,1]{1,0,2:T(8,128)(2,1)S(1)} %bitcast.134), kind=kOutput, calls=%fused_computation.2 | convolution fusion | flops 6442450944 | bytes 20971520 | tf_op jit(solution)/shard_map/rd,efd->erf/dot_general | solution.py:964
  187.7 8.2 %all-gather.14.cloned.1.call-done.h_ref.low_ref = bf16[512,1024]{1,0:T(8,128)(2,1)} async-done(((bf16[128,1024]{1,0:T(8,128)(2,1)}), bf16[512,1024]{1,0:T(8,128)(2,1)}) %all-gather.14.cloned.1.call-update) | async-done | bytes 1048592 | tf_op jit(solution)/shard_map/all_gather | solution.py:957
  195.9 23.8 %shard_map.266 = (bf16[512,1024]{1,0:T(8,128)(2,1)}, bf16[4,1024,768]{2,1,0:T(8,128)(2,1)}, bf16[4,1024,768]{2,1,0:T(8,128)(2,1)}, bf16[4,1024,768]{2,1,0:T(8,128)(2,1)}, f32[8,1024]{1,0:T(8,128)}) custom-call(bf16[512,1024]{1,0:T(8,128)(2,1)} %all-gather.14.cloned.1.call-done.h_ref.low_ref, bf16[1024,128]{1,0:T(8,128)(2,1)} %pad.25.router_ref, ...), custom_call_target="tpu_custom_call" | custom-call | flops 12884901888 | bytes 30408704 | tf_op jit(solution)/shard_map/pallas_call | solution.py:637
  225.3 23.4 %shard_map.267 = (bf16[512,1024]{1,0:T(8,128)(2,1)}, bf16[4,1024,768]{2,1,0:T(8,128)(2,1)}, bf16[4,1024,768]{2,1,0:T(8,128)(2,1)}, bf16[4,1024,768]{2,1,0:T(8,128)(2,1)}, f32[8,1024]{1,0:T(8,128)}) custom-call(bf16[512,1024]{1,0:T(8,128)(2,1)} %all-gather.10.cloned.1.call-done.h_ref.high_ref, ...), custom_call_target="tpu_custom_call", output_to_operand_aliasing={{1}: (6, {}), {2}: (7, {}), {3}: (8, {})} | custom-call | flops 12884901888 | bytes 30408704 | tf_op jit(solution)/shard_map/pallas_call | solution.py:637
  248.8 6.8 %shard_map.268 = bf16[2,704,1024]{2,1,0:T(8,128)(2,1)} custom-call(s32[1]{0:T(128)} %bitcast.20.first_ref, bf16[4,1024,768]{2,1,0:T(8,128)(2,1)} %get-tuple-element.85.left_ref, bf16[512,1024]{1,0:T(8,128)(2,1)} %all-gather.14.cloned.1.call-done.h_ref.low_ref, bf16[512,1024]{1,0:T(8,128)(2,1)} %all-gather.10.cloned.1.call-done.h_ref.high_ref), custom_call_target="tpu_custom_call" | custom-call | flops 402653184 | bytes 1048576 | tf_op jit(solution)/shard_map/pallas_call | solution.py:696
  255.6 6.8 %shard_map.272 = bf16[2,704,1024]{2,1,0:T(8,128)(2,1)} custom-call(s32[1]{0:T(128)} %bitcast.20.first_ref, bf16[4,1024,768]{2,1,0:T(8,128)(2,1)} %get-tuple-element.95.left_ref, bf16[1024,1024]{1,0:T(8,128)(2,1)} %bitcast.135, bf16[1024,1024]{1,0:T(8,128)(2,1)} %bitcast.136), custom_call_target="tpu_custom_call" | custom-call | flops 402653184 | bytes 1048576 | tf_op jit(solution)/shard_map/pallas_call | solution.py:696
  262.8 6.8 %shard_map.270 = bf16[2,704,1024]{2,1,0:T(8,128)(2,1)} custom-call(s32[1]{0:T(128)} %bitcast.20.first_ref, bf16[4,1024,768]{2,1,0:T(8,128)(2,1)} %get-tuple-element.89.left_ref, bf16[512,1024]{1,0:T(8,128)(2,1)} %all-gather.14.cloned.1.call-done.h_ref.low_ref, bf16[512,1024]{1,0:T(8,128)(2,1)} %all-gather.10.cloned.1.call-done.h_ref.high_ref), custom_call_target="tpu_custom_call" | custom-call | flops 402653184 | bytes 1048576 | tf_op jit(solution)/shard_map/pallas_call | solution.py:696
  269.9 7.2 %shard_map.269 = bf16[2,704,1024]{2,1,0:T(8,128)(2,1)} custom-call(s32[1]{0:T(128)} %bitcast.9.first_ref, bf16[4,1024,768]{2,1,0:T(8,128)(2,1)} %get-tuple-element.85.left_ref, bf16[512,1024]{1,0:T(8,128)(2,1)} %all-gather.14.cloned.1.call-done.h_ref.low_ref, bf16[512,1024]{1,0:T(8,128)(2,1)} %all-gather.10.cloned.1.call-done.h_ref.high_ref, ...), custom_call_target="tpu_custom_call" | custom-call | flops 402653184 | bytes 1048576 | tf_op jit(solution)/shard_map/pallas_call | solution.py:696
  277.2 7.2 %shard_map.273 = bf16[2,704,1024]{2,1,0:T(8,128)(2,1)} custom-call(s32[1]{0:T(128)} %bitcast.9.first_ref, bf16[4,1024,768]{2,1,0:T(8,128)(2,1)} %get-tuple-element.95.left_ref, bf16[1024,1024]{1,0:T(8,128)(2,1)} %bitcast.137, bf16[1024,1024]{1,0:T(8,128)(2,1)} %bitcast.138, bf16[2,704,1024]{2,1,0:T(8,128)(2,1)} %collective-permute-done.3.rest_0_), custom_call_target="tpu_custom_call" | custom-call | flops 402653184 | bytes 1048576 | tf_op jit(solution)/shard_map/pallas_call | solution.py:696
  284.4 7.3 %shard_map.271 = bf16[2,704,1024]{2,1,0:T(8,128)(2,1)} custom-call(s32[1]{0:T(128)} %bitcast.9.first_ref, bf16[4,1024,768]{2,1,0:T(8,128)(2,1)} %get-tuple-element.89.left_ref, bf16[512,1024]{1,0:T(8,128)(2,1)} %all-gather.14.cloned.1.call-done.h_ref.low_ref, bf16[512,1024]{1,0:T(8,128)(2,1)} %all-gather.10.cloned.1.call-done.h_ref.high_ref, ...), custom_call_target="tpu_custom_call" | custom-call | flops 402653184 | bytes 1048576 | tf_op jit(solution)/shard_map/pallas_call | solution.py:696
  307.1 9.9 %bitcast_convert_fusion = bf16[1024,1024]{1,0:T(8,128)(2,1)S(1)} fusion(bf16[4,704,1024]{2,1,0:T(8,128)(2,1)} %param.28, bf16[4,1024,768]{2,1,0:T(8,128)(2,1)} %get-tuple-element.95.left_ref), kind=kOutput, calls=%fused_computation.3 | convolution fusion | flops 5906628608 | bytes 14155776 | tf_op jit(solution)/shard_map/ecf,efd->cd/dot_general | solution.py:1014
  326.6 55.6 %shard_map.274 = (bf16[32,64,128]{2,1,0:T(8,128)(2,1)}, bf16[32,128,128]{2,1,0:T(8,128)(2,1)}, bf16[32,128,128]{2,1,0:T(8,128)(2,1)}, f32[1,128]{1,0:T(1,128)}) custom-call(s32[64]{0:T(128)} %reshape.310.nat_ref, s32[32]{0:T(128)} %select_reduce_fusion.1.order_ref, s32[64]{0:T(128)} %and_select_fusion.1.low_ref, s32[64]{0:T(128)} %get-tuple-element.178.high_ref, ...), custom_call_target="tpu_custom_call" | custom-call | flops 8589934592 | bytes 52428800 | tf_op jit(solution)/shard_map/pallas_call | solution.py:340
  397.9 24.8 %all-to-all-done.3 = bf16[8,4,192,128]{3,2,1,0:T(8,128)(2,1)S(1)} async-done(((bf16[8,4,192,128]{3,2,1,0:T(8,128)(2,1)}), bf16[8,4,192,128]{3,2,1,0:T(8,128)(2,1)S(1)}, u32[]{:S(2)}, u32[]{:S(2)}) %all-to-all-start.3) | async-done | bytes 1572896 | tf_op jit(solution)/shard_map/all_to_all | solution.py:1045
  423.8 9.5 %shard_map.275 = (bf16[1024,1024]{1,0:T(8,128)(2,1)}, bf16[1088,1024]{1,0:T(8,128)(2,1)}) custom-call(s32[4]{0:T(128)} %and_select_fusion.turn_ref, bf16[4,2,4,192,128]{4,3,2,1,0:T(8,128)(2,1)} %bitcast.163, bf16[1024,1024]{1,0:T(8,128)(2,1)} %all-gather.6.cloned.1.call-done.h_ref, bf16[1024,256]{1,0:T(8,128)(2,1)} %query_ref.3, bf16[1024,256]{1,0:T(8,128)(2,1)} %key_ref.3, ...), custom_call_target="tpu_custom_call" | custom-call | flops 3221225472 | bytes 8912896 | tf_op jit(solution)/shard_map/pallas_call | solution.py:489
  458.6 6.7 %collective-permute-done.11 = bf16[136,1024]{1,0:T(8,128)(2,1)} collective-permute-done((bf16[136,1024]{1,0:T(8,128)(2,1)}, bf16[136,1024]{1,0:T(8,128)(2,1)}, u32[]{:S(2)}, u32[]{:S(2)}) %collective-permute-start.11) | collective-permute-done | bytes 278560 | tf_op jit(solution)/shard_map/ppermute | solution.py:782
  466.7 28.2 %collective-permute-done.13 = bf16[256,1024]{1,0:T(8,128)(2,1)} collective-permute-done((bf16[256,1024]{1,0:T(8,128)(2,1)}, bf16[256,1024]{1,0:T(8,128)(2,1)}, u32[]{:S(2)}, u32[]{:S(2)}) %collective-permute-start.13) | collective-permute-done | bytes 524320 | tf_op jit(solution)/shard_map/ppermute | solution.py:778
  500.3 14.8 %all-reduce.9.cloned.1.call-done = (bf16[2,704,1024]{2,1,0:T(8,128)(2,1)}, bf16[2,704,1024]{2,1,0:T(8,128)(2,1)}, bf16[2,704,1024]{2,1,0:T(8,128)(2,1)}) async-done(((bf16[2,704,1024]{2,1,0:T(8,128)(2,1)}, bf16[2,704,1024]{2,1,0:T(8,128)(2,1)}, bf16[2,704,1024]{2,1,0:T(8,128)(2,1)}), (bf16[2,704,1024]{2,1,0:T(8,128)(2,1)}, bf16[2,704,1024]{2,1,0:T(8,128)(2,1)}, ...) | async-done | bytes 8650768 | tf_op jit(solution)/shard_map/psum | solution.py:1000
  517.3 8.8 %shard_map.276 = (f32[4,704,1024]{2,1,0:T(8,128)}, f32[4,704,1024]{2,1,0:T(8,128)}, f32[4,704,1024]{2,1,0:T(8,128)}) custom-call(s32[1]{0:T(128)} %bitcast.9.first_ref, bf16[2,704,1024]{2,1,0:T(8,128)(2,1)} %get-tuple-element.124.refs_0_, bf16[2,704,1024]{2,1,0:T(8,128)(2,1)} %get-tuple-element.125.refs_1_, bf16[2,704,1024]{2,1,0:T(8,128)(2,1)} %get-tuple-element.126.refs_2_), custom_call_target="tpu_custom_call" | custom-call | bytes 25952256 | tf_op jit(solution)/shard_map/pallas_call | solution.py:533
  548.1 8.9 %shard_map.277 = (f32[4,704,1024]{2,1,0:T(8,128)}, f32[4,704,1024]{2,1,0:T(8,128)}, f32[4,704,1024]{2,1,0:T(8,128)}) custom-call(s32[1]{0:T(128)} %bitcast.20.first_ref, bf16[2,704,1024]{2,1,0:T(8,128)(2,1)} %collective-permute-done.22.refs_0_, ...), custom_call_target="tpu_custom_call", output_to_operand_aliasing={{0}: (4, {}), {1}: (5, {}), {2}: (6, {})} | custom-call | bytes 25952256 | tf_op jit(solution)/shard_map/pallas_call | solution.py:533
  (268 shorter events, 155.6 us)
Async XLA Ops:
  7.2 52.1 %all-gather.6.cloned.1.call-start = ((), (), s32[]{:S(2)}) async-start(), calls=%async_computation.7 | async-start | bytes 2621440 | tf_op jit(solution)/shard_map/all_gather | solution.py:766
  10.5 154.5 %all-gather.8.cloned.1.call-start = ((), (), s32[]{:S(2)}) async-start(), calls=%async_computation.8 | async-start | bytes 2621440 | tf_op jit(solution)/shard_map/all_gather | solution.py:823
  66.2 24.8 %all-to-all-start = ((bf16[8,4,192,128]{3,2,1,0:T(8,128)(2,1)}), bf16[8,4,192,128]{3,2,1,0:T(8,128)(2,1)S(1)}, u32[]{:S(2)}, u32[]{:S(2)}) async-start(bf16[8,4,192,128]{3,2,1,0:T(8,128)(2,1)} %bitcast.164), calls=%async_computation | async-start | bytes 3145728 | tf_op jit(solution)/shard_map/all_to_all | solution.py:927
  69.9 102.7 %all-gather.12.cloned.1.call-start = ((), (), s32[]{:S(2)}) async-start(), calls=%async_computation.10 | async-start | bytes 2621440 | tf_op jit(solution)/shard_map/all_gather | solution.py:834
  147.5 48.5 %all-gather.14.cloned.1.call-start = ((), (), s32[]{:S(2)}) async-start(), calls=%async_computation.11 | async-start | bytes 1310720 | tf_op jit(solution)/shard_map/all_gather | solution.py:957
  168.7 56.7 %all-gather.10.cloned.1.call-start = ((), (), s32[]{:S(2)}) async-start(), calls=%async_computation.9 | async-start | bytes 1310720 | tf_op jit(solution)/shard_map/all_gather | solution.py:957
  174.5 81.1 %reduce-scatter.4.cloned.1.call-start = ((), (), s32[]{:S(2)}) async-start(), calls=%async_computation.12 | async-start | bytes 1310720 | tf_op jit(solution)/shard_map/reduce_scatter | solution.py:972
  219.8 76.8 %reduce-scatter.6.cloned.1.call-start = ((), (), s32[]{:S(2)}) async-start(), calls=%async_computation.13 | async-start | bytes 1310720 | tf_op jit(solution)/shard_map/reduce_scatter | solution.py:972
  269.6 245.4 %all-reduce.9.cloned.1.call-start = ((), (), s32[]{:S(2)}) async-start(), calls=%async_computation.15 | async-start | bytes 17301504 | tf_op jit(solution)/shard_map/psum | solution.py:1000
  322.4 59.8 %collective-permute-start.6 = (bf16[256,1024]{1,0:T(8,128)(2,1)S(1)}, bf16[256,1024]{1,0:T(8,128)(2,1)S(1)}, u32[]{:S(2)}, u32[]{:S(2)}) collective-permute-start(bf16[256,1024]{1,0:T(8,128)(2,1)S(1)} %get-tuple-element.192), channel_id=1, source_target_pairs={{0,3},{1,0},{2,1},{3,2},{4,7},{5,4},{6,5},{7,6},{8,11},{9,8},{10,9... | collective-permute-start | bytes 1572872 | tf_op jit(solution)/shard_map/ppermute | solution.py:778
  325.5 56.8 %collective-permute-start.5 = (bf16[256,1024]{1,0:T(8,128)(2,1)S(1)}, bf16[256,1024]{1,0:T(8,128)(2,1)S(1)}, u32[]{:S(2)}, u32[]{:S(2)}) collective-permute-start(bf16[256,1024]{1,0:T(8,128)(2,1)S(1)} %get-tuple-element.193), channel_id=1, source_target_pairs={{0,2},{1,3},{2,0},{3,1},{4,6},{5,7},{6,4},{7,5},{8,10},{9,11},{10,... | collective-permute-start | bytes 1572872 | tf_op jit(solution)/shard_map/ppermute | solution.py:778
  326.6 55.7 %collective-permute-start.4 = (bf16[256,1024]{1,0:T(8,128)(2,1)S(1)}, bf16[256,1024]{1,0:T(8,128)(2,1)S(1)}, u32[]{:S(2)}, u32[]{:S(2)}) collective-permute-start(bf16[256,1024]{1,0:T(8,128)(2,1)S(1)} %get-tuple-element.194), channel_id=1, source_target_pairs={{0,1},{1,2},{2,3},{3,0},{4,5},{5,6},{6,7},{7,4},{8,9},{9,10},{10,1... | collective-permute-start | bytes 1572872 | tf_op jit(solution)/shard_map/ppermute | solution.py:778
  388.1 34.5 %all-to-all-start.3 = ((bf16[8,4,192,128]{3,2,1,0:T(8,128)(2,1)}), bf16[8,4,192,128]{3,2,1,0:T(8,128)(2,1)S(1)}, u32[]{:S(2)}, u32[]{:S(2)}) async-start(bf16[8,4,192,128]{3,2,1,0:T(8,128)(2,1)} %bitcast.33), calls=%async_computation.5 | async-start | bytes 3145728 | tf_op jit(solution)/shard_map/all_to_all | solution.py:1045
  391.9 171.0 %reduce-scatter.8.cloned.1.call-start = ((), (), s32[]{:S(2)}) async-start(), calls=%async_computation.14 | async-start | bytes 2621440 | tf_op jit(solution)/shard_map/reduce_scatter | solution.py:1075
  440.5 24.8 %collective-permute-start.11 = (bf16[136,1024]{1,0:T(8,128)(2,1)}, bf16[136,1024]{1,0:T(8,128)(2,1)}, u32[]{:S(2)}, u32[]{:S(2)}) collective-permute-start(bf16[136,1024]{1,0:T(8,128)(2,1)} %get-tuple-element.197), channel_id=1, source_target_pairs={{0,24},{4,28},{8,16},{12,20},{16,8},{20,12},{24,0},{28,4},{1,25},{... | collective-permute-start | bytes 835592 | tf_op jit(solution)/shard_map/ppermute | solution.py:782
  442.5 22.8 %collective-permute-start.10 = (bf16[136,1024]{1,0:T(8,128)(2,1)}, bf16[136,1024]{1,0:T(8,128)(2,1)}, u32[]{:S(2)}, u32[]{:S(2)}) collective-permute-start(bf16[136,1024]{1,0:T(8,128)(2,1)} %get-tuple-element.198), channel_id=1, source_target_pairs={{0,16},{4,20},{8,24},{12,28},{16,0},{20,4},{24,8},{28,12},{1,17},{... | collective-permute-start | bytes 835592 | tf_op jit(solution)/shard_map/ppermute | solution.py:782
  445.2 21.5 %collective-permute-start.14 = (bf16[256,1024]{1,0:T(8,128)(2,1)}, bf16[256,1024]{1,0:T(8,128)(2,1)}, u32[]{:S(2)}, u32[]{:S(2)}) collective-permute-start(bf16[256,1024]{1,0:T(8,128)(2,1)} %get-tuple-element.188), channel_id=1, source_target_pairs={{0,3},{1,0},{2,1},{3,2},{4,7},{5,4},{6,5},{7,6},{8,11},{9,8},{10,9... | collective-permute-start | bytes 1572872 | tf_op jit(solution)/shard_map/ppermute | solution.py:778
  449.4 45.5 %collective-permute-start.13 = (bf16[256,1024]{1,0:T(8,128)(2,1)}, bf16[256,1024]{1,0:T(8,128)(2,1)}, u32[]{:S(2)}, u32[]{:S(2)}) collective-permute-start(bf16[256,1024]{1,0:T(8,128)(2,1)} %get-tuple-element.189), channel_id=1, source_target_pairs={{0,2},{1,3},{2,0},{3,1},{4,6},{5,7},{6,4},{7,5},{8,10},{9,11},{10,... | collective-permute-start | bytes 1572872 | tf_op jit(solution)/shard_map/ppermute | solution.py:778
  455.2 39.7 %collective-permute-start.12 = (bf16[256,1024]{1,0:T(8,128)(2,1)}, bf16[256,1024]{1,0:T(8,128)(2,1)}, u32[]{:S(2)}, u32[]{:S(2)}) collective-permute-start(bf16[256,1024]{1,0:T(8,128)(2,1)} %get-tuple-element.190), channel_id=1, source_target_pairs={{0,1},{1,2},{2,3},{3,0},{4,5},{5,6},{6,7},{7,4},{8,9},{9,10},{10,1... | collective-permute-start | bytes 1572872 | tf_op jit(solution)/shard_map/ppermute | solution.py:778
  494.9 20.2 %collective-permute-start.15 = (bf16[136,1024]{1,0:T(8,128)(2,1)S(1)}, bf16[136,1024]{1,0:T(8,128)(2,1)S(1)}, u32[]{:S(2)}, u32[]{:S(2)}) collective-permute-start(bf16[136,1024]{1,0:T(8,128)(2,1)S(1)} %fusion.21), channel_id=1, source_target_pairs={{0,8},{4,12},{8,0},{12,4},{16,24},{20,28},{24,16},{28,20},{1,9},{5... | collective-permute-start | bytes 835592 | tf_op jit(solution)/shard_map/ppermute | solution.py:782
  495.2 21.4 %collective-permute-start.17 = (bf16[136,1024]{1,0:T(8,128)(2,1)S(1)}, bf16[136,1024]{1,0:T(8,128)(2,1)S(1)}, u32[]{:S(2)}, u32[]{:S(2)}) collective-permute-start(bf16[136,1024]{1,0:T(8,128)(2,1)S(1)} %fusion.21), channel_id=1, source_target_pairs={{0,24},{4,28},{8,16},{12,20},{16,8},{20,12},{24,0},{28,4},{1,25},{... | collective-permute-start | bytes 835592 | tf_op jit(solution)/shard_map/ppermute | solution.py:782
  526.1 21.9 %collective-permute-start.22 = (bf16[2,704,1024]{2,1,0:T(8,128)(2,1)}, bf16[2,704,1024]{2,1,0:T(8,128)(2,1)}, u32[]{:S(2)}, u32[]{:S(2)}) collective-permute-start(bf16[2,704,1024]{2,1,0:T(8,128)(2,1)} %get-tuple-element.124.refs_0_), channel_id=1, source_target_pairs={{0,4},{4,0},{8,12},{12,8},{16,20},{20,16},{24,28},{28,24},{1,5},{5... | collective-permute-start | bytes 8650760 | tf_op jit(solution)/shard_map/ppermute | solution.py:782
  526.6 21.5 %collective-permute-start.23 = (bf16[2,704,1024]{2,1,0:T(8,128)(2,1)}, bf16[2,704,1024]{2,1,0:T(8,128)(2,1)}, u32[]{:S(2)}, u32[]{:S(2)}) collective-permute-start(bf16[2,704,1024]{2,1,0:T(8,128)(2,1)} %get-tuple-element.125.refs_1_), channel_id=1, source_target_pairs={{0,4},{4,0},{8,12},{12,8},{16,20},{20,16},{24,28},{28,24},{1,5},{5... | collective-permute-start | bytes 8650760 | tf_op jit(solution)/shard_map/ppermute | solution.py:782
  526.7 21.4 %collective-permute-start.24 = (bf16[2,704,1024]{2,1,0:T(8,128)(2,1)}, bf16[2,704,1024]{2,1,0:T(8,128)(2,1)}, u32[]{:S(2)}, u32[]{:S(2)}) collective-permute-start(bf16[2,704,1024]{2,1,0:T(8,128)(2,1)} %get-tuple-element.126.refs_2_), channel_id=1, source_target_pairs={{0,4},{4,0},{8,12},{12,8},{16,20},{20,16},{24,28},{28,24},{1,5},{5... | collective-permute-start | bytes 8650760 | tf_op jit(solution)/shard_map/ppermute | solution.py:782
  (54 other events, 425.8 us)
Sparse Core Ops, SparseCore 0:
  10.6 48.6 all-gather.5
  60.9 44.6 all-gather.7
  107.1 44.8 all-gather.11
  168.8 27.0 all-gather.13
  197.9 27.4 all-gather.9
  228.1 26.6 reduce-scatter.3
  269.8 26.8 reduce-scatter.5
  301.1 213.9 all-reduce.8
  517.4 45.4 reduce-scatter.7
